TPU v7x, 512 devices: a whole 4x4x16 slice. The times are simulated.
512 devices in a mesh: gx: 32 (over z_hi, y, core), gy: 16 (over x, z_lo).
Axes of the slice: x: 4, y: 4, z: 16 (z_hi: 4, z_lo: 4; z = z_hi * 4 + z_lo), core: 2. Of those that a mesh axis runs over, the one named last changes fastest.
Arguments:
- node_state: bfloat16 [262144, 256], P(('gx', 'gy')), may hold values from -6 to 6
- node_grad: bfloat16 [262144, 256], P(('gx', 'gy')), may hold values from -6 to 6
- edge_blocks: bfloat16 [2048, 3, 128, 128], P(('gx', 'gy')), may hold values from -0.3125 to 0.3125
- adjacency: int32 [2048, 3], P(('gx', 'gy')), may hold values from 0 to 3
- cut_source: int32 [32, 16, 4, 2], P('gx', 'gy'), may hold values from 0 to 3
- cut_target: int32 [32, 16, 4, 2], P('gx', 'gy'), may hold values from 0 to 3
- cut_blocks: bfloat16 [32, 16, 4, 2, 128, 128], P('gx', 'gy'), may hold values from -0.3125 to 0.3125
- clusters: int32 [262144], P(('gx', 'gy')), may hold values from 0 to 767, as said below
- edge_lift: bfloat16 [256, 256], replicated, may hold values from -0.375 to 0.375
- edge_bias: bfloat16 [256], replicated, may hold values from -3 to 3
- edge_emit: bfloat16 [256, 256], replicated, may hold values from -0.375 to 0.375
- node_lift: bfloat16 [768, 256], replicated, may hold values from -0.21875 to 0.21875
- node_bias: bfloat16 [256], replicated, may hold values from -3 to 3
- node_emit: bfloat16 [256, 256], replicated, may hold values from -0.375 to 0.375
- norm_gain: bfloat16 [256], replicated, may hold values from 0.5 to 1.5
Outputs:
- updated: bfloat16 [262144, 256], P(('gx', 'gy'))
- state_grad: bfloat16 [262144, 256], P(('gx', 'gy'))
- edgelift_grad: float32 [256, 256], replicated
- edgebias_grad: float32 [256], replicated
- edgeemit_grad: float32 [256, 256], replicated
- nodelift_grad: float32 [768, 256], replicated
- nodebias_grad: float32 [256], replicated
- nodeemit_grad: float32 [256, 256], replicated
- normgain_grad: float32 [256], replicated
Inputs may be any that keep to these rules, and one draw needn't show every extreme that they name: `clusters`: clusters are numbered within a group (the same index along gy); cluster c is owned by the partition at index c // 24 along gx, and in every group each cluster is named by at least one node of its owner.
All inputs are finite; a program needn't handle non-finite values.
Results may differ from a plain program's by a relative error of at most 0.02.
Values may be sent and summed in bfloat16 or wider, within the bound.
No kernel may reach another device: no remote copies, remote signals or barrier semaphores. Data moves between devices by JAX's collectives and lax.ppermute only.
A program may use at most 64 MiB of HBM per device.

v0:
```python
import jax
import jax.numpy as jnp
from jax import lax
from jax.sharding import PartitionSpec as P

CLUS_DEV = 24


NORM_EPS = 1e-05
HIGHEST = lax.Precision.HIGHEST


def from_behind(value, axis, steps):
    count = lax.axis_size(axis)
    initial, last = (max(0, -steps), min(count, count - steps))
    return lax.ppermute(value, axis, [(source, source + steps) for source in range(initial, last)])


def product(left, right):
    return jnp.dot(left, right, preferred_element_type=jnp.float32)


def product_across(left, right, precision=None):
    return lax.dot_general(
        left,
        right,
        (((0,), (0,)), ((), ())),
        preferred_element_type=jnp.float32,
        precision=precision,
    )


def product_back(left, right, precision=None):
    return lax.dot_general(
        left,
        right,
        (((1,), (1,)), ((), ())),
        preferred_element_type=jnp.float32,
        precision=precision,
    )


def silu_slope(operand):
    sigmoid = jax.nn.sigmoid(operand)
    return sigmoid * (1.0 + operand * (1.0 - sigmoid))


def edge_front(states, edge_lift, edge_bias):
    lifted = (product(states, edge_lift) + edge_bias.astype(jnp.float32)).astype(jnp.bfloat16)
    active = jax.nn.silu(lifted.astype(jnp.float32)).astype(jnp.bfloat16)
    return (lifted, active)


def travel(partials, direction):
    received = []
    for index_pos, offset in ((0, 1), (1, -1)):
        received.append(from_behind(partials[index_pos], "gx", offset * direction))
    for index_pos, offset in ((2, 1), (3, -1)):
        received.append(from_behind(partials[index_pos], "gy", offset * direction))
    return jnp.stack(received)


def pool_group(values, onehot):
    partial_sums = product_across(onehot, values)
    counts = jnp.sum(onehot, axis=0, dtype=jnp.float32)
    totals, tallies = (
        lax.psum_scatter(
            partial_sums.astype(jnp.bfloat16), "gx", scatter_dimension=0, tiled=True
        ).astype(jnp.float32),
        lax.psum_scatter(counts.astype(jnp.bfloat16), "gx", scatter_dimension=0, tiled=True).astype(
            jnp.float32
        ),
    )
    cluster_means = (totals / tallies[:, None]).astype(jnp.bfloat16)
    all_means = lax.all_gather(cluster_means, "gx", axis=0, tiled=True)
    return product(onehot, all_means).astype(jnp.bfloat16)


def shards(
    node_state,
    node_grad,
    edge_blocks,
    adjacency,
    cut_source,
    cut_target,
    cut_blocks,
    clusters,
    edge_lift,
    edge_bias,
    edge_emit,
    node_lift,
    node_bias,
    node_emit,
    norm_gain,
):
    tile_count = edge_blocks.shape[0]
    tile_rows = edge_blocks.shape[2]
    row_count, features = node_state.shape
    source_dev = cut_source[0, 0]
    target_dev = cut_target[0, 0]
    cut_dev = cut_blocks[0, 0]
    tile_ids = jnp.arange(tile_count, dtype=jnp.int32)
    lifted, active = edge_front(node_state, edge_lift, edge_bias)
    message = product(active, edge_emit).astype(jnp.bfloat16)
    tiles_msg = message.reshape(tile_count, tile_rows, features)
    partials = jnp.einsum(
        "pcij,pcjf->pcif", cut_dev, tiles_msg[source_dev], preferred_element_type=jnp.float32
    ).astype(jnp.bfloat16)
    arrived = travel(partials, 1)
    local_sum = jnp.einsum(
        "tkij,tkjf->tif", edge_blocks, tiles_msg[adjacency], preferred_element_type=jnp.float32
    )
    target_hot = (target_dev[:, :, None] == tile_ids).astype(jnp.bfloat16)
    incoming = jnp.einsum("pct,pcif->tif", target_hot, arrived, preferred_element_type=jnp.float32)
    aggregate = (local_sum + incoming).astype(jnp.bfloat16).reshape(row_count, features)
    onehot = (
        clusters[:, None] == jnp.arange(CLUS_DEV * lax.axis_size("gx"), dtype=jnp.int32)
    ).astype(jnp.bfloat16)
    lift_state = node_lift[:features]
    lift_agg = node_lift[features : 2 * features]
    lift_coarse = node_lift[2 * features :]
    coarse = pool_group(node_state, onehot)
    node_lifted = (
        product(node_state, lift_state)
        + product(aggregate, lift_agg)
        + product(coarse, lift_coarse)
        + node_bias.astype(jnp.float32)
    ).astype(jnp.bfloat16)
    node_active = jax.nn.silu(node_lifted.astype(jnp.float32)).astype(jnp.bfloat16)
    emitted = product(node_active, node_emit)
    center = emitted - jnp.mean(emitted, axis=-1, keepdims=True)
    inverse = lax.rsqrt(jnp.mean(center * center, axis=-1, keepdims=True) + NORM_EPS)
    normed = center * inverse
    gain_wide = norm_gain.astype(jnp.float32)
    updated = (node_state.astype(jnp.float32) + gain_wide * normed).astype(jnp.bfloat16)
    upstream = node_grad.astype(jnp.float32)
    gain_grad = jnp.sum(upstream * normed, axis=0)
    scaled = upstream * gain_wide
    emit_grad = inverse * (
        scaled
        - jnp.mean(scaled, axis=-1, keepdims=True)
        - normed * jnp.mean(scaled * normed, axis=-1, keepdims=True)
    )
    emit_weight_grad = product_across(node_active.astype(jnp.float32), emit_grad, HIGHEST)
    active_grad = product_back(emit_grad, node_emit.astype(jnp.float32), HIGHEST).astype(
        jnp.bfloat16
    )
    lifted_grad = (
        active_grad.astype(jnp.float32) * silu_slope(node_lifted.astype(jnp.float32))
    ).astype(jnp.bfloat16)
    lift_grad = jnp.concatenate(
        [
            product_across(node_state, lifted_grad),
            product_across(aggregate, lifted_grad),
            product_across(coarse, lifted_grad),
        ],
        axis=0,
    )
    bias_grad = jnp.sum(lifted_grad.astype(jnp.float32), axis=0)
    aggregate_grad = product_back(lifted_grad, lift_agg).astype(jnp.bfloat16)
    coarse_grad = product_back(lifted_grad, lift_coarse).astype(jnp.bfloat16)
    pooled_grad = pool_group(coarse_grad, onehot)
    grad_tiles = aggregate_grad.reshape(tile_count, tile_rows, features)
    returned = travel(grad_tiles[target_dev], -1)
    spread = jnp.einsum(
        "tkij,tif->tkjf", edge_blocks, grad_tiles, preferred_element_type=jnp.float32
    )
    source_hot = (adjacency[:, :, None] == tile_ids).astype(jnp.float32)
    local_grad = jnp.einsum("tks,tkjf->sjf", source_hot, spread, precision=HIGHEST)
    cut_spread = jnp.einsum(
        "pcij,pcif->pcjf", cut_dev, returned, preferred_element_type=jnp.float32
    )
    cut_hot = (source_dev[:, :, None] == tile_ids).astype(jnp.float32)
    cut_grad = jnp.einsum("pcs,pcjf->sjf", cut_hot, cut_spread, precision=HIGHEST)
    message_grad = (local_grad + cut_grad).astype(jnp.bfloat16).reshape(row_count, features)
    edge_emit_grad = product_across(active, message_grad)
    edge_active_grad = product_back(message_grad, edge_emit).astype(jnp.bfloat16)
    edge_lifted_grad = (
        edge_active_grad.astype(jnp.float32) * silu_slope(lifted.astype(jnp.float32))
    ).astype(jnp.bfloat16)
    edge_lift_grad = product_across(node_state, edge_lifted_grad)
    edge_bias_grad = jnp.sum(edge_lifted_grad.astype(jnp.float32), axis=0)
    state_grad = (
        upstream
        + product_back(lifted_grad, lift_state)
        + pooled_grad.astype(jnp.float32)
        + product_back(edge_lifted_grad, edge_lift)
    ).astype(jnp.bfloat16)
    summed = lax.psum(
        (
            edge_lift_grad,
            edge_bias_grad,
            edge_emit_grad,
            lift_grad,
            bias_grad,
            emit_weight_grad,
            gain_grad,
        ),
        ("gx", "gy"),
    )
    grad_scale = float(row_count * lax.axis_size("gx") * lax.axis_size("gy")) ** (-0.5)
    return (
        updated,
        state_grad,
        summed[0] * grad_scale,
        summed[1] * grad_scale,
        summed[2] * grad_scale,
        summed[3] * grad_scale,
        summed[4] * grad_scale,
        summed[5] * grad_scale,
        summed[6] * grad_scale,
    )


def solution(mesh):
    placed = (
        P(("gx", "gy"), None),
        P(("gx", "gy"), None),
        P(("gx", "gy"), None, None, None),
        P(("gx", "gy"), None),
        P("gx", "gy", None, None),
        P("gx", "gy", None, None),
        P("gx", "gy", None, None, None, None),
        P(("gx", "gy")),
        P(),
        P(),
        P(),
        P(),
        P(),
        P(),
        P(),
    )
    return jax.shard_map(
        shards,
        mesh=mesh,
        in_specs=placed,
        out_specs=(P(("gx", "gy"), None), P(("gx", "gy"), None), P(), P(), P(), P(), P(), P(), P()),
        check_vma=False,
    )
```

profile of v0, /device:TPU:1, one launch (start us, length us, event | category | flops | bytes accessed | tf_op | source)
XLA Modules:
  0.0 823.3 jit_solution(15981693021913500574)
XLA Ops:
  7.2 0.7 convert_element_type.131
  8.0 0.7 compare_select_fusion.2
  8.8 2.1 multiply_convert_fusion.1
  11.2 0.5 copy-done.3
  11.6 0.6 gather_fusion.1
  12.6 4.6 collective-permute-start
  17.3 5.5 collective-permute-start.1
  22.8 1.3 collective-permute-start.2
  24.1 1.3 collective-permute-start.3
  25.4 1.4 fusion.5
  27.2 1.1 fusion.55
  28.4 87.9 %all-reduce = bf16[768]{0:T(1024)(128)(2,1)S(1)} all-reduce(bf16[768]{0:T(1024)(128)(2,1)S(1)} %fusion.28), channel_id=3, replica_groups=mesh['gx'=32,'gy'=16] {'gx'}, use_global_device_ids=true, to_apply=%region_2.3.clone | all-reduce | flops 768 | bytes 3072
  116.3 1.3 dynamic-slice
  118.2 0.6 dynamic-slice_convert_fusion
  118.8 0.8 copy.109
  119.8 0.6 gather_fusion
  120.4 1.2 convert_element_type.145
  121.7 1.2 convert_element_type.130
  123.3 0.4 copy.112
  123.7 0.5 convolution_bitcast_fusion.2
  124.9 18.8 %reduce-scatter.3.cloned.1.call-done = bf16[24,256]{1,0:T(8,128)(2,1)} async-done(((bf16[768,256]{1,0:T(8,128)(2,1)}), bf16[24,256]{1,0:T(8,128)(2,1)}) %reduce-scatter.3.cloned.1.call-update) | async-done | bytes 12304 | tf_op jit(solution)/shard_map/reduce_scatter | solution.py:67
  143.8 0.8 divide_convert_fusion.1
  144.5 55.7 %all_gather.6 = bf16[768,256]{1,0:T(8,128)(2,1)S(1)} all-gather(bf16[24,256]{1,0:T(8,128)(2,1)S(1)} %divide_convert_fusion.1), channel_id=1, replica_groups=mesh['gx'=32,'gy'=16] {'gx'}, dimensions={0}, use_global_device_ids=true | all-gather | bytes 405504 | tf_op jit(solution)/shard_map/all_gather | solution.py:75
  200.2 0.4 fusion.11
  201.4 0.4 copy-done.6
  201.9 1.0 fusion.39
  202.8 1.3 fusion.57
  204.2 1.3 convert_reduce_fusion
  205.7 1.0 fusion.75
  206.7 1.0 convolution_bitcast_fusion.6
  207.9 1.4 fusion.6
  209.3 0.6 gather_fusion.2
  210.0 0.7 copy.147
  210.7 2.1 collective-permute-start.4
  212.8 0.7 copy.148
  213.5 3.5 collective-permute-start.5
  217.0 0.8 copy.149
  217.8 1.3 collective-permute-start.6
  219.1 0.8 copy.150
  219.8 4.6 collective-permute-start.7
  224.5 1.6 convolution_bitcast_fusion
  226.0 1.9 copy.119
  228.2 0.8 copy.130
  229.1 1.6 convolution_bitcast_fusion.5
  230.6 2.0 pad_maximum_fusion
  232.6 2.4 convolution_bitcast_fusion.1
  235.0 1.7 copy.125
  236.8 1.0 fusion.27
  238.5 101.5 %all-reduce.1 = (f32[256]{0:T(256)S(1)}, f32[256]{0:T(256)S(1)}, f32[256]{0:T(256)S(1)}) all-reduce(f32[256]{0:T(256)S(1)} %get-tuple-element.77, f32[256]{0:T(256)S(1)} %copy-done.22, f32[256]{0:T(256)S(1)} %get-tuple-element.54), channel_id=1, replica_groups=mesh['gx'=32,'gy'=16] {'gx','gy'}, use_global_device_ids=true, to_apply=%region_10.11 | all-reduce | flops 768 | bytes 6144 | tf_op jit(solution)/shard_map/psum | solution.py:189
  340.1 0.6 broadcast_multiply_fusion.7
  340.6 0.6 broadcast_multiply_fusion.8
  341.2 0.6 broadcast_multiply_fusion.9
  341.8 1.0 fusion.73
  342.8 1.0 convolution_bitcast_fusion.7
  343.8 0.8 divide_convert_fusion
  344.6 53.2 %all_gather.7 = bf16[768,256]{1,0:T(8,128)(2,1)S(1)} all-gather(bf16[24,256]{1,0:T(8,128)(2,1)S(1)} %divide_convert_fusion), channel_id=1, replica_groups=mesh['gx'=32,'gy'=16] {'gx'}, dimensions={0}, use_global_device_ids=true | all-gather | bytes 405504 | tf_op jit(solution)/shard_map/all_gather | solution.py:75
  397.8 0.6 fusion.13
  398.4 1.2 fusion.8
  399.8 0.8 copy.131
  400.7 411.4 %all-reduce.5.cloned.1.call-done = (f32[256,256]{0,1:T(8,128)}, f32[256,256]{0,1:T(8,128)}, f32[768,256]{1,0:T(8,128)}, f32[256,256]{0,1:T(8,128)}) async-done(((f32[256,256]{0,1:T(8,128)}, f32[256,256]{0,1:T(8,128)}, f32[768,256]{1,0:T(8,128)}, f32[256,256]{0,1:T(8,128)}), (f32[256,256]{0,1:T(8,128)}, f32[256,256]{0,1:T(8,128)}, f32[768,256]{1,0:T(8,128)}, ...) | async-done | bytes 1572880 | tf_op jit(solution)/shard_map/psum | solution.py:189
  812.1 2.1 broadcast_multiply_fusion
  814.2 0.8 copy.132
  815.1 0.8 copy.133
  816.0 0.8 copy.134
  (103 shorter events, 5.2 us)
Async XLA Ops:
  7.2 117.0 %copy-start = (bf16[4,3,128,128]{3,2,1,0:T(8,128)(2,1)S(1)}, bf16[4,3,128,128]{3,2,1,0:T(8,128)(2,1)}, u32[]{:S(2)}) copy-start(bf16[4,3,128,128]{3,2,1,0:T(8,128)(2,1)} %param.17) | copy-start | bytes 1179652
  7.2 3.7 copy-start.13
  7.2 136.6 %reduce-scatter.3.cloned.1.call-start = ((), (), s32[]{:S(2)}) async-start(), calls=%async_computation.2 | async-start | bytes 405504 | tf_op jit(solution)/shard_map/reduce_scatter | solution.py:67
  8.8 3.4 copy-start.7
  10.9 0.7 copy-start.3
  11.6 13.7 %copy-start.1 = (bf16[512,256]{1,0:T(8,128)(2,1)S(1)}, bf16[512,256]{1,0:T(8,128)(2,1)}, u32[]{:S(2)}) copy-start(bf16[512,256]{1,0:T(8,128)(2,1)} %param.15) | copy-start | bytes 786436
  11.6 13.7 %copy-start.24 = (s32[512]{0:T(512)S(1)}, s32[512]{0:T(512)}, u32[]{:S(2)}) copy-start(s32[512]{0:T(512)} %param.22) | copy-start | bytes 6148
  12.6 14.6 %copy-start.16 = (s32[4,3]{1,0:T(4,128)S(1)}, s32[4,3]{1,0:T(4,128)}, u32[]{:S(2)}) copy-start(s32[4,3]{1,0:T(4,128)} %param.18) | copy-start | bytes 148
  12.6 103.7 %copy-start.17 = (s32[1,1,4,2]{2,3,1,0:T(2,128)S(1)}, s32[1,1,4,2]{2,3,1,0:T(2,128)}, u32[]{:S(2)}) copy-start(s32[1,1,4,2]{2,3,1,0:T(2,128)} %param.20) | copy-start | bytes 100
  12.6 110.5 %collective-permute-start = (bf16[2,128,256]{1,2,0:T(8,128)(2,1)S(1)}, bf16[2,128,256]{1,2,0:T(8,128)(2,1)S(1)}, u32[]{:S(2)}, u32[]{:S(2)}) collective-permute-start(bf16[2,128,256]{1,2,0:T(8,128)(2,1)S(1)} %get-tuple-element.69), channel_id=1, source_target_pairs={{0,16},{16,32},{32,48},{48,64},{64,80},{80,96},{96,112},{112,128},... | collective-permute-start | bytes 393224 | tf_op jit(solution)/shard_map/ppermute | solution.py:16
  17.3 105.9 %collective-permute-start.1 = (bf16[2,128,256]{1,2,0:T(8,128)(2,1)S(1)}, bf16[2,128,256]{1,2,0:T(8,128)(2,1)S(1)}, u32[]{:S(2)}, u32[]{:S(2)}) collective-permute-start(bf16[2,128,256]{1,2,0:T(8,128)(2,1)S(1)} %get-tuple-element.72), channel_id=1, source_target_pairs={{16,0},{32,16},{48,32},{64,48},{80,64},{96,80},{112,96},{128,112},... | collective-permute-start | bytes 393224 | tf_op jit(solution)/shard_map/ppermute | solution.py:16
  22.8 100.4 %collective-permute-start.2 = (bf16[2,128,256]{1,2,0:T(8,128)(2,1)S(1)}, bf16[2,128,256]{1,2,0:T(8,128)(2,1)S(1)}, u32[]{:S(2)}, u32[]{:S(2)}) collective-permute-start(bf16[2,128,256]{1,2,0:T(8,128)(2,1)S(1)} %get-tuple-element.71), channel_id=1, source_target_pairs={{0,1},{1,2},{2,3},{3,4},{4,5},{5,6},{6,7},{7,8},{8,9},{9,10},{10,1... | collective-permute-start | bytes 393224 | tf_op jit(solution)/shard_map/ppermute | solution.py:16
  24.1 99.1 %collective-permute-start.3 = (bf16[2,128,256]{1,2,0:T(8,128)(2,1)S(1)}, bf16[2,128,256]{1,2,0:T(8,128)(2,1)S(1)}, u32[]{:S(2)}, u32[]{:S(2)}) collective-permute-start(bf16[2,128,256]{1,2,0:T(8,128)(2,1)S(1)} %get-tuple-element.70), channel_id=1, source_target_pairs={{1,0},{2,1},{3,2},{4,3},{5,4},{6,5},{7,6},{8,7},{9,8},{10,9},{11,1... | collective-permute-start | bytes 393224 | tf_op jit(solution)/shard_map/ppermute | solution.py:16
  26.8 94.8 %copy-start.9 = (bf16[512,256]{1,0:T(8,128)(2,1)S(1)}, bf16[512,256]{1,0:T(8,128)(2,1)}, u32[]{:S(2)}) copy-start(bf16[512,256]{1,0:T(8,128)(2,1)} %param.16) | copy-start | bytes 786436
  26.8 316.9 %reduce-scatter.5.cloned.1.call-start = ((), (), s32[]{:S(2)}) async-start(), calls=%async_computation.3 | async-start | bytes 405504 | tf_op jit(solution)/shard_map/reduce_scatter | solution.py:67
  123.7 1.0 copy-start.2
  124.2 19.6 %copy-start.19 = (f32[24]{0:T(128)S(1)}, f32[24]{0:T(128)}, u32[]{:S(2)}) copy-start(f32[24]{0:T(128)} %dynamic-slice_convert_fusion) | copy-start | bytes 292
  124.2 76.0 %copy-start.25 = (s32[512]{0:T(512)S(1)}, s32[512]{0:T(512)}, u32[]{:S(2)}) copy-start(s32[512]{0:T(512)} %param.22) | copy-start | bytes 6148
  124.5 76.1 %copy-start.21 = (f32[256]{0:T(256)S(1)}, f32[256]{0:T(256)}, u32[]{:S(2)}) copy-start(f32[256]{0:T(256)} %convert_element_type.145) | copy-start | bytes 3076
  124.9 76.0 %copy-start.23 = (bf16[256,256]{1,0:T(8,128)(2,1)S(1)}, bf16[256,256]{1,0:T(8,128)(2,1)}, u32[]{:S(2)}) copy-start(bf16[256,256]{1,0:T(8,128)(2,1)} %param.28) | copy-start | bytes 393220
  200.9 1.0 copy-start.6
  200.9 0.9 copy-start.20
  210.7 21.9 %collective-permute-start.4 = (bf16[2,128,256]{1,2,0:T(8,128)(2,1)}, bf16[2,128,256]{1,2,0:T(8,128)(2,1)}, u32[]{:S(2)}, u32[]{:S(2)}) collective-permute-start(bf16[2,128,256]{1,2,0:T(8,128)(2,1)} %copy.147), channel_id=1, source_target_pairs={{16,0},{32,16},{48,32},{64,48},{80,64},{96,80},{112,96},{128,112},... | collective-permute-start | bytes 393224 | tf_op jit(solution)/shard_map/ppermute | solution.py:16
  213.5 19.1 %collective-permute-start.5 = (bf16[2,128,256]{1,2,0:T(8,128)(2,1)}, bf16[2,128,256]{1,2,0:T(8,128)(2,1)}, u32[]{:S(2)}, u32[]{:S(2)}) collective-permute-start(bf16[2,128,256]{1,2,0:T(8,128)(2,1)} %copy.148), channel_id=1, source_target_pairs={{0,16},{16,32},{32,48},{48,64},{64,80},{80,96},{96,112},{112,128},... | collective-permute-start | bytes 393224 | tf_op jit(solution)/shard_map/ppermute | solution.py:16
  217.8 14.8 %collective-permute-start.6 = (bf16[2,128,256]{1,2,0:T(8,128)(2,1)}, bf16[2,128,256]{1,2,0:T(8,128)(2,1)}, u32[]{:S(2)}, u32[]{:S(2)}) collective-permute-start(bf16[2,128,256]{1,2,0:T(8,128)(2,1)} %copy.149), channel_id=1, source_target_pairs={{1,0},{2,1},{3,2},{4,3},{5,4},{6,5},{7,6},{8,7},{9,8},{10,9},{11,1... | collective-permute-start | bytes 393224 | tf_op jit(solution)/shard_map/ppermute | solution.py:16
  219.8 12.8 %collective-permute-start.7 = (bf16[2,128,256]{1,2,0:T(8,128)(2,1)}, bf16[2,128,256]{1,2,0:T(8,128)(2,1)}, u32[]{:S(2)}, u32[]{:S(2)}) collective-permute-start(bf16[2,128,256]{1,2,0:T(8,128)(2,1)} %copy.150), channel_id=1, source_target_pairs={{0,1},{1,2},{2,3},{3,4},{4,5},{5,6},{6,7},{7,8},{8,9},{9,10},{10,1... | collective-permute-start | bytes 393224 | tf_op jit(solution)/shard_map/ppermute | solution.py:16
  226.0 2.2 copy-start.5
  228.0 584.1 %all-reduce.5.cloned.1.call-start = ((), (), s32[]{:S(2)}) async-start(), calls=%async_computation.4 | async-start | bytes 3145728 | tf_op jit(solution)/shard_map/psum | solution.py:189
  229.1 3.6 copy-start.8
  235.0 1.8 copy-start.18
  236.7 1.0 copy-start.14
  236.8 1.1 copy-start.27
  237.9 0.7 copy-start.22
  237.9 103.9 %copy-start.4 = (bf16[512,256]{1,0:T(8,128)(2,1)S(1)}, bf16[512,256]{1,0:T(8,128)(2,1)}, u32[]{:S(2)}) copy-start(bf16[512,256]{1,0:T(8,128)(2,1)} %copy-done.3) | copy-start | bytes 786436
  342.8 55.1 %copy-start.26 = (s32[512]{0:T(512)S(1)}, s32[512]{0:T(512)}, u32[]{:S(2)}) copy-start(s32[512]{0:T(512)} %param.22) | copy-start | bytes 6148
  397.8 1.7 copy-start.15
  812.1 2.1 copy-start.12
  812.1 3.0 copy-start.11
  812.1 3.9 copy-start.10
Sparse Core Ops, SparseCore 0:
  27.0 116.7 reduce-scatter.2
  228.1 102.1 reduce-scatter.4
  343.9 468.1 all-reduce.4
where the time goes:
time: 825 us; the launch traced here: 823 us
  waiting for transfers between devices  430 us (52%)
  blocking collectives  298 us (36%)
  matrix products  24.5 us (3%)
  starting transfers between devices  24.4 us (3%)
  local copies, waits for them, and re-layouts  17.5 us (2%)
  between operations  15 us (2%)
  other arithmetic  13.2 us (2%)
    psum x1, waiting for transfers between devices, shards(): lax.psum((edge_lift_grad, edge_bias_grad, edge_emit_grad, lift_grad, bias...  411 us
    all_gather x2, blocking collectives, pool_group(): all_means = lax.all_gather(cluster_means, 'gx', axis=0, tiled=True)  109 us
    psum x1, blocking collectives, shards(): lax.psum((edge_lift_grad, edge_bias_grad, edge_emit_grad, lift_grad, bias...  102 us
    unnamed x1, blocking collectives  87.9 us
    ppermute x8, starting transfers between devices, from_behind(): lax.ppermute(value, axis, [(source, source + steps) for source in range(i...  24.1 us
    reduce_scatter x2, waiting for transfers between devices, pool_group(): lax.psum_scatter(partial_sums.astype(jnp.bfloat16), 'gx', scatter_dimensi...  18.8 us
  transfers between devices with their start and end apart: 11, of which 2 were waited for; matrix products, arithmetic and copies ran while one was open for 4% of the time, Pallas kernels for 0%

commit v1 on v0

v1 whole, which is shorter than its diff:
```python
import functools

import jax
import jax.numpy as jnp
from jax import lax
from jax.experimental import pallas as pl
from jax.experimental.pallas import tpu as pltpu
from jax.sharding import Mesh
from jax.sharding import PartitionSpec as P

CLUS_DEV = 24
NORM_EPS = 1e-05
TILE = 128
F32 = jnp.float32
BF16 = jnp.bfloat16
VMEM_LIMIT = 24 * 1024 * 1024


def mm(left, right):
    return jnp.dot(left, right, preferred_element_type=F32)


def mm_tn(left, right):
    return lax.dot_general(left, right, (((0,), (0,)), ((), ())), preferred_element_type=F32)


def mm_nt(left, right):
    return lax.dot_general(left, right, (((1,), (1,)), ((), ())), preferred_element_type=F32)


def tile_rows(index):
    return pl.ds(pl.multiple_of(index * TILE, TILE), TILE)


def rows_of(tile):
    return slice(tile * TILE, (tile + 1) * TILE)


def hot_rows(clus_row, first, count):
    ids = lax.broadcasted_iota(jnp.int32, (count, clus_row.shape[1]), 0) + first
    return jnp.where(ids == clus_row, 1.0, 0.0).astype(BF16)


def hot_columns(clus_row, clusters):
    spread = jnp.broadcast_to(clus_row.astype(F32), (TILE, TILE)).T
    spread = jnp.concatenate([spread] * (-(-clusters // TILE)), axis=1)[:, :clusters]
    ids = lax.broadcasted_iota(jnp.int32, (TILE, clusters), 1).astype(F32)
    return jnp.where(ids == spread, 1.0, 0.0).astype(BF16)


def call(kernel, outs, in_specs=None, scratch=(), aliases=None, out_specs=None, flops=0, moved=0):
    options = {}
    if in_specs is not None:
        options["in_specs"] = in_specs
    if out_specs is not None:
        options["out_specs"] = out_specs
    return pl.pallas_call(
        kernel,
        out_shape=outs,
        scratch_shapes=list(scratch),
        input_output_aliases=aliases or {},
        compiler_params=pltpu.CompilerParams(vmem_limit_bytes=VMEM_LIMIT),
        cost_estimate=pl.CostEstimate(flops=flops, bytes_accessed=moved, transcendentals=0),
        **options,
    )


def vmem(count):
    return [pl.BlockSpec(memory_space=pltpu.VMEM)] * count


def smem(count):
    return [pl.BlockSpec(memory_space=pltpu.SMEM)] * count


def like(shape, kind):
    return jax.ShapeDtypeStruct(shape, kind)


def front_kernel(sizes, source, adjacency, clus, state, edge_lift, edge_bias, edge_emit, blocks,
                 cuts, pool, part0, part1, part2, part3, lifted, active, local, message):
    peers, share = sizes
    tiles = state.shape[0] // TILE
    clus_row = clus[...]
    ones = jnp.ones((16, state.shape[0]), BF16)
    low_half = lax.broadcasted_iota(jnp.int32, (16, TILE), 0) >= 8
    bias = edge_bias[...].astype(F32)
    for tile in range(tiles):
        rows = rows_of(tile)
        value = (mm(state[rows], edge_lift[...]) + bias).astype(BF16)
        lifted[rows] = value
        wide = value.astype(F32)
        hidden = (wide * jax.nn.sigmoid(wide)).astype(BF16)
        active[rows] = hidden
        message[rows] = mm(hidden, edge_emit[...]).astype(BF16)
    for slot, part in enumerate((part0, part1, part2, part3)):
        for cut in range(cuts.shape[1]):
            part[rows_of(cut)] = mm(
                cuts[slot, cut], message[tile_rows(source[slot, cut])]
            ).astype(BF16)
    for peer in range(peers):
        hot = hot_rows(clus_row, peer * share, TILE)
        pool[peer, 0:share] = mm(hot, state[...])[:share].astype(BF16)
        count = mm_nt(ones, hot)
        high = jnp.floor(count * (1.0 / 16.0))
        pool[peer, share:share + 16, 0:TILE] = jnp.where(
            low_half, count - 16.0 * high, high
        ).astype(BF16)
        pool[peer, share:share + 16, TILE:] = jnp.zeros((16, state.shape[1] - TILE), BF16)
    for tile in range(tiles):
        total = mm(blocks[tile, 0], message[tile_rows(adjacency[tile, 0])])
        for slot in range(1, blocks.shape[1]):
            total += mm(blocks[tile, slot], message[tile_rows(adjacency[tile, slot])])
        local[rows_of(tile)] = total


def sum_kernel(copies, received, out):
    total = jnp.sum(received[...].astype(F32), axis=0).astype(BF16)
    for index in range(copies):
        out[index] = total


def mean_kernel(share, received, means, counts):
    total = jnp.sum(received[...].astype(F32), axis=0)
    high, low = total[share:share + 1, 0:TILE], total[share + 8:share + 9, 0:TILE]
    count = jnp.broadcast_to(high * 16.0 + low, (TILE, TILE)).T[:share]
    count = jnp.concatenate([count] * (means.shape[1] // TILE), axis=1)
    counts[...] = count
    means[...] = (total[:share] / count).astype(BF16)


def node_kernel(target, clus, state, upstream, local, arrived0, arrived1, arrived2, arrived3,
                means, node_lift, node_bias, node_emit, norm_gain,
                updated, aggregate, coarse, active, emit_grad, lifted_grad, aggregate_grad,
                coarse_grad, back0, back1, back2, back3, vectors, summed):
    features = state.shape[1]
    clusters = means.shape[0]
    summed[...] = local[...]
    for slot, arrived in enumerate((arrived0, arrived1, arrived2, arrived3)):
        for cut in range(arrived.shape[0] // TILE):
            summed[tile_rows(target[slot, cut])] += arrived[rows_of(cut)].astype(F32)
    lift_state = node_lift[0:features]
    lift_agg = node_lift[features:2 * features]
    lift_coarse = node_lift[2 * features:]
    bias = node_bias[...].astype(F32)
    gain = norm_gain[...].astype(F32)
    gain_grad = jnp.zeros((1, features), F32)
    bias_grad = jnp.zeros((1, features), F32)
    for tile in range(state.shape[0] // TILE):
        rows = rows_of(tile)
        here = state[rows]
        agg = summed[rows].astype(BF16)
        aggregate[rows] = agg
        hot = hot_columns(clus[0:1, rows], clusters)
        pooled = mm(hot, means[...]).astype(BF16)
        coarse[rows] = pooled
        lifted = (
            mm(here, lift_state) + mm(agg, lift_agg) + mm(pooled, lift_coarse) + bias
        ).astype(BF16).astype(F32)
        gate = jax.nn.sigmoid(lifted)
        hidden = (lifted * gate).astype(BF16)
        active[rows] = hidden
        emitted = mm(hidden, node_emit[...])
        center = emitted - jnp.mean(emitted, axis=-1, keepdims=True)
        inverse = lax.rsqrt(jnp.mean(center * center, axis=-1, keepdims=True) + NORM_EPS)
        normed = center * inverse
        updated[rows] = (here.astype(F32) + gain * normed).astype(BF16)
        above = upstream[rows].astype(F32)
        gain_grad += jnp.sum(above * normed, axis=0, keepdims=True)
        scaled = above * gain
        grad = (
            inverse
            * (
                scaled
                - jnp.mean(scaled, axis=-1, keepdims=True)
                - normed * jnp.mean(scaled * normed, axis=-1, keepdims=True)
            )
        ).astype(BF16)
        emit_grad[rows] = grad
        active_grad = mm_nt(grad, node_emit[...]).astype(BF16).astype(F32)
        slope = gate * (1.0 + lifted * (1.0 - gate))
        down = (active_grad * slope).astype(BF16)
        lifted_grad[rows] = down
        bias_grad += jnp.sum(down.astype(F32), axis=0, keepdims=True)
        aggregate_grad[rows] = mm_nt(down, lift_agg).astype(BF16)
        coarse_grad[rows] = mm_nt(down, lift_coarse).astype(BF16)
    for slot, back in enumerate((back0, back1, back2, back3)):
        for cut in range(back.shape[0] // TILE):
            back[rows_of(cut)] = aggregate_grad[tile_rows(target[slot, cut])]
    vectors[...] = jnp.zeros(vectors.shape, F32)
    vectors[0:1] = bias_grad
    vectors[1:2] = gain_grad


def put_chunks(packed, first, size, start, value):
    done = 0
    while done < value.shape[0]:
        peer, offset = divmod(start + done, size)
        count = min(size - offset, value.shape[0] - done)
        packed[peer, first + offset:first + offset + count] = value[done:done + count].astype(BF16)
        done += count


def weight_kernel(sizes, adjacency, clus, state, upstream, aggregate, coarse, active, emit_grad,
                  lifted_grad, aggregate_grad, coarse_grad, blocks, node_lift,
                  packed, local, partial):
    peers, share, node_rows, _ = sizes
    features = state.shape[1]
    clus_row = clus[...]
    for peer in range(peers):
        packed[peer, 0:share] = mm(
            hot_rows(clus_row, peer * share, share), coarse_grad[...]
        ).astype(BF16)
    down = lifted_grad[...]
    for index, block in enumerate((state, aggregate, coarse)):
        put_chunks(packed, share, node_rows, index * features, mm_tn(block[...], down))
    put_chunks(packed, share, node_rows, 3 * features, mm_tn(active[...], emit_grad[...]))
    local[...] = jnp.zeros(local.shape, F32)
    for tile in range(state.shape[0] // TILE):
        rows = rows_of(tile)
        for slot in range(blocks.shape[1]):
            local[tile_rows(adjacency[tile, slot])] += mm_tn(
                blocks[tile, slot], aggregate_grad[rows]
            )
        partial[rows] = upstream[rows].astype(F32) + mm_nt(
            lifted_grad[rows], node_lift[0:features]
        )


def edge_kernel(sizes, source, state, lifted, active, local, back0, back1, back2, back3, cuts,
                edge_lift, edge_emit, partial, vectors, packed_in,
                packed, partial_out, total, message_grad, lifted_grad, edge_part, sem):
    peers, share, node_rows, edge_rows = sizes
    features = state.shape[1]
    total[...] = local[...]
    for slot, back in enumerate((back0, back1, back2, back3)):
        for cut in range(cuts.shape[1]):
            total[tile_rows(source[slot, cut])] += mm_tn(cuts[slot, cut], back[rows_of(cut)])
    bias_grad = jnp.zeros((1, features), F32)
    for tile in range(state.shape[0] // TILE):
        rows = rows_of(tile)
        grad = total[rows].astype(BF16)
        message_grad[rows] = grad
        active_grad = mm_nt(grad, edge_emit[...]).astype(BF16).astype(F32)
        wide = lifted[rows].astype(F32)
        gate = jax.nn.sigmoid(wide)
        down = (active_grad * (gate * (1.0 + wide * (1.0 - gate)))).astype(BF16)
        lifted_grad[rows] = down
        bias_grad += jnp.sum(down.astype(F32), axis=0, keepdims=True)
        partial_out[rows] = partial[rows] + mm_nt(down, edge_lift[...])
    put_chunks(edge_part, 0, edge_rows, 0, mm_tn(state[...], lifted_grad[...]))
    put_chunks(edge_part, 0, edge_rows, features, mm_tn(active[...], message_grad[...]))
    edge_part[:, edge_rows:] = jnp.zeros((peers, 16, features), BF16)
    last = lax.broadcasted_iota(jnp.int32, (16, features), 0)
    edge_part[0, edge_rows:] = jnp.where(
        last == 0, vectors[0:1], jnp.where(last == 1, vectors[1:2], jnp.where(last == 2, bias_grad, 0.0))
    ).astype(BF16)
    place = packed.at[:, pl.ds(share + node_rows, edge_rows + 16), :]
    copy = pltpu.make_async_copy(edge_part, place, sem)
    copy.start()
    copy.wait()


def split_kernel(share, received, pool, grads):
    total = jnp.sum(received[...].astype(F32), axis=0)
    pool[...] = total[:share].astype(BF16)
    used = total.shape[0] - share
    chunk = grads.shape[1]
    for index in range(grads.shape[0]):
        first = index * chunk
        count = max(0, min(chunk, used - first))
        if count:
            grads[index, 0:count] = total[share + first:share + first + count].astype(BF16)
        if count < chunk:
            grads[index, count:] = jnp.zeros((chunk - count, total.shape[1]), BF16)


def join_kernel(pool, received, out):
    share = pool.shape[0]
    grads = jnp.sum(received[...].astype(F32), axis=0).astype(BF16)
    for index in range(out.shape[0]):
        out[index, 0:share] = pool[...]
        out[index, share:] = grads


def settle_kernel(share, received, counts, means, grads):
    total = jnp.sum(received[...].astype(F32), axis=0)
    means[...] = (total[:share] / counts[...]).astype(BF16)
    whole = total[share:].astype(BF16)
    for index in range(grads.shape[0]):
        grads[index] = whole


def last_kernel(sizes, scale, clus, partial, gathered, state_grad, edge_lift, edge_bias, edge_emit,
                node_lift, node_bias, node_emit, norm_gain, means):
    peers, share, node_rows, edge_rows = sizes
    features = partial.shape[1]
    for peer in range(peers):
        means[peer * share:(peer + 1) * share] = gathered[peer, 0:share]
    for tile in range(partial.shape[0] // TILE):
        rows = rows_of(tile)
        pooled = mm(hot_columns(clus[0:1, rows], peers * share), means[...])
        state_grad[rows] = (partial[rows] + pooled).astype(BF16)

    def take(first, size, outs):
        for index, out in enumerate(outs):
            start, done = index * features, 0
            height = out.shape[0]
            if index and outs[0].shape[0] != features:
                start = outs[0].shape[0]
            while done < height:
                peer, offset = divmod(start + done, size)
                count = min(size - offset, height - done)
                out[done:done + count] = (
                    gathered[peer, first + offset:first + offset + count].astype(F32) * scale
                )
                done += count

    take(share, node_rows, (node_lift, node_emit))
    take(share + node_rows, edge_rows, (edge_lift, edge_emit))
    tail = gathered[0, share + node_rows + edge_rows:].astype(F32) * scale
    node_bias[...] = tail[0:1]
    norm_gain[...] = tail[1:2]
    edge_bias[...] = tail[2:3]


def shards(
    node_state,
    node_grad,
    edge_blocks,
    adjacency,
    cut_source,
    cut_target,
    cut_blocks,
    clusters,
    edge_lift,
    edge_bias,
    edge_emit,
    node_lift,
    node_bias,
    node_emit,
    norm_gain,
):
    far, peers, columns = (lax.axis_size(name) for name in ("far", "near", "gy"))
    rows, features = node_state.shape
    along = far * peers
    share = CLUS_DEV * far
    node_rows = 4 * features // peers
    edge_rows = 2 * features // peers
    sizes = (peers, share, node_rows, edge_rows)
    packed_rows = share + node_rows + edge_rows + 16
    chunk = -(-(packed_rows - share) // (16 * columns)) * 16
    source, target = cut_source[0, 0], cut_target[0, 0]
    cuts = cut_blocks[0, 0]
    cut_rows = cuts.shape[1] * TILE
    clus = clusters.reshape(1, rows)
    bias_row, node_bias_row, gain_row = (v.reshape(1, features) for v in (edge_bias, node_bias, norm_gain))
    wide = like((rows, features), F32)
    narrow = like((rows, features), BF16)
    cut_part = like((cut_rows, features), BF16)
    layer = 2 * rows * features * features

    def shift(value, axis, steps, count):
        pairs = [(i, i + steps) for i in range(max(0, -steps), min(count, count - steps))]
        return lax.ppermute(value, axis, pairs)

    def travel(parts, direction):
        gx = ("far", "near")
        return [
            shift(parts[0], gx, direction, along),
            shift(parts[1], gx, -direction, along),
            shift(parts[2], "gy", direction, columns),
            shift(parts[3], "gy", -direction, columns),
        ]

    front = call(
        functools.partial(front_kernel, (peers, share)),
        [like((peers, share + 16, features), BF16)] + [cut_part] * 4 + [narrow, narrow, wide],
        smem(2) + vmem(7),
        [pltpu.VMEM((rows, features), BF16)],
        flops=8 * layer,
        moved=4 << 20,
    )
    pool, part0, part1, part2, part3, lifted, active, local = front(
        source, adjacency, clus, node_state, edge_lift, bias_row, edge_emit, edge_blocks, cuts
    )
    arrived = travel([part0, part1, part2, part3], 1)

    received = lax.all_to_all(pool, "near", 0, 0, tiled=True)
    summed = call(
        functools.partial(sum_kernel, far), like((far, share + 16, features), BF16), moved=1 << 20
    )(received)
    received = lax.all_to_all(summed, "far", 0, 0, tiled=True)
    means, counts = call(
        functools.partial(mean_kernel, share),
        [like((share, features), BF16), like((share, features), F32)],
        moved=1 << 20,
    )(received)
    all_means = lax.all_gather(means, "near", axis=0, tiled=True)

    node = call(
        node_kernel,
        [narrow] * 8 + [cut_part] * 4 + [like((8, features), F32)],
        smem(1) + vmem(13),
        [pltpu.VMEM((rows, features), F32)],
        flops=10 * layer,
        moved=4 << 20,
    )
    (updated, aggregate, coarse, node_active, emit_grad, lifted_grad, aggregate_grad, coarse_grad,
     back0, back1, back2, back3, vectors) = node(
        target, clus, node_state, node_grad, local, *arrived, all_means, node_lift, node_bias_row,
        node_emit, gain_row,
    )
    returned = travel([back0, back1, back2, back3], -1)

    weights = call(
        functools.partial(weight_kernel, sizes),
        [like((peers, packed_rows, features), BF16), wide, wide],
        smem(1) + vmem(12),
        flops=8 * layer,
        moved=5 << 20,
    )
    packed, message_local, partial = weights(
        adjacency, clus, node_state, node_grad, aggregate, coarse, node_active, emit_grad,
        lifted_grad, aggregate_grad, coarse_grad, edge_blocks, node_lift,
    )
    anywhere = pl.BlockSpec(memory_space=pl.ANY)
    edge = call(
        functools.partial(edge_kernel, sizes),
        [like((peers, packed_rows, features), BF16), wide],
        smem(1) + vmem(13) + [anywhere],
        [
            pltpu.VMEM((rows, features), F32),
            pltpu.VMEM((rows, features), BF16),
            pltpu.VMEM((rows, features), BF16),
            pltpu.VMEM((peers, edge_rows + 16, features), BF16),
            pltpu.SemaphoreType.DMA,
        ],
        {14: 0},
        [anywhere] + vmem(1),
        flops=8 * layer,
        moved=5 << 20,
    )
    packed, partial = edge(
        source, node_state, lifted, active, message_local, *returned, cuts, edge_lift, edge_emit,
        partial, vectors, packed,
    )

    received = lax.all_to_all(packed, "near", 0, 0, tiled=True)
    pool, grads = call(
        functools.partial(split_kernel, share),
        [like((share, features), BF16), like((columns, chunk, features), BF16)],
        moved=1 << 20,
    )(received)
    received = lax.all_to_all(grads, "gy", 0, 0, tiled=True)
    joined = call(
        join_kernel, like((far, share + chunk, features), BF16), moved=1 << 20
    )(pool, received)
    received = lax.all_to_all(joined, "far", 0, 0, tiled=True)
    means, grads = call(
        functools.partial(settle_kernel, share),
        [like((share, features), BF16), like((columns, chunk, features), BF16)],
        moved=1 << 20,
    )(received, counts)
    grads = lax.all_to_all(grads, "gy", 0, 0, tiled=True).reshape(columns * chunk, features)
    gathered = lax.all_gather(
        jnp.concatenate([means, grads[:packed_rows - share]], axis=0), "near", axis=0, tiled=False
    )
    scale = float(rows * along * columns) ** (-0.5)
    square, line = like((features, features), F32), like((1, features), F32)
    (state_grad, edge_lift_grad, edge_bias_grad, edge_emit_grad, node_lift_grad, node_bias_grad,
     node_emit_grad, gain_grad) = call(
        functools.partial(last_kernel, sizes, scale),
        [narrow, square, line, square, like((3 * features, features), F32), line, square, line],
        vmem(3),
        [pltpu.VMEM((peers * share, features), BF16)],
        flops=3 * layer,
        moved=4 << 20,
    )(clus, partial, gathered)
    return (
        updated,
        state_grad,
        edge_lift_grad,
        edge_bias_grad.reshape(features),
        edge_emit_grad,
        node_lift_grad,
        node_bias_grad.reshape(features),
        node_emit_grad,
        gain_grad.reshape(features),
    )


def solution(mesh):
    gx, gy = mesh.shape["gx"], mesh.shape["gy"]
    near = 8 if gx % 8 == 0 and gx > 8 else 4
    grid = Mesh(mesh.devices.reshape(gx // near, near, gy), ("far", "near", "gy"))
    both, across = ("far", "near", "gy"), ("far", "near")
    placed = (
        P(both, None),
        P(both, None),
        P(both, None, None, None),
        P(both, None),
        P(across, "gy", None, None),
        P(across, "gy", None, None),
        P(across, "gy", None, None, None, None),
        P(both),
        P(),
        P(),
        P(),
        P(),
        P(),
        P(),
        P(),
    )
    return jax.shard_map(
        shards,
        mesh=grid,
        in_specs=placed,
        out_specs=(P(both, None), P(both, None), P(), P(), P(), P(), P(), P(), P()),
        check_vma=False,
    )
```

time: 825 us -> 216 us (0.26)
  waiting for transfers between devices: 430 us -> 30.3 us
  blocking collectives: 298 us -> 117 us
  matrix products: 24.5 us -> 0 us
  Pallas kernels: 0 us -> 12.6 us
  other arithmetic: 13.2 us -> 0.68 us
  local copies, waits for them, and re-layouts: 17.5 us -> 8.97 us
    psum x1 -> x0, waiting for transfers between devices: 411 us -> none  [shards(): lax.psum((edge_lift_grad, edge_bias_grad, edge_emit_grad, lift_grad, bias...]
    psum x1 -> x0, blocking collectives: 102 us -> none  [shards(): lax.psum((edge_lift_grad, edge_bias_grad, edge_emit_grad, lift_grad, bias...]
    all_to_all x0 -> x5, blocking collectives: none -> 95.8 us  [the longest x1 26.6 us: shards(): received = lax.all_to_all(packed, 'near', 0, 0, tiled=True)]
    unnamed x1 -> x0, blocking collectives: 87.9 us -> none
    all_gather x2 -> x1, blocking collectives: 109 us -> 21.1 us  [shards(): all_means = lax.all_gather(means, 'near', axis=0, tiled=True)]
    all_gather x0 -> x1, waiting for transfers between devices: none -> 25.4 us  [shards(): lax.all_gather(jnp.concatenate([means, grads[:packed_rows - share]], axis...]
    dot_general x28 -> x0, matrix products: 24.5 us -> none  [the longest x8 8.35 us: product_across(): lax.dot_general(left, right, (((0,), (0,)), ((), ())), preferred_element_...]
    reduce_scatter x2 -> x0, waiting for transfers between devices: 18.8 us -> none  [pool_group(): lax.psum_scatter(partial_sums.astype(jnp.bfloat16), 'gx', scatter_dimensi...]
  transfers between devices with their start and end apart: 11 -> 10, of which waited for: 2 -> 4; matrix products, arithmetic and copies ran while one was open for 4% -> 0% of each run, Pallas kernels for 0% -> 1%
where the time goes in v1:
time: 216 us; the launch traced here: 215 us
  blocking collectives  117 us (54%)
  starting transfers between devices  31.3 us (14%)
  waiting for transfers between devices  30.3 us (14%)
  between operations  14.4 us (7%)
  Pallas kernels  12.6 us (6%)
  local copies, waits for them, and re-layouts  8.97 us (4%)
    all_to_all x1, blocking collectives, shards(): received = lax.all_to_all(packed, 'near', 0, 0, tiled=True)  26.6 us
    all_to_all x1, blocking collectives, shards(): received = lax.all_to_all(joined, 'far', 0, 0, tiled=True)  26.3 us
    all_gather x1, waiting for transfers between devices, shards(): lax.all_gather(jnp.concatenate([means, grads[:packed_rows - share]], axis...  25.4 us
    all_gather x1, blocking collectives, shards(): all_means = lax.all_gather(means, 'near', axis=0, tiled=True)  21.1 us
    ppermute x8, starting transfers between devices, shift(): return lax.ppermute(value, axis, pairs)  20 us
    all_to_all x1, blocking collectives, shards(): received = lax.all_to_all(pool, 'near', 0, 0, tiled=True)  18.1 us
    all_to_all x1, blocking collectives, shards(): received = lax.all_to_all(grads, 'gy', 0, 0, tiled=True)  14.3 us
    all_to_all x1, starting transfers between devices, shards(): received = lax.all_to_all(summed, 'far', 0, 0, tiled=True)  11.3 us
  transfers between devices with their start and end apart: 10, of which 4 were waited for; matrix products, arithmetic and copies ran while one was open for 0% of the time, Pallas kernels for 1%

profile of v1, /device:TPU:1, one launch (start us, length us, event | category | flops | bytes accessed | tf_op | source)
XLA Modules:
  0.0 215.1 jit_solution(8051276656474000137)
XLA Ops:
  7.2 0.7 reshape.42.edge_bias
  7.8 0.8 copy.25.source
  8.6 0.9 copy-done
  9.6 1.0 copy-done.5
  10.5 0.9 copy-done.7
  11.5 0.9 copy-done.10
  12.4 0.9 copy-done.12
  13.3 0.7 copy-done.14
  14.0 0.7 copy-done.16
  14.7 2.0 shard_map.214
  16.7 0.0 copy-start.19
  16.7 0.0 copy-start.20
  16.7 0.0 copy-start.18
  16.7 0.0 copy-start.1
  16.8 0.0 copy-start.2
  16.8 0.0 copy-start.4
  16.8 0.0 copy-start.9
  16.8 0.0 copy-start.15
  16.8 18.1 %all_to_all.30.received = bf16[8,112,256]{2,1,0:T(8,128)(2,1)S(1)} all-to-all(bf16[8,112,256]{2,1,0:T(8,128)(2,1)S(1)} %get-tuple-element.54), channel_id=1, replica_groups=mesh['far'=4,'near'=8,'gy'=16] {'near'}, dimensions={0} | all-to-all | bytes 917504 | tf_op jit(solution)/shard_map/all_to_all | solution.py:389
  35.0 0.8 shard_map.215
  35.7 11.3 %all-to-all-start.1 = ((bf16[4,112,256]{2,1,0:T(8,128)(2,1)}), bf16[4,112,256]{2,1,0:T(8,128)(2,1)S(1)}, u32[]{:S(2)}, u32[]{:S(2)}) async-start(bf16[4,112,256]{2,1,0:T(8,128)(2,1)} %shard_map.215), calls=%async_computation.1 | async-start | bytes 458752 | tf_op jit(solution)/shard_map/all_to_all | solution.py:393
  47.0 0.0 all-gather.3.cloned.1.call-start
  47.0 3.3 %collective-permute-start = (bf16[256,256]{1,0:T(8,128)(2,1)S(1)}, bf16[256,256]{1,0:T(8,128)(2,1)S(1)}, u32[]{:S(2)}, u32[]{:S(2)}) collective-permute-start(bf16[256,256]{1,0:T(8,128)(2,1)S(1)} %get-tuple-element.50), channel_id=1, source_target_pairs={{0,16},{16,32},{32,48},{48,64},{64,80},{80,96},{96,112},{112,128},... | collective-permute-start | bytes 393224 | tf_op jit(solution)/shard_map/ppermute | solution.py:365
  50.3 1.9 collective-permute-start.1
  52.2 2.6 %collective-permute-start.2 = (bf16[256,256]{1,0:T(8,128)(2,1)S(1)}, bf16[256,256]{1,0:T(8,128)(2,1)S(1)}, u32[]{:S(2)}, u32[]{:S(2)}) collective-permute-start(bf16[256,256]{1,0:T(8,128)(2,1)S(1)} %get-tuple-element.52), channel_id=1, source_target_pairs={{0,1},{1,2},{2,3},{3,4},{4,5},{5,6},{6,7},{7,8},{8,9},{9,10},{10,1... | collective-permute-start | bytes 393224 | tf_op jit(solution)/shard_map/ppermute | solution.py:365
  54.9 1.3 collective-permute-start.3
  56.2 0.0 copy-done.19
  56.2 0.0 copy-done.20
  56.2 0.0 copy-done.18
  56.3 0.1 copy.26.target
  56.3 3.7 %all-to-all-done.1.received = bf16[4,112,256]{2,1,0:T(8,128)(2,1)S(1)} async-done(((bf16[4,112,256]{2,1,0:T(8,128)(2,1)}), bf16[4,112,256]{2,1,0:T(8,128)(2,1)S(1)}, u32[]{:S(2)}, u32[]{:S(2)}) %all-to-all-start.1) | async-done | bytes 229408 | tf_op jit(solution)/shard_map/all_to_all | solution.py:393
  60.0 0.1 shard_map.216
  60.2 21.1 %all_gather.9.means = bf16[768,256]{1,0:T(8,128)(2,1)S(1)} all-gather(bf16[96,256]{1,0:T(8,128)(2,1)S(1)} %get-tuple-element.55), channel_id=1, replica_groups=mesh['far'=4,'near'=8,'gy'=16] {'near'}, dimensions={0}, use_global_device_ids=true | all-gather | bytes 442368 | tf_op jit(solution)/shard_map/all_gather | solution.py:399
  81.2 0.0 collective-permute-done.arrived0
  81.2 0.0 collective-permute-done.1.arrived1
  81.2 0.0 collective-permute-done.2.arrived2
  81.2 0.0 collective-permute-done.3.arrived3
  81.3 0.0 copy-start.6
  81.3 0.0 copy-start.17
  81.3 4.6 %shard_map.217 = (bf16[512,256]{1,0:T(8,128)(2,1)}, bf16[512,256]{1,0:T(8,128)(2,1)S(1)}, bf16[512,256]{1,0:T(8,128)(2,1)S(1)}, bf16[512,256]{1,0:T(8,128)(2,1)S...) custom-call(s32[4,2]{1,0:T(4,128)S(1)} %copy.26.target, ...), custom_call_target="tpu_custom_call" | custom-call | flops 671088640 | bytes 4194304 | tf_op jit(solution)/shard_map/pallas_call | solution.py:410
  85.9 2.1 collective-permute-start.4
  88.0 3.5 %collective-permute-start.5 = (bf16[256,256]{1,0:T(8,128)(2,1)S(1)}, bf16[256,256]{1,0:T(8,128)(2,1)S(1)}, u32[]{:S(2)}, u32[]{:S(2)}) collective-permute-start(bf16[256,256]{1,0:T(8,128)(2,1)S(1)} %get-tuple-element.68), channel_id=1, source_target_pairs={{0,16},{16,32},{32,48},{48,64},{64,80},{80,96},{96,112},{112,128},... | collective-permute-start | bytes 393224 | tf_op jit(solution)/shard_map/ppermute | solution.py:365
  91.5 1.3 collective-permute-start.6
  92.8 4.0 %collective-permute-start.7 = (bf16[256,256]{1,0:T(8,128)(2,1)S(1)}, bf16[256,256]{1,0:T(8,128)(2,1)S(1)}, u32[]{:S(2)}, u32[]{:S(2)}) collective-permute-start(bf16[256,256]{1,0:T(8,128)(2,1)S(1)} %get-tuple-element.70), channel_id=1, source_target_pairs={{0,1},{1,2},{2,3},{3,4},{4,5},{5,6},{6,7},{7,8},{8,9},{9,10},{10,1... | collective-permute-start | bytes 393224 | tf_op jit(solution)/shard_map/ppermute | solution.py:365
  96.8 0.0 copy-start.8
  96.8 0.0 copy-start.11
  96.8 0.0 copy-start.13
  96.8 1.7 shard_map.218
  98.6 0.0 collective-permute-done.4.back0
  98.6 0.0 collective-permute-done.5.back1
  98.6 0.5 collective-permute-done.6.back2
  99.1 0.7 collective-permute-done.7.back3
  99.7 0.0 copy-done.8
  99.8 1.6 shard_map.219
  101.4 26.6 %all_to_all.31.received = bf16[8,304,256]{2,1,0:T(8,128)(2,1)S(1)} all-to-all(bf16[8,304,256]{2,1,0:T(8,128)(2,1)S(1)} %get-tuple-element.75), channel_id=1, replica_groups=mesh['far'=4,'near'=8,'gy'=16] {'near'}, dimensions={0} | all-to-all | bytes 2490368 | tf_op jit(solution)/shard_map/all_to_all | solution.py:449
  128.0 0.2 shard_map.220
  128.2 14.3 %all_to_all.32.received = bf16[16,16,256]{2,1,0:T(8,128)(2,1)S(1)} all-to-all(bf16[16,16,256]{2,1,0:T(8,128)(2,1)S(1)} %get-tuple-element.77), channel_id=1, replica_groups=mesh['far'=4,'near'=8,'gy'=16] {'gy'}, dimensions={0} | all-to-all | bytes 262144 | tf_op jit(solution)/shard_map/all_to_all | solution.py:455
  142.5 26.3 %all_to_all.33.received = bf16[4,112,256]{2,1,0:T(8,128)(2,1)S(1)} all-to-all(bf16[4,112,256]{2,1,0:T(8,128)(2,1)S(1)} %shard_map.221), channel_id=1, replica_groups=mesh['far'=4,'near'=8,'gy'=16] {'far'}, dimensions={0} | all-to-all | bytes 458752 | tf_op jit(solution)/shard_map/all_to_all | solution.py:459
  168.8 10.5 %all_to_all.34 = bf16[16,16,256]{2,1,0:T(8,128)(2,1)S(1)} all-to-all(bf16[16,16,256]{2,1,0:T(8,128)(2,1)S(1)} %get-tuple-element.80), channel_id=1, replica_groups=mesh['far'=4,'near'=8,'gy'=16] {'gy'}, dimensions={0} | all-to-all | bytes 262144 | tf_op jit(solution)/shard_map/all_to_all | solution.py:465
  179.3 0.7 pad_maximum_fusion
  180.0 0.0 all-gather.3.cloned.1.call-update
  180.0 25.4 %all-gather.3.cloned.1.call-done = bf16[2432,256]{1,0:T(8,128)(2,1)} async-done(((bf16[304,256]{1,0:T(8,128)(2,1)}), bf16[2432,256]{1,0:T(8,128)(2,1)}) %all-gather.3.cloned.1.call-update) | async-done | bytes 1245200 | tf_op jit(solution)/shard_map/all_gather | solution.py:466
  205.4 1.3 copy-done.3
  206.7 1.6 shard_map.223
  (22 shorter events, 0.1 us)
Async XLA Ops:
  8.6 0.9 copy-start
  9.6 1.0 copy-start.5
  10.5 0.9 copy-start.7
  11.5 0.9 copy-start.10
  12.4 0.9 copy-start.12
  13.3 0.7 copy-start.14
  14.0 0.7 copy-start.16
  16.7 39.5 %copy-start.19 = (bf16[256]{0:T(256)(128)(2,1)S(1)}, bf16[256]{0:T(256)(128)(2,1)}, u32[]{:S(2)}) copy-start(bf16[256]{0:T(256)(128)(2,1)} %param.27) | copy-start | bytes 1540
  16.7 39.5 %copy-start.20 = (bf16[256]{0:T(256)(128)(2,1)S(1)}, bf16[256]{0:T(256)(128)(2,1)}, u32[]{:S(2)}) copy-start(bf16[256]{0:T(256)(128)(2,1)} %param.29) | copy-start | bytes 1540
  16.7 39.5 %copy-start.18 = (s32[1,1,4,2]{2,3,1,0:T(2,128)S(1)}, s32[1,1,4,2]{2,3,1,0:T(2,128)}, u32[]{:S(2)}) copy-start(s32[1,1,4,2]{2,3,1,0:T(2,128)} %param.20) | copy-start | bytes 100
  16.7 64.5 %copy-start.1 = (bf16[512,256]{1,0:T(8,128)(2,1)S(1)}, bf16[512,256]{1,0:T(8,128)(2,1)}, u32[]{:S(2)}) copy-start(bf16[512,256]{1,0:T(8,128)(2,1)} %state.7) | copy-start | bytes 786436
  16.8 64.5 %copy-start.2 = (bf16[768,256]{1,0:T(8,128)(2,1)S(1)}, bf16[768,256]{1,0:T(8,128)(2,1)}, u32[]{:S(2)}) copy-start(bf16[768,256]{1,0:T(8,128)(2,1)} %node_lift.3) | copy-start | bytes 1179652
  16.8 64.5 %copy-start.4 = (bf16[512,256]{1,0:T(8,128)(2,1)S(1)}, bf16[512,256]{1,0:T(8,128)(2,1)}, u32[]{:S(2)}) copy-start(bf16[512,256]{1,0:T(8,128)(2,1)} %upstream.3) | copy-start | bytes 786436
  16.8 64.5 %copy-start.9 = (bf16[256,256]{1,0:T(8,128)(2,1)S(1)}, bf16[256,256]{1,0:T(8,128)(2,1)}, u32[]{:S(2)}) copy-start(bf16[256,256]{1,0:T(8,128)(2,1)} %node_emit.1) | copy-start | bytes 393220
  16.8 64.5 %copy-start.15 = (s32[512]{0:T(512)S(1)}, s32[512]{0:T(512)}, u32[]{:S(2)}) copy-start(s32[512]{0:T(512)} %param.22) | copy-start | bytes 6148
  35.7 24.3 %all-to-all-start.1 = ((bf16[4,112,256]{2,1,0:T(8,128)(2,1)}), bf16[4,112,256]{2,1,0:T(8,128)(2,1)S(1)}, u32[]{:S(2)}, u32[]{:S(2)}) async-start(bf16[4,112,256]{2,1,0:T(8,128)(2,1)} %shard_map.215), calls=%async_computation.1 | async-start | bytes 458752 | tf_op jit(solution)/shard_map/all_to_all | solution.py:393
  47.0 158.4 %all-gather.3.cloned.1.call-start = ((), (), s32[]{:S(2)}) async-start(), calls=%async_computation.6 | async-start | bytes 1400832 | tf_op jit(solution)/shard_map/all_gather | solution.py:466
  47.0 34.2 %collective-permute-start = (bf16[256,256]{1,0:T(8,128)(2,1)S(1)}, bf16[256,256]{1,0:T(8,128)(2,1)S(1)}, u32[]{:S(2)}, u32[]{:S(2)}) collective-permute-start(bf16[256,256]{1,0:T(8,128)(2,1)S(1)} %get-tuple-element.50), channel_id=1, source_target_pairs={{0,16},{16,32},{32,48},{48,64},{64,80},{80,96},{96,112},{112,128},... | collective-permute-start | bytes 393224 | tf_op jit(solution)/shard_map/ppermute | solution.py:365
  50.3 30.9 %collective-permute-start.1 = (bf16[256,256]{1,0:T(8,128)(2,1)S(1)}, bf16[256,256]{1,0:T(8,128)(2,1)S(1)}, u32[]{:S(2)}, u32[]{:S(2)}) collective-permute-start(bf16[256,256]{1,0:T(8,128)(2,1)S(1)} %get-tuple-element.51), channel_id=1, source_target_pairs={{16,0},{32,16},{48,32},{64,48},{80,64},{96,80},{112,96},{128,112},... | collective-permute-start | bytes 393224 | tf_op jit(solution)/shard_map/ppermute | solution.py:365
  52.2 29.0 %collective-permute-start.2 = (bf16[256,256]{1,0:T(8,128)(2,1)S(1)}, bf16[256,256]{1,0:T(8,128)(2,1)S(1)}, u32[]{:S(2)}, u32[]{:S(2)}) collective-permute-start(bf16[256,256]{1,0:T(8,128)(2,1)S(1)} %get-tuple-element.52), channel_id=1, source_target_pairs={{0,1},{1,2},{2,3},{3,4},{4,5},{5,6},{6,7},{7,8},{8,9},{9,10},{10,1... | collective-permute-start | bytes 393224 | tf_op jit(solution)/shard_map/ppermute | solution.py:365
  54.9 26.3 %collective-permute-start.3 = (bf16[256,256]{1,0:T(8,128)(2,1)S(1)}, bf16[256,256]{1,0:T(8,128)(2,1)S(1)}, u32[]{:S(2)}, u32[]{:S(2)}) collective-permute-start(bf16[256,256]{1,0:T(8,128)(2,1)S(1)} %get-tuple-element.53), channel_id=1, source_target_pairs={{1,0},{2,1},{3,2},{4,3},{5,4},{6,5},{7,6},{8,7},{9,8},{10,9},{11,1... | collective-permute-start | bytes 393224 | tf_op jit(solution)/shard_map/ppermute | solution.py:365
  81.3 15.5 %copy-start.6 = (bf16[4,3,128,128]{3,2,1,0:T(8,128)(2,1)S(1)}, bf16[4,3,128,128]{3,2,1,0:T(8,128)(2,1)}, u32[]{:S(2)}) copy-start(bf16[4,3,128,128]{3,2,1,0:T(8,128)(2,1)} %blocks.3) | copy-start | bytes 1179652
  81.3 15.5 %copy-start.17 = (s32[4,3]{1,0:T(4,128)S(1)}, s32[4,3]{1,0:T(4,128)}, u32[]{:S(2)}) copy-start(s32[4,3]{1,0:T(4,128)} %adjacency.3) | copy-start | bytes 148
  85.9 12.6 %collective-permute-start.4 = (bf16[256,256]{1,0:T(8,128)(2,1)S(1)}, bf16[256,256]{1,0:T(8,128)(2,1)S(1)}, u32[]{:S(2)}, u32[]{:S(2)}) collective-permute-start(bf16[256,256]{1,0:T(8,128)(2,1)S(1)} %get-tuple-element.67), channel_id=1, source_target_pairs={{16,0},{32,16},{48,32},{64,48},{80,64},{96,80},{112,96},{128,112},... | collective-permute-start | bytes 393224 | tf_op jit(solution)/shard_map/ppermute | solution.py:365
  88.0 10.6 %collective-permute-start.5 = (bf16[256,256]{1,0:T(8,128)(2,1)S(1)}, bf16[256,256]{1,0:T(8,128)(2,1)S(1)}, u32[]{:S(2)}, u32[]{:S(2)}) collective-permute-start(bf16[256,256]{1,0:T(8,128)(2,1)S(1)} %get-tuple-element.68), channel_id=1, source_target_pairs={{0,16},{16,32},{32,48},{48,64},{64,80},{80,96},{96,112},{112,128},... | collective-permute-start | bytes 393224 | tf_op jit(solution)/shard_map/ppermute | solution.py:365
  91.5 7.6 %collective-permute-start.6 = (bf16[256,256]{1,0:T(8,128)(2,1)S(1)}, bf16[256,256]{1,0:T(8,128)(2,1)S(1)}, u32[]{:S(2)}, u32[]{:S(2)}) collective-permute-start(bf16[256,256]{1,0:T(8,128)(2,1)S(1)} %get-tuple-element.69), channel_id=1, source_target_pairs={{1,0},{2,1},{3,2},{4,3},{5,4},{6,5},{7,6},{8,7},{9,8},{10,9},{11,1... | collective-permute-start | bytes 393224 | tf_op jit(solution)/shard_map/ppermute | solution.py:365
  92.8 7.0 %collective-permute-start.7 = (bf16[256,256]{1,0:T(8,128)(2,1)S(1)}, bf16[256,256]{1,0:T(8,128)(2,1)S(1)}, u32[]{:S(2)}, u32[]{:S(2)}) collective-permute-start(bf16[256,256]{1,0:T(8,128)(2,1)S(1)} %get-tuple-element.70), channel_id=1, source_target_pairs={{0,1},{1,2},{2,3},{3,4},{4,5},{5,6},{6,7},{7,8},{8,9},{9,10},{10,1... | collective-permute-start | bytes 393224 | tf_op jit(solution)/shard_map/ppermute | solution.py:365
  96.8 2.9 %copy-start.8 = (bf16[1,1,4,2,128,128]{5,4,3,2,1,0:T(8,128)(2,1)S(1)}, bf16[1,1,4,2,128,128]{5,4,3,2,1,0:T(8,128)(2,1)}, u32[]{:S(2)}) copy-start(bf16[1,1,4,2,128,128]{5,4,3,2,1,0:T(8,128)(2,1)} %param.21) | copy-start | bytes 786436
  96.8 2.9 %copy-start.11 = (bf16[256,256]{1,0:T(8,128)(2,1)S(1)}, bf16[256,256]{1,0:T(8,128)(2,1)}, u32[]{:S(2)}) copy-start(bf16[256,256]{1,0:T(8,128)(2,1)} %edge_lift.3) | copy-start | bytes 393220
  96.8 2.9 %copy-start.13 = (bf16[256,256]{1,0:T(8,128)(2,1)S(1)}, bf16[256,256]{1,0:T(8,128)(2,1)}, u32[]{:S(2)}) copy-start(bf16[256,256]{1,0:T(8,128)(2,1)} %edge_emit.3) | copy-start | bytes 393220
  205.4 1.3 copy-start.3
Sparse Core Ops, SparseCore 0:
  180.1 25.2 all-gather.2

commit v2 on v1

v2 whole, which is shorter than its diff:
```python
import functools

import jax
import jax.numpy as jnp
from jax import lax
from jax.experimental import pallas as pl
from jax.experimental.pallas import tpu as pltpu
from jax.sharding import Mesh
from jax.sharding import PartitionSpec as P

CLUS_DEV = 24
NORM_EPS = 1e-05
TILE = 128
F32 = jnp.float32
BF16 = jnp.bfloat16
VMEM_LIMIT = 24 * 1024 * 1024
FIRST_LIMIT = 60 * 1024 * 1024


def mm(left, right):
    return jnp.dot(left, right, preferred_element_type=F32)


def mm_tn(left, right):
    return lax.dot_general(left, right, (((0,), (0,)), ((), ())), preferred_element_type=F32)


def mm_nt(left, right):
    return lax.dot_general(left, right, (((1,), (1,)), ((), ())), preferred_element_type=F32)


def tile_rows(index):
    return pl.ds(pl.multiple_of(index * TILE, TILE), TILE)


def rows_of(tile):
    return slice(tile * TILE, (tile + 1) * TILE)


def hot_rows(clus_row, first, count):
    ids = lax.broadcasted_iota(jnp.int32, (count, clus_row.shape[1]), 0) + first
    return jnp.where(ids == clus_row, 1.0, 0.0).astype(BF16)


def hot_columns(clus_row, clusters):
    spread = jnp.broadcast_to(clus_row.astype(F32), (TILE, TILE)).T
    spread = jnp.concatenate([spread] * (-(-clusters // TILE)), axis=1)[:, :clusters]
    ids = lax.broadcasted_iota(jnp.int32, (TILE, clusters), 1).astype(F32)
    return jnp.where(ids == spread, 1.0, 0.0).astype(BF16)


def slots(side):
    near, gy = lax.axis_index("core"), lax.rem(lax.axis_index("gy"), 2)
    out = (1 - near, 3 - gy, 2 + gy, near)
    return out if side == "out" else (near, 2 + gy, 3 - gy, 1 - near)


def call(kernel, outs, in_specs=None, scratch=(), limit=VMEM_LIMIT, out_specs=None, flops=0, moved=0):
    options = {}
    if in_specs is not None:
        options["in_specs"] = in_specs
    if out_specs is not None:
        options["out_specs"] = out_specs
    return pl.pallas_call(
        kernel,
        out_shape=outs,
        scratch_shapes=list(scratch),
        compiler_params=pltpu.CompilerParams(vmem_limit_bytes=limit),
        cost_estimate=pl.CostEstimate(flops=flops, bytes_accessed=moved, transcendentals=0),
        **options,
    )


def vmem(count):
    return [pl.BlockSpec(memory_space=pltpu.VMEM)] * count


def smem(count):
    return [pl.BlockSpec(memory_space=pltpu.SMEM)] * count


def like(shape, kind):
    return jax.ShapeDtypeStruct(shape, kind)


def front_kernel(share, *refs):
    far, refs = refs[:11], refs[11:]
    (pool, part0, part1, part2, part3, lifted, active, local, params), refs = refs[:9], refs[9:]
    near, (message, sems) = refs[:11], refs[11:]
    copies = [
        pltpu.make_async_copy(*pair, sems.at[index])
        for index, pair in enumerate(zip(far, near))
    ]
    for copy in copies:
        copy.start()
    (clus, state, edge_bias, node_bias, norm_gain, edge_lift, edge_emit, source, adjacency, cuts,
     blocks) = near
    rows, features = state.shape
    tiles = rows // TILE
    for copy in copies[:2]:
        copy.wait()
    clus_row = clus[...]
    ones = jnp.ones((16, rows), BF16)
    line = lax.broadcasted_iota(jnp.int32, (16, TILE), 0)
    for peer in range(pool.shape[0]):
        hot = hot_rows(clus_row, peer * share, TILE)
        pool[peer, 0:share] = mm(hot, state[...])[:share].astype(BF16)
        count = mm_nt(ones, hot)
        eights = jnp.floor(count * 0.125)
        high = jnp.floor(eights * 0.125)
        digits = jnp.where(
            line < 4, count - 8.0 * eights, jnp.where(line < 8, eights - 8.0 * high, high)
        )
        pool[peer, share:share + 16, 0:TILE] = digits.astype(BF16)
        pool[peer, share:share + 16, TILE:] = jnp.zeros((16, features - TILE), BF16)
    for copy in copies[2:]:
        copy.wait()
    params[...] = jnp.zeros(params.shape, F32)
    for index, vector in enumerate((node_bias, norm_gain)):
        params[index:index + 1] = vector[...].astype(F32).reshape(1, -1)
    bias = edge_bias[...].astype(F32).reshape(1, -1)
    for tile in range(tiles):
        rows = rows_of(tile)
        value = (mm(state[rows], edge_lift[...]) + bias).astype(BF16)
        lifted[rows] = value
        wide = value.astype(F32)
        hidden = (wide * jax.nn.sigmoid(wide)).astype(BF16)
        active[rows] = hidden
        message[rows] = mm(hidden, edge_emit[...]).astype(BF16)
    for slot, part in zip(slots("out"), (part0, part1, part2, part3)):
        for cut in range(cuts.shape[1]):
            part[rows_of(cut)] = mm(
                cuts[slot, cut], message[tile_rows(source[cut, slot])]
            ).astype(BF16)
    for tile in range(tiles):
        total = mm(blocks[tile, 0], message[tile_rows(adjacency[tile, 0])])
        for slot in range(1, blocks.shape[1]):
            total += mm(blocks[tile, slot], message[tile_rows(adjacency[tile, slot])])
        local[rows_of(tile)] = total


def aggregate_kernel(target, local, arrived0, arrived1, arrived2, arrived3, aggregate, summed):
    summed[...] = local[...]
    for slot, arrived in zip(slots("in"), (arrived0, arrived1, arrived2, arrived3)):
        for cut in range(arrived.shape[0] // TILE):
            summed[tile_rows(target[cut, slot])] += arrived[rows_of(cut)].astype(F32)
    aggregate[...] = summed[...].astype(BF16)


def sum_kernel(received, out):
    total = jnp.sum(received[...].astype(F32), axis=0).astype(BF16)
    for peer in range(out.shape[0]):
        out[peer] = total


def mean_kernel(share, received, means, counts):
    total = jnp.sum(received[...].astype(F32), axis=0)
    low, middle, high = (total[share + row:share + row + 1, 0:TILE] for row in (0, 4, 8))
    count = jnp.broadcast_to(high * 64.0 + middle * 8.0 + low, (TILE, TILE)).T[:share]
    count = jnp.concatenate([count] * (means.shape[2] // TILE), axis=1)
    counts[...] = count
    mean = (total[:share] / count).astype(BF16)
    for peer in range(means.shape[0]):
        means[peer] = mean


def node_kernel(target, clus, state, upstream, aggregate, mine, other, node_lift, node_emit, params,
                updated, coarse, active, emit_grad, lifted_grad, aggregate_grad,
                coarse_grad, back0, back1, back2, back3, vectors, means):
    features = state.shape[1]
    clusters, share = means.shape[0], mine.shape[1]
    core = lax.axis_index("core")
    for peer in range(clusters // share):
        means[peer * share:(peer + 1) * share] = jnp.where(
            core == peer % 2, mine[peer // 2], other[peer // 2]
        )
    lift_state = node_lift[0:features]
    lift_agg = node_lift[features:2 * features]
    lift_coarse = node_lift[2 * features:]
    bias = params[0:1]
    gain = params[1:2]
    gain_grad = jnp.zeros((1, features), F32)
    bias_grad = jnp.zeros((1, features), F32)
    for tile in range(state.shape[0] // TILE):
        rows = rows_of(tile)
        here = state[rows]
        agg = aggregate[rows]
        hot = hot_columns(clus[0:1, rows], clusters)
        pooled = mm(hot, means[...]).astype(BF16)
        coarse[rows] = pooled
        lifted = (
            mm(here, lift_state) + mm(agg, lift_agg) + mm(pooled, lift_coarse) + bias
        ).astype(BF16).astype(F32)
        gate = jax.nn.sigmoid(lifted)
        hidden = (lifted * gate).astype(BF16)
        active[rows] = hidden
        emitted = mm(hidden, node_emit[...])
        center = emitted - jnp.mean(emitted, axis=-1, keepdims=True)
        inverse = lax.rsqrt(jnp.mean(center * center, axis=-1, keepdims=True) + NORM_EPS)
        normed = center * inverse
        updated[rows] = (here.astype(F32) + gain * normed).astype(BF16)
        above = upstream[rows].astype(F32)
        gain_grad += jnp.sum(above * normed, axis=0, keepdims=True)
        scaled = above * gain
        grad = (
            inverse
            * (
                scaled
                - jnp.mean(scaled, axis=-1, keepdims=True)
                - normed * jnp.mean(scaled * normed, axis=-1, keepdims=True)
            )
        ).astype(BF16)
        emit_grad[rows] = grad
        active_grad = mm_nt(grad, node_emit[...]).astype(BF16).astype(F32)
        slope = gate * (1.0 + lifted * (1.0 - gate))
        down = (active_grad * slope).astype(BF16)
        lifted_grad[rows] = down
        bias_grad += jnp.sum(down.astype(F32), axis=0, keepdims=True)
        aggregate_grad[rows] = mm_nt(down, lift_agg).astype(BF16)
        coarse_grad[rows] = mm_nt(down, lift_coarse).astype(BF16)
    for slot, back in zip(slots("in"), (back0, back1, back2, back3)):
        for cut in range(back.shape[0] // TILE):
            back[rows_of(cut)] = aggregate_grad[tile_rows(target[cut, slot])]
    vectors[...] = jnp.zeros(vectors.shape, F32)
    vectors[0:1] = bias_grad
    vectors[1:2] = gain_grad


def put_chunks(packed, first, size, start, value):
    done = 0
    while done < value.shape[0]:
        peer, offset = divmod(start + done, size)
        count = min(size - offset, value.shape[0] - done)
        packed[peer, first + offset:first + offset + count] = value[done:done + count].astype(BF16)
        done += count


def part_ways(stack, keep, send):
    core = lax.axis_index("core")
    for index in range(keep.shape[0]):
        keep[index] = stack[2 * index + core]
        send[index] = stack[2 * index + 1 - core]


def weight_kernel(sizes, adjacency, clus, state, upstream, aggregate, coarse, active, emit_grad,
                  lifted_grad, aggregate_grad, coarse_grad, blocks, node_lift,
                  keep, send, local, partial, stack):
    peers, share, node_rows, _ = sizes
    features = state.shape[1]
    clus_row = clus[...]
    for peer in range(peers):
        stack[peer, 0:share] = mm(
            hot_rows(clus_row, peer * share, share), coarse_grad[...]
        ).astype(BF16)
    down = lifted_grad[...]
    for index, block in enumerate((state, aggregate, coarse)):
        put_chunks(stack, share, node_rows, index * features, mm_tn(block[...], down))
    put_chunks(stack, share, node_rows, 3 * features, mm_tn(active[...], emit_grad[...]))
    part_ways(stack, keep, send)
    local[...] = jnp.zeros(local.shape, F32)
    for tile in range(state.shape[0] // TILE):
        rows = rows_of(tile)
        for slot in range(blocks.shape[1]):
            local[tile_rows(adjacency[tile, slot])] += mm_tn(
                blocks[tile, slot], aggregate_grad[rows]
            )
        partial[rows] = upstream[rows].astype(F32) + mm_nt(
            lifted_grad[rows], node_lift[0:features]
        )


def edge_kernel(sizes, source, state, lifted, active, local, back0, back1, back2, back3, cuts,
                edge_lift, edge_emit, partial, vectors,
                keep, send, partial_out, total, message_grad, lifted_grad, edge_part):
    peers, _, _, edge_rows = sizes
    features = state.shape[1]
    total[...] = local[...]
    for slot, back in zip(slots("out"), (back0, back1, back2, back3)):
        for cut in range(cuts.shape[1]):
            total[tile_rows(source[cut, slot])] += mm_tn(cuts[slot, cut], back[rows_of(cut)])
    bias_grad = jnp.zeros((1, features), F32)
    for tile in range(state.shape[0] // TILE):
        rows = rows_of(tile)
        grad = total[rows].astype(BF16)
        message_grad[rows] = grad
        active_grad = mm_nt(grad, edge_emit[...]).astype(BF16).astype(F32)
        wide = lifted[rows].astype(F32)
        gate = jax.nn.sigmoid(wide)
        down = (active_grad * (gate * (1.0 + wide * (1.0 - gate)))).astype(BF16)
        lifted_grad[rows] = down
        bias_grad += jnp.sum(down.astype(F32), axis=0, keepdims=True)
        partial_out[rows] = partial[rows] + mm_nt(down, edge_lift[...])
    put_chunks(edge_part, 0, edge_rows, 0, mm_tn(state[...], lifted_grad[...]))
    put_chunks(edge_part, 0, edge_rows, features, mm_tn(active[...], message_grad[...]))
    edge_part[:, edge_rows:] = jnp.zeros((peers, 16, features), BF16)
    last = lax.broadcasted_iota(jnp.int32, (16, features), 0)
    edge_part[0, edge_rows:] = jnp.where(
        last == 0, vectors[0:1], jnp.where(last == 1, vectors[1:2], jnp.where(last == 2, bias_grad, 0.0))
    ).astype(BF16)
    part_ways(edge_part, keep, send)


def merge_kernel(keep_node, keep_edge, got_node, got_edge, out):
    rows = keep_node.shape[1]
    out[:, 0:rows] = (keep_node[...].astype(F32) + got_node[...].astype(F32)).astype(BF16)
    out[:, rows:] = (keep_edge[...].astype(F32) + got_edge[...].astype(F32)).astype(BF16)


def split_kernel(share, received, pool, grads):
    total = jnp.sum(received[...].astype(F32), axis=0).astype(BF16)
    pool[...] = total[:share]
    chunk = grads.shape[1]
    row = 0
    while row < total.shape[0] - share:
        index, offset = divmod(row, chunk)
        grads[index, offset:offset + 16] = total[share + row:share + row + 16]
        row += 16
    while row < grads.shape[0] * chunk:
        index, offset = divmod(row, chunk)
        grads[index, offset:offset + 16] = jnp.zeros((16, grads.shape[2]), BF16)
        row += 16


def join_kernel(pool, received, out):
    share = pool.shape[0]
    grads = jnp.sum(received[...].astype(F32), axis=0).astype(BF16)
    for peer in range(out.shape[0]):
        out[peer, 0:share] = pool[...]
        out[peer, share:] = grads


def settle_kernel(share, received, counts, means, grads):
    total = jnp.sum(received[...].astype(F32), axis=0)
    means[...] = (total[:share] / counts[...]).astype(BF16)
    whole = total[share:].astype(BF16)
    for index in range(grads.shape[0]):
        grads[index] = whole


def spread_kernel(means, grads, out):
    share, used = means.shape[0], out.shape[1] - means.shape[0]
    chunk = grads.shape[1]
    for peer in range(out.shape[0]):
        out[peer, 0:share] = means[...]
        for first in range(0, used, chunk):
            count = min(chunk, used - first)
            out[peer, share + first:share + first + count] = grads[first // chunk, 0:count]


def last_kernel(sizes, scale, clus, partial, mine, other, state_grad, edge_lift, edge_bias,
                edge_emit, node_lift, node_bias, node_emit, norm_gain, means):
    peers, share, node_rows, edge_rows = sizes
    features = partial.shape[1]
    core = lax.axis_index("core")

    def gathered(peer, first, count):
        rows = slice(first, first + count)
        return jnp.where(core == peer % 2, mine[peer // 2, rows], other[peer // 2, rows])

    for peer in range(peers):
        means[peer * share:(peer + 1) * share] = gathered(peer, 0, share)
    for tile in range(partial.shape[0] // TILE):
        rows = rows_of(tile)
        pooled = mm(hot_columns(clus[0:1, rows], peers * share), means[...])
        state_grad[rows] = (partial[rows] + pooled).astype(BF16)

    def take(first, size, outs):
        start = 0
        for out in outs:
            done = 0
            while done < out.shape[0]:
                peer, offset = divmod(start + done, size)
                count = min(size - offset, out.shape[0] - done)
                out[done:done + count] = gathered(peer, first + offset, count).astype(F32) * scale
                done += count
            start += done

    take(share, node_rows, (node_lift, node_emit))
    take(share + node_rows, edge_rows, (edge_lift, edge_emit))
    tail = gathered(0, share + node_rows + edge_rows, 16).astype(F32) * scale
    node_bias[...] = tail[0:1]
    norm_gain[...] = tail[1:2]
    edge_bias[...] = tail[2:3]


def shards(
    node_state,
    node_grad,
    edge_blocks,
    adjacency,
    cut_source,
    cut_target,
    cut_blocks,
    clusters,
    edge_lift,
    edge_bias,
    edge_emit,
    node_lift,
    node_bias,
    node_emit,
    norm_gain,
):
    near = ("y", "core")
    far, across, columns = (lax.axis_size(name) for name in ("far", "y", "gy"))
    peers = 2 * across
    rows, features = node_state.shape
    along = far * peers
    share = CLUS_DEV * far
    node_rows = 4 * features // peers
    edge_rows = 2 * features // peers
    sizes = (peers, share, node_rows, edge_rows)
    packed_rows = share + node_rows + edge_rows + 16
    chunk = -(-(packed_rows - share) // (16 * columns)) * 16
    source, target = cut_source[0, 0].T, cut_target[0, 0].T
    cuts = cut_blocks[0, 0]
    cut_rows = cuts.shape[1] * TILE
    clus = clusters.reshape(1, rows)
    wide = like((rows, features), F32)
    narrow = like((rows, features), BF16)
    cut_part = like((cut_rows, features), BF16)
    layer = 2 * rows * features * features

    gx = ("far", *near)
    both_cores = [(0, 1), (1, 0)]

    def swap(parts):
        moved = []
        for part, axis, count, first in zip(
            parts, (gx, "gy", "gy", gx), (along, columns, columns, along), (1, 1, 0, 0)
        ):
            pairs = [(i, i + 1) for i in range(first, count - 1, 2)]
            moved.append(lax.ppermute(part, axis, pairs + [(j, i) for i, j in pairs]))
        return moved

    operands = (clus, node_state, edge_bias, node_bias, norm_gain, edge_lift, edge_emit, source,
                adjacency, cuts, edge_blocks)
    tables = (source, adjacency)
    pool, part0, part1, part2, part3, lifted, active, local, params = call(
        functools.partial(front_kernel, share),
        [like((peers, share + 16, features), BF16)] + [cut_part] * 4
        + [narrow, narrow, wide, like((8, features), F32)],
        [pl.BlockSpec(memory_space=pl.ANY)] * len(operands),
        [
            (pltpu.SMEM if any(v is table for table in tables) else pltpu.VMEM)(v.shape, v.dtype)
            for v in operands
        ]
        + [pltpu.VMEM((rows, features), BF16), pltpu.SemaphoreType.DMA((len(operands),))],
        FIRST_LIMIT,
        out_specs=vmem(9),
        flops=8 * layer,
        moved=4 << 20,
    )(*operands)
    received = lax.all_to_all(pool, near, 0, 0, tiled=True)
    summed = call(
        sum_kernel,
        like((far, share + 16, features), BF16),
        vmem(1),
        out_specs=pl.BlockSpec(memory_space=pltpu.VMEM),
        moved=1 << 20,
    )(received)
    arrived = swap((part0, part1, part2, part3))
    received = lax.all_to_all(summed, "far", 0, 0, tiled=True)
    received, *arrived = lax.optimization_barrier((received, *arrived))
    means, counts = call(
        functools.partial(mean_kernel, share),
        [like((across, share, features), BF16), like((share, features), F32)],
        vmem(1),
        out_specs=vmem(2),
        moved=1 << 20,
    )(received)
    my_means = lax.all_to_all(means, "y", 0, 0, tiled=True)
    other_means = lax.ppermute(my_means, "core", both_cores)
    local, my_means, *arrived = lax.optimization_barrier((local, my_means, *arrived))
    aggregate = call(
        aggregate_kernel,
        narrow,
        smem(1) + vmem(5),
        [pltpu.VMEM((rows, features), F32)],
        moved=2 << 20,
    )(target, local, *arrived)

    (updated, coarse, node_active, emit_grad, lifted_grad, aggregate_grad, coarse_grad,
     back0, back1, back2, back3, vectors) = call(
        node_kernel,
        [narrow] * 7 + [cut_part] * 4 + [like((8, features), F32)],
        smem(1) + vmem(9),
        [pltpu.VMEM((peers * share, features), BF16)],
        flops=10 * layer,
        moved=4 << 20,
    )(target, clus, node_state, node_grad, aggregate, my_means, other_means, node_lift, node_emit,
      params)

    keep_node, send_node, message_local, partial = call(
        functools.partial(weight_kernel, sizes),
        [like((across, share + node_rows, features), BF16)] * 2 + [wide, wide],
        smem(1) + vmem(12),
        [pltpu.VMEM((peers, share + node_rows, features), BF16)],
        flops=8 * layer,
        moved=5 << 20,
    )(adjacency, clus, node_state, node_grad, aggregate, coarse, node_active, emit_grad,
      lifted_grad, aggregate_grad, coarse_grad, edge_blocks, node_lift)
    returned = swap((back0, back1, back2, back3))
    send_node, *returned = lax.optimization_barrier((send_node, *returned))
    got_node = lax.ppermute(send_node, "core", both_cores)
    keep_edge, send_edge, partial = call(
        functools.partial(edge_kernel, sizes),
        [like((across, edge_rows + 16, features), BF16)] * 2 + [wide],
        smem(1) + vmem(13),
        [
            pltpu.VMEM((rows, features), F32),
            pltpu.VMEM((rows, features), BF16),
            pltpu.VMEM((rows, features), BF16),
            pltpu.VMEM((peers, edge_rows + 16, features), BF16),
        ],
        flops=8 * layer,
        moved=5 << 20,
    )(source, node_state, lifted, active, message_local, *returned, cuts, edge_lift, edge_emit,
      partial, vectors)
    got_edge = lax.ppermute(send_edge, "core", both_cores)
    merged = call(
        merge_kernel, like((across, packed_rows, features), BF16), vmem(4), moved=2 << 20
    )(keep_node, keep_edge, got_node, got_edge)
    received = lax.all_to_all(merged, "y", 0, 0, tiled=True)
    pool, grads = call(
        functools.partial(split_kernel, share),
        [like((share, features), BF16), like((columns, chunk, features), BF16)],
        vmem(1),
        moved=1 << 20,
    )(received)
    received = lax.all_to_all(grads, "gy", 0, 0, tiled=True)
    joined = call(
        join_kernel, like((far, share + chunk, features), BF16), vmem(2), moved=1 << 20
    )(pool, received)
    received = lax.all_to_all(joined, "far", 0, 0, tiled=True)
    means, grads = call(
        functools.partial(settle_kernel, share),
        [like((share, features), BF16), like((columns, chunk, features), BF16)],
        vmem(2),
        moved=1 << 20,
    )(received, counts)
    grads = lax.all_to_all(grads, "gy", 0, 0, tiled=True)
    spread = call(
        spread_kernel, like((across, packed_rows, features), BF16), vmem(2), moved=2 << 20
    )(means, grads)
    mine = lax.all_to_all(spread, "y", 0, 0, tiled=True)
    other = lax.ppermute(mine, "core", both_cores)
    scale = float(rows * along * columns) ** (-0.5)
    square, line = like((features, features), F32), like((1, features), F32)
    (state_grad, edge_lift_grad, edge_bias_grad, edge_emit_grad, node_lift_grad, node_bias_grad,
     node_emit_grad, gain_grad) = call(
        functools.partial(last_kernel, sizes, scale),
        [narrow, square, line, square, like((3 * features, features), F32), line, square, line],
        vmem(4),
        [pltpu.VMEM((peers * share, features), BF16)],
        flops=3 * layer,
        moved=4 << 20,
    )(clus, partial, mine, other)
    return (
        updated,
        state_grad,
        edge_lift_grad,
        edge_bias_grad.reshape(features),
        edge_emit_grad,
        node_lift_grad,
        node_bias_grad.reshape(features),
        node_emit_grad,
        gain_grad.reshape(features),
    )


def solution(mesh):
    gx, gy = mesh.shape["gx"], mesh.shape["gy"]
    near = 8 if gx % 8 == 0 and gx > 8 else 4
    grid = Mesh(
        mesh.devices.reshape(gx // near, near // 2, 2, gy), ("far", "y", "core", "gy")
    )
    across = ("far", "y", "core")
    both = (*across, "gy")
    placed = (
        P(both, None),
        P(both, None),
        P(both, None, None, None),
        P(both, None),
        P(across, "gy", None, None),
        P(across, "gy", None, None),
        P(across, "gy", None, None, None, None),
        P(both),
        P(),
        P(),
        P(),
        P(),
        P(),
        P(),
        P(),
    )
    return jax.shard_map(
        shards,
        mesh=grid,
        in_specs=placed,
        out_specs=(P(both, None), P(both, None), P(), P(), P(), P(), P(), P(), P()),
        check_vma=False,
    )
```

time: 216 us -> 188 us (0.87)
  waiting for transfers between devices: 30.3 us -> 8.87 us
  starting transfers between devices: 31.3 us -> 50.9 us
  between operations: 14.4 us -> 0.99 us
  blocking collectives: 117 us -> 108 us
  local copies, waits for them, and re-layouts: 8.97 us -> 2.44 us
  Pallas kernels: 12.6 us -> 15.5 us
    all_gather x1 -> x0, waiting for transfers between devices: 25.4 us -> none  [shards(): lax.all_gather(jnp.concatenate([means, grads[:packed_rows - share]], axis...]
    all_gather x1 -> x0, blocking collectives: 21.1 us -> none  [shards(): all_means = lax.all_gather(means, 'near', axis=0, tiled=True)]
    ppermute x8 -> x12, starting transfers between devices: 20 us -> 40.3 us  [the longest x8 21.4 us: swap(): moved.append(lax.ppermute(part, axis, pairs + [(j, i) for i, j in pairs]))]
    all_to_all x3 -> x5, blocking collectives: 55.2 us -> 69.6 us  [the longest x1 19 us: shards(): received = lax.all_to_all(pool, near, 0, 0, tiled=True)]
    ppermute x8 -> x12, waiting for transfers between devices: 1.19 us -> 8.87 us  [the longest x8 5.85 us: swap(): moved.append(lax.ppermute(part, axis, pairs + [(j, i) for i, j in pairs]))]
    unnamed x42 -> x40, local copies, waits for them, and re-layouts: 7.44 us -> 2.44 us
    all_to_all x1, waiting for transfers between devices: 3.7 us -> 0.01 us  [shards(): received = lax.all_to_all(summed, 'far', 0, 0, tiled=True)]
    pallas_call x7 -> x10, Pallas kernels: 10.8 us -> 13.8 us  [the longest x1 4.65 us: shards(): call(node_kernel, [narrow] * 7 + [cut_part] * 4 + [like((8, features), F3...]
  transfers between devices with their start and end apart: 10 -> 13, of which waited for: 4 -> 3; matrix products, arithmetic and copies ran while one was open for 0% -> 0% of each run, Pallas kernels for 1% -> 2%
where the time goes in v2:
time: 188 us; the launch traced here: 187 us
  blocking collectives  108 us (57%)
  starting transfers between devices  50.9 us (27%)
  Pallas kernels  15.5 us (8%)
  waiting for transfers between devices  8.87 us (5%)
  local copies, waits for them, and re-layouts  2.44 us (1%)
    all_to_all x1, blocking collectives, shards(): received = lax.all_to_all(joined, 'far', 0, 0, tiled=True)  25.3 us
    ppermute x8, starting transfers between devices, swap(): moved.append(lax.ppermute(part, axis, pairs + [(j, i) for i, j in pairs]))  21.4 us
    all_to_all x1, blocking collectives, shards(): received = lax.all_to_all(pool, near, 0, 0, tiled=True)  19 us
    all_to_all x1, blocking collectives, shards(): received = lax.all_to_all(merged, 'y', 0, 0, tiled=True)  17.8 us
    all_to_all x1, blocking collectives, shards(): received = lax.all_to_all(grads, 'gy', 0, 0, tiled=True)  13.1 us
    all_to_all x1, blocking collectives, shards(): my_means = lax.all_to_all(means, 'y', 0, 0, tiled=True)  12.5 us
    all_to_all x1, starting transfers between devices, shards(): received = lax.all_to_all(summed, 'far', 0, 0, tiled=True)  10.7 us
    all_to_all x1, blocking collectives, shards(): grads = lax.all_to_all(grads, 'gy', 0, 0, tiled=True)  10.5 us
  transfers between devices with their start and end apart: 13, of which 3 were waited for; matrix products, arithmetic and copies ran while one was open for 0% of the time, Pallas kernels for 2%

profile of v2, /device:TPU:1, one launch (start us, length us, event | category | flops | bytes accessed | tf_op | source)
XLA Modules:
  0.0 186.9 jit_solution(12788299483496613249)
XLA Ops:
  0.6 3.7 %shard_map.214 = (bf16[8,112,256]{2,1,0:T(8,128)(2,1)}, bf16[256,256]{1,0:T(8,128)(2,1)}, bf16[256,256]{1,0:T(8,128)(2,1)}, bf16[256,256]{1,0:T(8,128)(2,1)}, bf...) custom-call(s32[1,512]{1,0:T(1,128)} %bitcast.13, ...), custom_call_target="tpu_custom_call" | custom-call | flops 536870912 | bytes 4194304 | tf_op jit(solution)/shard_map/pallas_call | solution.py:438
  4.4 19.0 %all_to_all.40.received = bf16[8,112,256]{2,1,0:T(8,128)(2,1)S(1)} all-to-all(bf16[8,112,256]{2,1,0:T(8,128)(2,1)} %get-tuple-element.68), channel_id=1, replica_groups=mesh['far'=4,'y'=4,'core'=2,'gy'=16] {'y','core'}, dimensions={0} | all-to-all | bytes 917504 | tf_op jit(solution)/shard_map/all_to_all | solution.py:453
  23.4 0.8 shard_map.215
  24.1 10.7 %all-to-all-start.1 = ((bf16[4,112,256]{2,1,0:T(8,128)(2,1)}), bf16[4,112,256]{2,1,0:T(8,128)(2,1)S(1)}, u32[]{:S(2)}, u32[]{:S(2)}) async-start(bf16[4,112,256]{2,1,0:T(8,128)(2,1)} %shard_map.215), calls=%async_computation.1 | async-start | bytes 458752 | tf_op jit(solution)/shard_map/all_to_all | solution.py:462
  34.8 0.0 copy-done.19
  34.8 3.3 %collective-permute-start = (bf16[256,256]{1,0:T(8,128)(2,1)S(1)}, bf16[256,256]{1,0:T(8,128)(2,1)S(1)}, u32[]{:S(2)}, u32[]{:S(2)}) collective-permute-start(bf16[256,256]{1,0:T(8,128)(2,1)S(1)} %copy-done.19), channel_id=1, source_target_pairs={{16,32},{48,64},{80,96},{112,128},{144,160},{176,192},{208,224},{2... | collective-permute-start | bytes 393224 | tf_op jit(solution)/shard_map/ppermute | solution.py:432
  38.1 0.0 copy-done.18
  38.1 0.7 collective-permute-start.1
  38.8 0.0 copy-done.17
  38.8 4.6 %collective-permute-start.2 = (bf16[256,256]{1,0:T(8,128)(2,1)S(1)}, bf16[256,256]{1,0:T(8,128)(2,1)S(1)}, u32[]{:S(2)}, u32[]{:S(2)}) collective-permute-start(bf16[256,256]{1,0:T(8,128)(2,1)S(1)} %copy-done.17), channel_id=1, source_target_pairs={{0,1},{2,3},{4,5},{6,7},{8,9},{10,11},{12,13},{14,15},{1,0},{3,2},... | collective-permute-start | bytes 393224 | tf_op jit(solution)/shard_map/ppermute | solution.py:432
  43.4 0.0 copy-done.16
  43.4 1.9 %collective-permute-start.3 = (bf16[256,256]{1,0:T(8,128)(2,1)S(1)}, bf16[256,256]{1,0:T(8,128)(2,1)S(1)}, u32[]{:S(2)}, u32[]{:S(2)}) collective-permute-start(bf16[256,256]{1,0:T(8,128)(2,1)S(1)} %copy-done.16), channel_id=1, source_target_pairs={{0,16},{32,48},{64,80},{96,112},{128,144},{160,176},{192,208},{224... | collective-permute-start | bytes 393224 | tf_op jit(solution)/shard_map/ppermute | solution.py:432
  45.4 0.0 collective-permute-done.arrived0
  45.4 0.0 collective-permute-done.1.arrived1
  45.4 5.8 %collective-permute-done.2.arrived2 = bf16[256,256]{1,0:T(8,128)(2,1)S(1)} collective-permute-done((bf16[256,256]{1,0:T(8,128)(2,1)S(1)}, bf16[256,256]{1,0:T(8,128)(2,1)S(1)}, u32[]{:S(2)}, u32[]{:S(2)}) %collective-permute-start.2) | collective-permute-done | bytes 131104 | tf_op jit(solution)/shard_map/ppermute | solution.py:432
  51.2 0.0 collective-permute-done.3.arrived3
  51.2 0.0 all-to-all-done.1.received
  51.2 0.1 shard_map.216
  51.3 12.5 %all_to_all.41.mine = bf16[4,96,256]{2,1,0:T(8,128)(2,1)S(1)} all-to-all(bf16[4,96,256]{2,1,0:T(8,128)(2,1)S(1)} %get-tuple-element.74), channel_id=1, replica_groups=mesh['far'=4,'y'=4,'core'=2,'gy'=16] {'y'}, dimensions={0} | all-to-all | bytes 393216 | tf_op jit(solution)/shard_map/all_to_all | solution.py:471
  63.8 6.0 %collective-permute-start.4 = (bf16[4,96,256]{2,1,0:T(8,128)(2,1)S(1)}, bf16[4,96,256]{2,1,0:T(8,128)(2,1)S(1)}, u32[]{:S(2)}, u32[]{:S(2)}) collective-permute-start(bf16[4,96,256]{2,1,0:T(8,128)(2,1)S(1)} %all_to_all.41.mine), channel_id=1, source_target_pairs={{0,16},{16,0},{1,17},{17,1},{2,18},{18,2},{3,19},{19,3},{4,20},{20... | collective-permute-start | bytes 589832 | tf_op jit(solution)/shard_map/ppermute | solution.py:472
  69.9 0.0 copy-start.13
  69.9 0.0 copy-done.1
  69.9 0.7 copy-done.13
  70.6 0.0 copy-start.14
  70.6 0.0 copy-start.15
  70.6 0.7 shard_map.217.aggregate
  71.3 0.0 collective-permute-done.4.other
  71.3 0.2 copy-done
  71.5 0.1 copy-done.3
  71.6 0.1 copy-done.4
  71.7 0.0 copy-done.10
  71.7 0.0 copy-done.14
  71.8 0.0 copy-done.15
  71.8 4.7 %shard_map.218 = (bf16[512,256]{1,0:T(8,128)(2,1)}, bf16[512,256]{1,0:T(8,128)(2,1)S(1)}, bf16[512,256]{1,0:T(8,128)(2,1)S(1)}, bf16[512,256]{1,0:T(8,128)(2,1)S...) custom-call(s32[2,4]{1,0:T(2,128)S(1)} %bitcast.20, ...), custom_call_target="tpu_custom_call" | custom-call | flops 671088640 | bytes 4194304 | tf_op jit(solution)/shard_map/pallas_call | solution.py:483
  76.4 2.1 %collective-permute-start.5 = (bf16[256,256]{1,0:T(8,128)(2,1)S(1)}, bf16[256,256]{1,0:T(8,128)(2,1)S(1)}, u32[]{:S(2)}, u32[]{:S(2)}) collective-permute-start(bf16[256,256]{1,0:T(8,128)(2,1)S(1)} %get-tuple-element.97), channel_id=1, source_target_pairs={{16,32},{48,64},{80,96},{112,128},{144,160},{176,192},{208,224},{2... | collective-permute-start | bytes 393224 | tf_op jit(solution)/shard_map/ppermute | solution.py:432
  78.5 0.7 collective-permute-start.6
  79.2 6.2 %collective-permute-start.7 = (bf16[256,256]{1,0:T(8,128)(2,1)S(1)}, bf16[256,256]{1,0:T(8,128)(2,1)S(1)}, u32[]{:S(2)}, u32[]{:S(2)}) collective-permute-start(bf16[256,256]{1,0:T(8,128)(2,1)S(1)} %get-tuple-element.99), channel_id=1, source_target_pairs={{0,1},{2,3},{4,5},{6,7},{8,9},{10,11},{12,13},{14,15},{1,0},{3,2},... | collective-permute-start | bytes 393224 | tf_op jit(solution)/shard_map/ppermute | solution.py:432
  85.4 1.9 %collective-permute-start.8 = (bf16[256,256]{1,0:T(8,128)(2,1)S(1)}, bf16[256,256]{1,0:T(8,128)(2,1)S(1)}, u32[]{:S(2)}, u32[]{:S(2)}) collective-permute-start(bf16[256,256]{1,0:T(8,128)(2,1)S(1)} %get-tuple-element.100), channel_id=1, source_target_pairs={{0,16},{32,48},{64,80},{96,112},{128,144},{160,176},{192,208},{224... | collective-permute-start | bytes 393224 | tf_op jit(solution)/shard_map/ppermute | solution.py:432
  87.4 0.0 copy-start.11
  87.4 0.0 copy-done.2
  87.4 0.7 copy-done.11
  88.0 0.0 copy-start.9
  88.1 2.1 %shard_map.219 = (bf16[4,224,256]{2,1,0:T(8,128)(2,1)S(1)}, bf16[4,224,256]{2,1,0:T(8,128)(2,1)S(1)}, f32[512,256]{1,0:T(8,128)S(1)}, f32[512,256]{1,0:T(8,128)S(1)}) custom-call(s32[4,3]{1,0:T(4,128)S(1)} %copy-done.11, s32[1,512]{1,0:T(1,128)S(1)} %bitcast.15, bf16[512,256]{1,0:T(8,128)(2,1)S(1)} %copy-done, bf16[512,256]{1,0:T(8,128)(2,1)S(1)} %copy-done.4, ...), custom_call_target="tpu_custom_call" | custom-call | flops 536870912 | bytes 5242880 | tf_op jit(solution)/shard_map/pallas_call | solution.py:493
  90.1 0.0 collective-permute-done.5.back0
  90.1 0.0 collective-permute-done.6.back1
  90.2 0.0 collective-permute-done.7.back2
  90.2 0.0 collective-permute-done.8.back3
  90.2 2.4 %collective-permute-start.9 = (bf16[4,224,256]{2,1,0:T(8,128)(2,1)S(1)}, bf16[4,224,256]{2,1,0:T(8,128)(2,1)S(1)}, u32[]{:S(2)}, u32[]{:S(2)}) collective-permute-start(bf16[4,224,256]{2,1,0:T(8,128)(2,1)S(1)} %get-tuple-element.110), channel_id=1, source_target_pairs={{0,16},{16,0},{1,17},{17,1},{2,18},{18,2},{3,19},{19,3},{4,20},{20... | collective-permute-start | bytes 1376264 | tf_op jit(solution)/shard_map/ppermute | solution.py:504
  92.6 0.0 copy-start.12
  92.6 0.6 copy-done.12
  93.3 1.6 shard_map.220
  94.9 1.9 %collective-permute-start.10 = (bf16[4,80,256]{2,1,0:T(8,128)(2,1)S(1)}, bf16[4,80,256]{2,1,0:T(8,128)(2,1)S(1)}, u32[]{:S(2)}, u32[]{:S(2)}) collective-permute-start(bf16[4,80,256]{2,1,0:T(8,128)(2,1)S(1)} %get-tuple-element.111), channel_id=1, source_target_pairs={{0,16},{16,0},{1,17},{17,1},{2,18},{18,2},{3,19},{19,3},{4,20},{20... | collective-permute-start | bytes 491528 | tf_op jit(solution)/shard_map/ppermute | solution.py:519
  96.8 1.4 collective-permute-done.10.got_edge
  98.2 0.0 collective-permute-done.9.got_node
  98.2 0.1 shard_map.221
  98.3 17.8 %all_to_all.42.received = bf16[4,304,256]{2,1,0:T(8,128)(2,1)S(1)} all-to-all(bf16[4,304,256]{2,1,0:T(8,128)(2,1)S(1)} %shard_map.221), channel_id=1, replica_groups=mesh['far'=4,'y'=4,'core'=2,'gy'=16] {'y'}, dimensions={0} | all-to-all | bytes 1245184 | tf_op jit(solution)/shard_map/all_to_all | solution.py:523
  116.1 0.1 shard_map.222
  116.2 13.1 %all_to_all.43.received = bf16[16,16,256]{2,1,0:T(8,128)(2,1)S(1)} all-to-all(bf16[16,16,256]{2,1,0:T(8,128)(2,1)S(1)} %get-tuple-element.113), channel_id=1, replica_groups=mesh['far'=4,'y'=4,'core'=2,'gy'=16] {'gy'}, dimensions={0} | all-to-all | bytes 262144 | tf_op jit(solution)/shard_map/all_to_all | solution.py:530
  129.4 25.3 %all_to_all.44.received = bf16[4,112,256]{2,1,0:T(8,128)(2,1)S(1)} all-to-all(bf16[4,112,256]{2,1,0:T(8,128)(2,1)S(1)} %shard_map.223), channel_id=1, replica_groups=mesh['far'=4,'y'=4,'core'=2,'gy'=16] {'far'}, dimensions={0} | all-to-all | bytes 458752 | tf_op jit(solution)/shard_map/all_to_all | solution.py:534
  154.7 10.5 %all_to_all.45.grads = bf16[16,16,256]{2,1,0:T(8,128)(2,1)S(1)} all-to-all(bf16[16,16,256]{2,1,0:T(8,128)(2,1)S(1)} %get-tuple-element.116), channel_id=1, replica_groups=mesh['far'=4,'y'=4,'core'=2,'gy'=16] {'gy'}, dimensions={0} | all-to-all | bytes 262144 | tf_op jit(solution)/shard_map/all_to_all | solution.py:541
  165.3 9.9 %all_to_all.46.mine = bf16[4,304,256]{2,1,0:T(8,128)(2,1)S(1)} all-to-all(bf16[4,304,256]{2,1,0:T(8,128)(2,1)S(1)} %shard_map.225), channel_id=1, replica_groups=mesh['far'=4,'y'=4,'core'=2,'gy'=16] {'y'}, dimensions={0} | all-to-all | bytes 1245184 | tf_op jit(solution)/shard_map/all_to_all | solution.py:545
  175.1 8.5 %collective-permute-start.11 = (bf16[4,304,256]{2,1,0:T(8,128)(2,1)S(1)}, bf16[4,304,256]{2,1,0:T(8,128)(2,1)S(1)}, u32[]{:S(2)}, u32[]{:S(2)}) collective-permute-start(bf16[4,304,256]{2,1,0:T(8,128)(2,1)S(1)} %all_to_all.46.mine), channel_id=1, source_target_pairs={{0,16},{16,0},{1,17},{17,1},{2,18},{18,2},{3,19},{19,3},{4,20},{20... | collective-permute-start | bytes 1867784 | tf_op jit(solution)/shard_map/ppermute | solution.py:546
  183.6 1.7 collective-permute-done.11.other
  185.3 1.6 shard_map.226
  (22 shorter events, 0.1 us)
Async XLA Ops:
  23.4 11.4 %copy-start.19 = (bf16[256,256]{1,0:T(8,128)(2,1)S(1)}, bf16[256,256]{1,0:T(8,128)(2,1)}, u32[]{:S(2)}) copy-start(bf16[256,256]{1,0:T(8,128)(2,1)} %get-tuple-element.69) | copy-start | bytes 393220
  23.4 14.7 %copy-start.18 = (bf16[256,256]{1,0:T(8,128)(2,1)S(1)}, bf16[256,256]{1,0:T(8,128)(2,1)}, u32[]{:S(2)}) copy-start(bf16[256,256]{1,0:T(8,128)(2,1)} %get-tuple-element.70) | copy-start | bytes 393220
  23.4 15.4 %copy-start.17 = (bf16[256,256]{1,0:T(8,128)(2,1)S(1)}, bf16[256,256]{1,0:T(8,128)(2,1)}, u32[]{:S(2)}) copy-start(bf16[256,256]{1,0:T(8,128)(2,1)} %get-tuple-element.71) | copy-start | bytes 393220
  23.4 20.1 %copy-start.16 = (bf16[256,256]{1,0:T(8,128)(2,1)S(1)}, bf16[256,256]{1,0:T(8,128)(2,1)}, u32[]{:S(2)}) copy-start(bf16[256,256]{1,0:T(8,128)(2,1)} %get-tuple-element.72) | copy-start | bytes 393220
  24.1 45.7 %copy-start.1 = (f32[512,256]{1,0:T(8,128)S(1)}, f32[512,256]{1,0:T(8,128)}, u32[]{:S(2)}) copy-start(f32[512,256]{1,0:T(8,128)} %get-tuple-element.79.local) | copy-start | bytes 1572868
  24.1 27.1 %all-to-all-start.1 = ((bf16[4,112,256]{2,1,0:T(8,128)(2,1)}), bf16[4,112,256]{2,1,0:T(8,128)(2,1)S(1)}, u32[]{:S(2)}, u32[]{:S(2)}) async-start(bf16[4,112,256]{2,1,0:T(8,128)(2,1)} %shard_map.215), calls=%async_computation.1 | async-start | bytes 458752 | tf_op jit(solution)/shard_map/all_to_all | solution.py:462
  34.8 10.6 %collective-permute-start = (bf16[256,256]{1,0:T(8,128)(2,1)S(1)}, bf16[256,256]{1,0:T(8,128)(2,1)S(1)}, u32[]{:S(2)}, u32[]{:S(2)}) collective-permute-start(bf16[256,256]{1,0:T(8,128)(2,1)S(1)} %copy-done.19), channel_id=1, source_target_pairs={{16,32},{48,64},{80,96},{112,128},{144,160},{176,192},{208,224},{2... | collective-permute-start | bytes 393224 | tf_op jit(solution)/shard_map/ppermute | solution.py:432
  38.1 7.3 %collective-permute-start.1 = (bf16[256,256]{1,0:T(8,128)(2,1)S(1)}, bf16[256,256]{1,0:T(8,128)(2,1)S(1)}, u32[]{:S(2)}, u32[]{:S(2)}) collective-permute-start(bf16[256,256]{1,0:T(8,128)(2,1)S(1)} %copy-done.18), channel_id=1, source_target_pairs={{1,2},{3,4},{5,6},{7,8},{9,10},{11,12},{13,14},{2,1},{4,3},{6,5},{... | collective-permute-start | bytes 393224 | tf_op jit(solution)/shard_map/ppermute | solution.py:432
  38.8 12.4 %collective-permute-start.2 = (bf16[256,256]{1,0:T(8,128)(2,1)S(1)}, bf16[256,256]{1,0:T(8,128)(2,1)S(1)}, u32[]{:S(2)}, u32[]{:S(2)}) collective-permute-start(bf16[256,256]{1,0:T(8,128)(2,1)S(1)} %copy-done.17), channel_id=1, source_target_pairs={{0,1},{2,3},{4,5},{6,7},{8,9},{10,11},{12,13},{14,15},{1,0},{3,2},... | collective-permute-start | bytes 393224 | tf_op jit(solution)/shard_map/ppermute | solution.py:432
  43.4 7.8 %collective-permute-start.3 = (bf16[256,256]{1,0:T(8,128)(2,1)S(1)}, bf16[256,256]{1,0:T(8,128)(2,1)S(1)}, u32[]{:S(2)}, u32[]{:S(2)}) collective-permute-start(bf16[256,256]{1,0:T(8,128)(2,1)S(1)} %copy-done.16), channel_id=1, source_target_pairs={{0,16},{32,48},{64,80},{96,112},{128,144},{160,176},{192,208},{224... | collective-permute-start | bytes 393224 | tf_op jit(solution)/shard_map/ppermute | solution.py:432
  63.8 7.5 %collective-permute-start.4 = (bf16[4,96,256]{2,1,0:T(8,128)(2,1)S(1)}, bf16[4,96,256]{2,1,0:T(8,128)(2,1)S(1)}, u32[]{:S(2)}, u32[]{:S(2)}) collective-permute-start(bf16[4,96,256]{2,1,0:T(8,128)(2,1)S(1)} %all_to_all.41.mine), channel_id=1, source_target_pairs={{0,16},{16,0},{1,17},{17,1},{2,18},{18,2},{3,19},{19,3},{4,20},{20... | collective-permute-start | bytes 589832 | tf_op jit(solution)/shard_map/ppermute | solution.py:472
  69.9 0.7 copy-start.13
  70.6 0.9 copy-start
  70.6 1.1 copy-start.3
  70.6 1.1 copy-start.4
  70.6 1.1 copy-start.10
  70.6 1.2 copy-start.14
  70.6 1.2 copy-start.15
  71.8 15.6 %copy-start.2 = (bf16[4,3,128,128]{3,2,1,0:T(8,128)(2,1)S(1)}, bf16[4,3,128,128]{3,2,1,0:T(8,128)(2,1)}, u32[]{:S(2)}) copy-start(bf16[4,3,128,128]{3,2,1,0:T(8,128)(2,1)} %blocks.1) | copy-start | bytes 1179652
  76.4 13.7 %collective-permute-start.5 = (bf16[256,256]{1,0:T(8,128)(2,1)S(1)}, bf16[256,256]{1,0:T(8,128)(2,1)S(1)}, u32[]{:S(2)}, u32[]{:S(2)}) collective-permute-start(bf16[256,256]{1,0:T(8,128)(2,1)S(1)} %get-tuple-element.97), channel_id=1, source_target_pairs={{16,32},{48,64},{80,96},{112,128},{144,160},{176,192},{208,224},{2... | collective-permute-start | bytes 393224 | tf_op jit(solution)/shard_map/ppermute | solution.py:432
  78.5 11.7 %collective-permute-start.6 = (bf16[256,256]{1,0:T(8,128)(2,1)S(1)}, bf16[256,256]{1,0:T(8,128)(2,1)S(1)}, u32[]{:S(2)}, u32[]{:S(2)}) collective-permute-start(bf16[256,256]{1,0:T(8,128)(2,1)S(1)} %get-tuple-element.98), channel_id=1, source_target_pairs={{1,2},{3,4},{5,6},{7,8},{9,10},{11,12},{13,14},{2,1},{4,3},{6,5},{... | collective-permute-start | bytes 393224 | tf_op jit(solution)/shard_map/ppermute | solution.py:432
  79.2 11.0 %collective-permute-start.7 = (bf16[256,256]{1,0:T(8,128)(2,1)S(1)}, bf16[256,256]{1,0:T(8,128)(2,1)S(1)}, u32[]{:S(2)}, u32[]{:S(2)}) collective-permute-start(bf16[256,256]{1,0:T(8,128)(2,1)S(1)} %get-tuple-element.99), channel_id=1, source_target_pairs={{0,1},{2,3},{4,5},{6,7},{8,9},{10,11},{12,13},{14,15},{1,0},{3,2},... | collective-permute-start | bytes 393224 | tf_op jit(solution)/shard_map/ppermute | solution.py:432
  85.4 4.7 %collective-permute-start.8 = (bf16[256,256]{1,0:T(8,128)(2,1)S(1)}, bf16[256,256]{1,0:T(8,128)(2,1)S(1)}, u32[]{:S(2)}, u32[]{:S(2)}) collective-permute-start(bf16[256,256]{1,0:T(8,128)(2,1)S(1)} %get-tuple-element.100), channel_id=1, source_target_pairs={{0,16},{32,48},{64,80},{96,112},{128,144},{160,176},{192,208},{224... | collective-permute-start | bytes 393224 | tf_op jit(solution)/shard_map/ppermute | solution.py:432
  87.4 0.7 copy-start.11
  88.0 4.6 %copy-start.5 = (bf16[1,1,4,2,128,128]{5,4,3,2,1,0:T(8,128)(2,1)S(1)}, bf16[1,1,4,2,128,128]{5,4,3,2,1,0:T(8,128)(2,1)}, u32[]{:S(2)}) copy-start(bf16[1,1,4,2,128,128]{5,4,3,2,1,0:T(8,128)(2,1)} %param.21) | copy-start | bytes 786436
  88.0 4.6 %copy-start.6 = (bf16[512,256]{1,0:T(8,128)(2,1)S(1)}, bf16[512,256]{1,0:T(8,128)(2,1)}, u32[]{:S(2)}) copy-start(bf16[512,256]{1,0:T(8,128)(2,1)} %get-tuple-element.87.lifted) | copy-start | bytes 786436
  88.0 4.6 %copy-start.7 = (bf16[512,256]{1,0:T(8,128)(2,1)S(1)}, bf16[512,256]{1,0:T(8,128)(2,1)}, u32[]{:S(2)}) copy-start(bf16[512,256]{1,0:T(8,128)(2,1)} %get-tuple-element.88.active) | copy-start | bytes 786436
  88.0 4.6 %copy-start.8 = (bf16[256,256]{1,0:T(8,128)(2,1)S(1)}, bf16[256,256]{1,0:T(8,128)(2,1)}, u32[]{:S(2)}) copy-start(bf16[256,256]{1,0:T(8,128)(2,1)} %edge_lift.1) | copy-start | bytes 393220
  88.0 4.6 %copy-start.9 = (bf16[256,256]{1,0:T(8,128)(2,1)S(1)}, bf16[256,256]{1,0:T(8,128)(2,1)}, u32[]{:S(2)}) copy-start(bf16[256,256]{1,0:T(8,128)(2,1)} %edge_emit.1) | copy-start | bytes 393220
  90.2 8.0 %collective-permute-start.9 = (bf16[4,224,256]{2,1,0:T(8,128)(2,1)S(1)}, bf16[4,224,256]{2,1,0:T(8,128)(2,1)S(1)}, u32[]{:S(2)}, u32[]{:S(2)}) collective-permute-start(bf16[4,224,256]{2,1,0:T(8,128)(2,1)S(1)} %get-tuple-element.110), channel_id=1, source_target_pairs={{0,16},{16,0},{1,17},{17,1},{2,18},{18,2},{3,19},{19,3},{4,20},{20... | collective-permute-start | bytes 1376264 | tf_op jit(solution)/shard_map/ppermute | solution.py:504
  92.6 0.7 copy-start.12
  94.9 3.3 %collective-permute-start.10 = (bf16[4,80,256]{2,1,0:T(8,128)(2,1)S(1)}, bf16[4,80,256]{2,1,0:T(8,128)(2,1)S(1)}, u32[]{:S(2)}, u32[]{:S(2)}) collective-permute-start(bf16[4,80,256]{2,1,0:T(8,128)(2,1)S(1)} %get-tuple-element.111), channel_id=1, source_target_pairs={{0,16},{16,0},{1,17},{17,1},{2,18},{18,2},{3,19},{19,3},{4,20},{20... | collective-permute-start | bytes 491528 | tf_op jit(solution)/shard_map/ppermute | solution.py:519
  175.1 10.2 %collective-permute-start.11 = (bf16[4,304,256]{2,1,0:T(8,128)(2,1)S(1)}, bf16[4,304,256]{2,1,0:T(8,128)(2,1)S(1)}, u32[]{:S(2)}, u32[]{:S(2)}) collective-permute-start(bf16[4,304,256]{2,1,0:T(8,128)(2,1)S(1)} %all_to_all.46.mine), channel_id=1, source_target_pairs={{0,16},{16,0},{1,17},{17,1},{2,18},{18,2},{3,19},{19,3},{4,20},{20... | collective-permute-start | bytes 1867784 | tf_op jit(solution)/shard_map/ppermute | solution.py:546

commit v3 on v2

--- a/solution.py
+++ b/solution.py
@@ -86,7 +86,7 @@
 def front_kernel(share, *refs):
     far, refs = refs[:11], refs[11:]
     (pool, part0, part1, part2, part3, lifted, active, local, params), refs = refs[:9], refs[9:]
-    near, (message, sems) = refs[:11], refs[11:]
+    near, (message, hot, sems) = refs[:11], refs[11:]
     copies = [
         pltpu.make_async_copy(*pair, sems.at[index])
         for index, pair in enumerate(zip(far, near))
@@ -100,12 +100,14 @@
     for copy in copies[:2]:
         copy.wait()
     clus_row = clus[...]
-    ones = jnp.ones((16, rows), BF16)
     line = lax.broadcasted_iota(jnp.int32, (16, TILE), 0)
     for peer in range(pool.shape[0]):
-        hot = hot_rows(clus_row, peer * share, TILE)
-        pool[peer, 0:share] = mm(hot, state[...])[:share].astype(BF16)
-        count = mm_nt(ones, hot)
+        hot[rows_of(peer)] = hot_rows(clus_row, peer * share, TILE)
+    sums = mm(hot[...], state[...])
+    counts = mm_nt(jnp.ones((16, rows), BF16), hot[...])
+    for peer in range(pool.shape[0]):
+        pool[peer, 0:share] = sums[peer * TILE:peer * TILE + share].astype(BF16)
+        count = counts[:, rows_of(peer)]
         eights = jnp.floor(count * 0.125)
         high = jnp.floor(eights * 0.125)
         digits = jnp.where(
@@ -119,14 +121,12 @@
     for index, vector in enumerate((node_bias, norm_gain)):
         params[index:index + 1] = vector[...].astype(F32).reshape(1, -1)
     bias = edge_bias[...].astype(F32).reshape(1, -1)
-    for tile in range(tiles):
-        rows = rows_of(tile)
-        value = (mm(state[rows], edge_lift[...]) + bias).astype(BF16)
-        lifted[rows] = value
-        wide = value.astype(F32)
-        hidden = (wide * jax.nn.sigmoid(wide)).astype(BF16)
-        active[rows] = hidden
-        message[rows] = mm(hidden, edge_emit[...]).astype(BF16)
+    value = (mm(state[...], edge_lift[...]) + bias).astype(BF16)
+    lifted[...] = value
+    wide = value.astype(F32)
+    hidden = (wide * jax.nn.sigmoid(wide)).astype(BF16)
+    active[...] = hidden
+    message[...] = mm(hidden, edge_emit[...]).astype(BF16)
     for slot, part in zip(slots("out"), (part0, part1, part2, part3)):
         for cut in range(cuts.shape[1]):
             part[rows_of(cut)] = mm(
@@ -148,13 +148,15 @@
 
 
 def sum_kernel(received, out):
-    total = jnp.sum(received[...].astype(F32), axis=0).astype(BF16)
-    for peer in range(out.shape[0]):
-        out[peer] = total
-
-
-def mean_kernel(share, received, means, counts):
-    total = jnp.sum(received[...].astype(F32), axis=0)
+    out[...] = jnp.sum(received[...].astype(F32), axis=0).astype(BF16)
+
+
+def add_kernel(mine, other, out):
+    out[...] = (mine[...].astype(F32) + other[...].astype(F32)).astype(BF16)
+
+
+def mean_kernel(share, mine, other, means, counts):
+    total = mine[...].astype(F32) + other[...].astype(F32)
     low, middle, high = (total[share + row:share + row + 1, 0:TILE] for row in (0, 4, 8))
     count = jnp.broadcast_to(high * 64.0 + middle * 8.0 + low, (TILE, TILE)).T[:share]
     count = jnp.concatenate([count] * (means.shape[2] // TILE), axis=1)
@@ -166,7 +168,7 @@
 
 def node_kernel(target, clus, state, upstream, aggregate, mine, other, node_lift, node_emit, params,
                 updated, coarse, active, emit_grad, lifted_grad, aggregate_grad,
-                coarse_grad, back0, back1, back2, back3, vectors, means):
+                coarse_grad, back0, back1, back2, vectors, means, slopes, hot):
     features = state.shape[1]
     clusters, share = means.shape[0], mine.shape[1]
     core = lax.axis_index("core")
@@ -181,44 +183,42 @@
     gain = params[1:2]
     gain_grad = jnp.zeros((1, features), F32)
     bias_grad = jnp.zeros((1, features), F32)
+    here = state[...]
     for tile in range(state.shape[0] // TILE):
-        rows = rows_of(tile)
-        here = state[rows]
-        agg = aggregate[rows]
-        hot = hot_columns(clus[0:1, rows], clusters)
-        pooled = mm(hot, means[...]).astype(BF16)
-        coarse[rows] = pooled
-        lifted = (
-            mm(here, lift_state) + mm(agg, lift_agg) + mm(pooled, lift_coarse) + bias
-        ).astype(BF16).astype(F32)
-        gate = jax.nn.sigmoid(lifted)
-        hidden = (lifted * gate).astype(BF16)
-        active[rows] = hidden
-        emitted = mm(hidden, node_emit[...])
-        center = emitted - jnp.mean(emitted, axis=-1, keepdims=True)
-        inverse = lax.rsqrt(jnp.mean(center * center, axis=-1, keepdims=True) + NORM_EPS)
-        normed = center * inverse
-        updated[rows] = (here.astype(F32) + gain * normed).astype(BF16)
-        above = upstream[rows].astype(F32)
-        gain_grad += jnp.sum(above * normed, axis=0, keepdims=True)
-        scaled = above * gain
-        grad = (
-            inverse
-            * (
-                scaled
-                - jnp.mean(scaled, axis=-1, keepdims=True)
-                - normed * jnp.mean(scaled * normed, axis=-1, keepdims=True)
-            )
-        ).astype(BF16)
-        emit_grad[rows] = grad
-        active_grad = mm_nt(grad, node_emit[...]).astype(BF16).astype(F32)
-        slope = gate * (1.0 + lifted * (1.0 - gate))
-        down = (active_grad * slope).astype(BF16)
-        lifted_grad[rows] = down
-        bias_grad += jnp.sum(down.astype(F32), axis=0, keepdims=True)
-        aggregate_grad[rows] = mm_nt(down, lift_agg).astype(BF16)
-        coarse_grad[rows] = mm_nt(down, lift_coarse).astype(BF16)
-    for slot, back in zip(slots("in"), (back0, back1, back2, back3)):
+        hot[rows_of(tile)] = hot_columns(clus[0:1, rows_of(tile)], clusters)
+    coarse[...] = mm(hot[...], means[...]).astype(BF16)
+    lifted = (
+        mm(here, lift_state) + mm(aggregate[...], lift_agg) + mm(coarse[...], lift_coarse)
+        + bias
+    ).astype(BF16).astype(F32)
+    gate = jax.nn.sigmoid(lifted)
+    hidden = (lifted * gate).astype(BF16)
+    active[...] = hidden
+    slopes[...] = gate * (1.0 + lifted * (1.0 - gate))
+    emitted = mm(hidden, node_emit[...])
+    center = emitted - jnp.mean(emitted, axis=-1, keepdims=True)
+    inverse = lax.rsqrt(jnp.mean(center * center, axis=-1, keepdims=True) + NORM_EPS)
+    normed = center * inverse
+    updated[...] = (here.astype(F32) + gain * normed).astype(BF16)
+    above = upstream[...].astype(F32)
+    gain_grad += jnp.sum(above * normed, axis=0, keepdims=True)
+    scaled = above * gain
+    grad = (
+        inverse
+        * (
+            scaled
+            - jnp.mean(scaled, axis=-1, keepdims=True)
+            - normed * jnp.mean(scaled * normed, axis=-1, keepdims=True)
+        )
+    ).astype(BF16)
+    emit_grad[...] = grad
+    active_grad = mm_nt(grad, node_emit[...]).astype(BF16).astype(F32)
+    down = (active_grad * slopes[...]).astype(BF16)
+    lifted_grad[...] = down
+    bias_grad += jnp.sum(down.astype(F32), axis=0, keepdims=True)
+    aggregate_grad[...] = mm_nt(down, lift_agg).astype(BF16)
+    coarse_grad[...] = mm_nt(down, lift_coarse).astype(BF16)
+    for slot, back in zip(slots("in"), (back0, back1, back2)):
         for cut in range(back.shape[0] // TILE):
             back[rows_of(cut)] = aggregate_grad[tile_rows(target[cut, slot])]
     vectors[...] = jnp.zeros(vectors.shape, F32)
@@ -239,24 +239,29 @@
     core = lax.axis_index("core")
     for index in range(keep.shape[0]):
         keep[index] = stack[2 * index + core]
-        send[index] = stack[2 * index + 1 - core]
-
-
-def weight_kernel(sizes, adjacency, clus, state, upstream, aggregate, coarse, active, emit_grad,
-                  lifted_grad, aggregate_grad, coarse_grad, blocks, node_lift,
-                  keep, send, local, partial, stack):
+        send[index, 0:stack.shape[1]] = stack[2 * index + 1 - core]
+
+
+def weight_kernel(sizes, adjacency, target, clus, state, upstream, aggregate, coarse, active,
+                  emit_grad, lifted_grad, aggregate_grad, coarse_grad, blocks, node_lift,
+                  keep, send, local, partial, stack, hot):
     peers, share, node_rows, _ = sizes
     features = state.shape[1]
     clus_row = clus[...]
     for peer in range(peers):
-        stack[peer, 0:share] = mm(
-            hot_rows(clus_row, peer * share, share), coarse_grad[...]
-        ).astype(BF16)
+        hot[peer * share:(peer + 1) * share] = hot_rows(clus_row, peer * share, share)
+    put_chunks(stack, 0, share, 0, mm(hot[...], coarse_grad[...]))
     down = lifted_grad[...]
     for index, block in enumerate((state, aggregate, coarse)):
         put_chunks(stack, share, node_rows, index * features, mm_tn(block[...], down))
     put_chunks(stack, share, node_rows, 3 * features, mm_tn(active[...], emit_grad[...]))
     part_ways(stack, keep, send)
+    each, last = send.shape[1] - keep.shape[1], slots("in")[3]
+    for index in range(send.shape[0]):
+        cut, row = divmod(index * each, TILE)
+        start = pl.multiple_of(target[cut, last] * TILE + row, each)
+        send[index, keep.shape[1]:] = aggregate_grad[pl.ds(start, each)]
+    partial[...] = upstream[...].astype(F32) + mm_nt(down, node_lift[0:features])
     local[...] = jnp.zeros(local.shape, F32)
     for tile in range(state.shape[0] // TILE):
         rows = rows_of(tile)
@@ -264,32 +269,28 @@
             local[tile_rows(adjacency[tile, slot])] += mm_tn(
                 blocks[tile, slot], aggregate_grad[rows]
             )
-        partial[rows] = upstream[rows].astype(F32) + mm_nt(
-            lifted_grad[rows], node_lift[0:features]
-        )
-
-
-def edge_kernel(sizes, source, state, lifted, active, local, back0, back1, back2, back3, cuts,
+
+
+def edge_kernel(sizes, source, state, lifted, active, local, back0, back1, back2, got_node, cuts,
                 edge_lift, edge_emit, partial, vectors,
                 keep, send, partial_out, total, message_grad, lifted_grad, edge_part):
-    peers, _, _, edge_rows = sizes
+    peers, share, node_rows, edge_rows = sizes
     features = state.shape[1]
     total[...] = local[...]
+    first = share + node_rows
+    back3 = jnp.concatenate([got_node[index, first:] for index in range(got_node.shape[0])], axis=0)
     for slot, back in zip(slots("out"), (back0, back1, back2, back3)):
         for cut in range(cuts.shape[1]):
             total[tile_rows(source[cut, slot])] += mm_tn(cuts[slot, cut], back[rows_of(cut)])
-    bias_grad = jnp.zeros((1, features), F32)
-    for tile in range(state.shape[0] // TILE):
-        rows = rows_of(tile)
-        grad = total[rows].astype(BF16)
-        message_grad[rows] = grad
-        active_grad = mm_nt(grad, edge_emit[...]).astype(BF16).astype(F32)
-        wide = lifted[rows].astype(F32)
-        gate = jax.nn.sigmoid(wide)
-        down = (active_grad * (gate * (1.0 + wide * (1.0 - gate)))).astype(BF16)
-        lifted_grad[rows] = down
-        bias_grad += jnp.sum(down.astype(F32), axis=0, keepdims=True)
-        partial_out[rows] = partial[rows] + mm_nt(down, edge_lift[...])
+    grad = total[...].astype(BF16)
+    message_grad[...] = grad
+    active_grad = mm_nt(grad, edge_emit[...]).astype(BF16).astype(F32)
+    wide = lifted[...].astype(F32)
+    gate = jax.nn.sigmoid(wide)
+    down = (active_grad * (gate * (1.0 + wide * (1.0 - gate)))).astype(BF16)
+    lifted_grad[...] = down
+    bias_grad = jnp.sum(down.astype(F32), axis=0, keepdims=True)
+    partial_out[...] = partial[...] + mm_nt(down, edge_lift[...])
     put_chunks(edge_part, 0, edge_rows, 0, mm_tn(state[...], lifted_grad[...]))
     put_chunks(edge_part, 0, edge_rows, features, mm_tn(active[...], message_grad[...]))
     edge_part[:, edge_rows:] = jnp.zeros((peers, 16, features), BF16)
@@ -302,7 +303,9 @@
 
 def merge_kernel(keep_node, keep_edge, got_node, got_edge, out):
     rows = keep_node.shape[1]
-    out[:, 0:rows] = (keep_node[...].astype(F32) + got_node[...].astype(F32)).astype(BF16)
+    out[:, 0:rows] = (
+        keep_node[...].astype(F32) + got_node[:, 0:rows].astype(F32)
+    ).astype(BF16)
     out[:, rows:] = (keep_edge[...].astype(F32) + got_edge[...].astype(F32)).astype(BF16)
 
 
@@ -348,7 +351,7 @@
 
 
 def last_kernel(sizes, scale, clus, partial, mine, other, state_grad, edge_lift, edge_bias,
-                edge_emit, node_lift, node_bias, node_emit, norm_gain, means):
+                edge_emit, node_lift, node_bias, node_emit, norm_gain, means, hot):
     peers, share, node_rows, edge_rows = sizes
     features = partial.shape[1]
     core = lax.axis_index("core")
@@ -361,8 +364,8 @@
         means[peer * share:(peer + 1) * share] = gathered(peer, 0, share)
     for tile in range(partial.shape[0] // TILE):
         rows = rows_of(tile)
-        pooled = mm(hot_columns(clus[0:1, rows], peers * share), means[...])
-        state_grad[rows] = (partial[rows] + pooled).astype(BF16)
+        hot[rows] = hot_columns(clus[0:1, rows], peers * share)
+    state_grad[...] = (partial[...] + mm(hot[...], means[...])).astype(BF16)
 
     def take(first, size, outs):
         start = 0
@@ -423,11 +426,11 @@
     gx = ("far", *near)
     both_cores = [(0, 1), (1, 0)]
 
-    def swap(parts):
+    ways = ((gx, along, 1), ("gy", columns, 1), ("gy", columns, 0), (gx, along, 0))
+
+    def swap(parts, ways=ways):
         moved = []
-        for part, axis, count, first in zip(
-            parts, (gx, "gy", "gy", gx), (along, columns, columns, along), (1, 1, 0, 0)
-        ):
+        for part, (axis, count, first) in zip(parts, ways):
             pairs = [(i, i + 1) for i in range(first, count - 1, 2)]
             moved.append(lax.ppermute(part, axis, pairs + [(j, i) for i, j in pairs]))
         return moved
@@ -444,7 +447,11 @@
             (pltpu.SMEM if any(v is table for table in tables) else pltpu.VMEM)(v.shape, v.dtype)
             for v in operands
         ]
-        + [pltpu.VMEM((rows, features), BF16), pltpu.SemaphoreType.DMA((len(operands),))],
+        + [
+            pltpu.VMEM((rows, features), BF16),
+            pltpu.VMEM((peers * TILE, rows), BF16),
+            pltpu.SemaphoreType.DMA((len(operands),)),
+        ],
         FIRST_LIMIT,
         out_specs=vmem(9),
         flops=8 * layer,
@@ -453,21 +460,28 @@
     received = lax.all_to_all(pool, near, 0, 0, tiled=True)
     summed = call(
         sum_kernel,
-        like((far, share + 16, features), BF16),
+        like((share + 16, features), BF16),
         vmem(1),
         out_specs=pl.BlockSpec(memory_space=pltpu.VMEM),
         moved=1 << 20,
     )(received)
-    arrived = swap((part0, part1, part2, part3))
-    received = lax.all_to_all(summed, "far", 0, 0, tiled=True)
-    received, *arrived = lax.optimization_barrier((received, *arrived))
+    meetings = [[(i, i ^ 1) for i in range(far)], [(i, far - 1 - i) for i in range(far)]]
+    summed, part0, part1 = lax.optimization_barrier((summed, part0, part1))
+    other = lax.ppermute(summed, "far", meetings[0])
+    arrived = swap((part0, part1), ways[:2])
+    if far > 2:
+        summed = call(add_kernel, like(summed.shape, BF16), vmem(2), moved=1 << 18)(summed, other)
+        summed, part2, part3 = lax.optimization_barrier((summed, part2, part3))
+        other = lax.ppermute(summed, "far", meetings[1])
+    arrived += swap((part2, part3), ways[2:])
+    summed, other, *arrived = lax.optimization_barrier((summed, other, *arrived))
     means, counts = call(
         functools.partial(mean_kernel, share),
         [like((across, share, features), BF16), like((share, features), F32)],
-        vmem(1),
+        vmem(2),
         out_specs=vmem(2),
         moved=1 << 20,
-    )(received)
+    )(summed, other)
     my_means = lax.all_to_all(means, "y", 0, 0, tiled=True)
     other_means = lax.ppermute(my_means, "core", both_cores)
     local, my_means, *arrived = lax.optimization_barrier((local, my_means, *arrived))
@@ -480,11 +494,15 @@
     )(target, local, *arrived)
 
     (updated, coarse, node_active, emit_grad, lifted_grad, aggregate_grad, coarse_grad,
-     back0, back1, back2, back3, vectors) = call(
+     back0, back1, back2, vectors) = call(
         node_kernel,
-        [narrow] * 7 + [cut_part] * 4 + [like((8, features), F32)],
+        [narrow] * 7 + [cut_part] * 3 + [like((8, features), F32)],
         smem(1) + vmem(9),
-        [pltpu.VMEM((peers * share, features), BF16)],
+        [
+            pltpu.VMEM((peers * share, features), BF16),
+            pltpu.VMEM((rows, features), F32),
+            pltpu.VMEM((rows, peers * share), BF16),
+        ],
         flops=10 * layer,
         moved=4 << 20,
     )(target, clus, node_state, node_grad, aggregate, my_means, other_means, node_lift, node_emit,
@@ -492,15 +510,22 @@
 
     keep_node, send_node, message_local, partial = call(
         functools.partial(weight_kernel, sizes),
-        [like((across, share + node_rows, features), BF16)] * 2 + [wide, wide],
-        smem(1) + vmem(12),
-        [pltpu.VMEM((peers, share + node_rows, features), BF16)],
+        [
+            like((across, share + node_rows, features), BF16),
+            like((across, share + node_rows + cut_rows // across, features), BF16),
+            wide,
+            wide,
+        ],
+        smem(2) + vmem(12),
+        [
+            pltpu.VMEM((peers, share + node_rows, features), BF16),
+            pltpu.VMEM((peers * share, rows), BF16),
+        ],
         flops=8 * layer,
         moved=5 << 20,
-    )(adjacency, clus, node_state, node_grad, aggregate, coarse, node_active, emit_grad,
+    )(adjacency, target, clus, node_state, node_grad, aggregate, coarse, node_active, emit_grad,
       lifted_grad, aggregate_grad, coarse_grad, edge_blocks, node_lift)
-    returned = swap((back0, back1, back2, back3))
-    send_node, *returned = lax.optimization_barrier((send_node, *returned))
+    returned = swap((back0, back1, back2))
     got_node = lax.ppermute(send_node, "core", both_cores)
     keep_edge, send_edge, partial = call(
         functools.partial(edge_kernel, sizes),
@@ -514,7 +539,7 @@
         ],
         flops=8 * layer,
         moved=5 << 20,
-    )(source, node_state, lifted, active, message_local, *returned, cuts, edge_lift, edge_emit,
+    )(source, node_state, lifted, active, message_local, *returned, got_node, cuts, edge_lift, edge_emit,
       partial, vectors)
     got_edge = lax.ppermute(send_edge, "core", both_cores)
     merged = call(
@@ -551,7 +576,7 @@
         functools.partial(last_kernel, sizes, scale),
         [narrow, square, line, square, like((3 * features, features), F32), line, square, line],
         vmem(4),
-        [pltpu.VMEM((peers * share, features), BF16)],
+        [pltpu.VMEM((peers * share, features), BF16), pltpu.VMEM((rows, peers * share), BF16)],
         flops=3 * layer,
         moved=4 << 20,
     )(clus, partial, mine, other)

time: 188 us -> 184 us (0.979)
  waiting for transfers between devices: 8.87 us -> 15 us
  blocking collectives: 108 us -> 102 us
  Pallas kernels: 15.5 us -> 12.7 us
    ppermute x0 -> x2, starting transfers between devices: none -> 13.9 us  [the longest x1 9.22 us: shards(): other = lax.ppermute(summed, 'far', meetings[1])]
    all_to_all x1 -> x0, starting transfers between devices: 10.7 us -> none  [shards(): received = lax.all_to_all(summed, 'far', 0, 0, tiled=True)]
    ppermute x0 -> x2, waiting for transfers between devices: none -> 6.14 us  [the longest x1 3.88 us: shards(): other = lax.ppermute(summed, 'far', meetings[0])]
    all_to_all x1, blocking collectives: 12.5 us -> 7.65 us  [shards(): my_means = lax.all_to_all(means, 'y', 0, 0, tiled=True)]
    all_to_all x1, blocking collectives: 25.3 us -> 21.9 us  [shards(): received = lax.all_to_all(joined, 'far', 0, 0, tiled=True)]
    all_to_all x1, blocking collectives: 13.1 us -> 16.5 us  [shards(): received = lax.all_to_all(grads, 'gy', 0, 0, tiled=True)]
    ppermute x8 -> x7, starting transfers between devices: 21.4 us -> 18.6 us  [swap(): moved.append(lax.ppermute(part, axis, pairs + [(j, i) for i, j in pairs]))]
    pallas_call x2 -> x3, Pallas kernels: 5.4 us -> 2.75 us  [the longest x1 2.67 us: shards(): call(node_kernel, [narrow] * 7 + [cut_part] * 3 + [like((8, features), F3...]
  transfers between devices with their start and end apart: 13 -> 13, of which waited for: 3 -> 5; matrix products, arithmetic and copies ran while one was open for 0% -> 0% of each run, Pallas kernels for 2% -> 0%
where the time goes in v3:
time: 184 us; the launch traced here: 183 us
  blocking collectives  102 us (55%)
  starting transfers between devices  49.9 us (27%)
  waiting for transfers between devices  15 us (8%)
  Pallas kernels  12.7 us (7%)
  local copies, waits for them, and re-layouts  2.47 us (1%)
    all_to_all x1, blocking collectives, shards(): received = lax.all_to_all(joined, 'far', 0, 0, tiled=True)  21.9 us
    all_to_all x1, blocking collectives, shards(): received = lax.all_to_all(pool, near, 0, 0, tiled=True)  19.1 us
    ppermute x7, starting transfers between devices, swap(): moved.append(lax.ppermute(part, axis, pairs + [(j, i) for i, j in pairs]))  18.6 us
    all_to_all x1, blocking collectives, shards(): received = lax.all_to_all(grads, 'gy', 0, 0, tiled=True)  16.5 us
    all_to_all x1, blocking collectives, shards(): received = lax.all_to_all(merged, 'y', 0, 0, tiled=True)  16.4 us
    all_to_all x1, blocking collectives, shards(): grads = lax.all_to_all(grads, 'gy', 0, 0, tiled=True)  10.6 us
    ppermute x1, starting transfers between devices, shards(): other = lax.ppermute(mine, 'core', both_cores)  9.96 us
    all_to_all x1, blocking collectives, shards(): mine = lax.all_to_all(spread, 'y', 0, 0, tiled=True)  9.85 us
  transfers between devices with their start and end apart: 13, of which 5 were waited for; matrix products, arithmetic and copies ran while one was open for 0% of the time, Pallas kernels for 0%

profile of v3, /device:TPU:1, one launch (start us, length us, event | category | flops | bytes accessed | tf_op | source)
XLA Modules:
  0.0 183.0 jit_solution(5971527460821754428)
XLA Ops:
  0.6 3.7 %shard_map.214 = (bf16[8,112,256]{2,1,0:T(8,128)(2,1)}, bf16[256,256]{1,0:T(8,128)(2,1)}, bf16[256,256]{1,0:T(8,128)(2,1)}, bf16[256,256]{1,0:T(8,128)(2,1)}, bf...) custom-call(s32[1,512]{1,0:T(1,128)} %bitcast.13, ...), custom_call_target="tpu_custom_call" | custom-call | flops 536870912 | bytes 4194304 | tf_op jit(solution)/shard_map/pallas_call | solution.py:441
  4.4 0.0 copy-start.19
  4.4 0.0 copy-start.18
  4.4 0.0 copy-start.17
  4.4 19.1 %all_to_all.35.received = bf16[8,112,256]{2,1,0:T(8,128)(2,1)S(1)} all-to-all(bf16[8,112,256]{2,1,0:T(8,128)(2,1)} %get-tuple-element.69), channel_id=1, replica_groups=mesh['far'=4,'y'=4,'core'=2,'gy'=16] {'y','core'}, dimensions={0} | all-to-all | bytes 917504 | tf_op jit(solution)/shard_map/all_to_all | solution.py:460
  23.6 0.1 shard_map.215.mine
  23.6 0.0 copy-start.16
  23.6 4.7 %collective-permute-start = (bf16[112,256]{1,0:T(8,128)(2,1)S(1)}, bf16[112,256]{1,0:T(8,128)(2,1)S(1)}, u32[]{:S(2)}, u32[]{:S(2)}) collective-permute-start(bf16[112,256]{1,0:T(8,128)(2,1)S(1)} %shard_map.215.mine), channel_id=1, source_target_pairs={{0,128},{128,0},{256,384},{384,256},{1,129},{129,1},{257,385},{385... | collective-permute-start | bytes 172040 | tf_op jit(solution)/shard_map/ppermute | solution.py:470
  28.3 0.0 copy-done.19
  28.3 3.3 %collective-permute-start.2 = (bf16[256,256]{1,0:T(8,128)(2,1)S(1)}, bf16[256,256]{1,0:T(8,128)(2,1)S(1)}, u32[]{:S(2)}, u32[]{:S(2)}) collective-permute-start(bf16[256,256]{1,0:T(8,128)(2,1)S(1)} %copy-done.19), channel_id=1, source_target_pairs={{16,32},{48,64},{80,96},{112,128},{144,160},{176,192},{208,224},{2... | collective-permute-start | bytes 393224 | tf_op jit(solution)/shard_map/ppermute | solution.py:435
  31.6 0.0 copy-done.18
  31.6 0.7 collective-permute-start.3
  32.3 3.9 %collective-permute-done.other = bf16[112,256]{1,0:T(8,128)(2,1)S(1)} collective-permute-done((bf16[112,256]{1,0:T(8,128)(2,1)S(1)}, bf16[112,256]{1,0:T(8,128)(2,1)S(1)}, u32[]{:S(2)}, u32[]{:S(2)}) %collective-permute-start) | collective-permute-done | bytes 57376 | tf_op jit(solution)/shard_map/ppermute | solution.py:470
  36.2 0.0 copy-done.17
  36.2 2.6 %collective-permute-start.4 = (bf16[256,256]{1,0:T(8,128)(2,1)S(1)}, bf16[256,256]{1,0:T(8,128)(2,1)S(1)}, u32[]{:S(2)}, u32[]{:S(2)}) collective-permute-start(bf16[256,256]{1,0:T(8,128)(2,1)S(1)} %copy-done.17), channel_id=1, source_target_pairs={{0,1},{2,3},{4,5},{6,7},{8,9},{10,11},{12,13},{14,15},{1,0},{3,2},... | collective-permute-start | bytes 393224 | tf_op jit(solution)/shard_map/ppermute | solution.py:435
  38.8 0.0 copy-done.16
  38.8 1.9 %collective-permute-start.5 = (bf16[256,256]{1,0:T(8,128)(2,1)S(1)}, bf16[256,256]{1,0:T(8,128)(2,1)S(1)}, u32[]{:S(2)}, u32[]{:S(2)}) collective-permute-start(bf16[256,256]{1,0:T(8,128)(2,1)S(1)} %copy-done.16), channel_id=1, source_target_pairs={{0,16},{32,48},{64,80},{96,112},{128,144},{160,176},{192,208},{224... | collective-permute-start | bytes 393224 | tf_op jit(solution)/shard_map/ppermute | solution.py:435
  40.7 9.2 %collective-permute-start.1 = (bf16[112,256]{1,0:T(8,128)(2,1)S(1)}, bf16[112,256]{1,0:T(8,128)(2,1)S(1)}, u32[]{:S(2)}, u32[]{:S(2)}) collective-permute-start(bf16[112,256]{1,0:T(8,128)(2,1)S(1)} %shard_map.216.mine), channel_id=1, source_target_pairs={{0,384},{128,256},{256,128},{384,0},{1,385},{129,257},{257,129},{3... | collective-permute-start | bytes 172040 | tf_op jit(solution)/shard_map/ppermute | solution.py:475
  50.0 2.3 %collective-permute-done.1.other = bf16[112,256]{1,0:T(8,128)(2,1)S(1)} collective-permute-done((bf16[112,256]{1,0:T(8,128)(2,1)S(1)}, bf16[112,256]{1,0:T(8,128)(2,1)S(1)}, u32[]{:S(2)}, u32[]{:S(2)}) %collective-permute-start.1) | collective-permute-done | bytes 57376 | tf_op jit(solution)/shard_map/ppermute | solution.py:475
  52.2 0.0 collective-permute-done.2.arrived0
  52.2 0.0 collective-permute-done.3.arrived1
  52.2 0.0 collective-permute-done.4.arrived2
  52.2 0.0 collective-permute-done.5.arrived3
  52.3 0.1 shard_map.217
  52.4 7.6 %all_to_all.36.mine = bf16[4,96,256]{2,1,0:T(8,128)(2,1)S(1)} all-to-all(bf16[4,96,256]{2,1,0:T(8,128)(2,1)S(1)} %get-tuple-element.82), channel_id=1, replica_groups=mesh['far'=4,'y'=4,'core'=2,'gy'=16] {'y'}, dimensions={0} | all-to-all | bytes 393216 | tf_op jit(solution)/shard_map/all_to_all | solution.py:485
  60.0 3.5 %collective-permute-start.6 = (bf16[4,96,256]{2,1,0:T(8,128)(2,1)S(1)}, bf16[4,96,256]{2,1,0:T(8,128)(2,1)S(1)}, u32[]{:S(2)}, u32[]{:S(2)}) collective-permute-start(bf16[4,96,256]{2,1,0:T(8,128)(2,1)S(1)} %all_to_all.36.mine), channel_id=1, source_target_pairs={{0,16},{16,0},{1,17},{17,1},{2,18},{18,2},{3,19},{19,3},{4,20},{20... | collective-permute-start | bytes 589832 | tf_op jit(solution)/shard_map/ppermute | solution.py:486
  63.6 0.0 copy-start.11
  63.6 0.0 copy-done.1
  63.6 0.7 copy-done.11
  64.3 0.0 copy-start.14
  64.3 0.0 copy-start.15
  64.3 0.7 shard_map.218.aggregate
  65.0 0.0 collective-permute-done.6.other
  65.0 0.2 copy-done
  65.2 0.1 copy-done.3
  65.3 0.1 copy-done.4
  65.4 0.0 copy-done.10
  65.4 0.0 copy-done.14
  65.4 2.7 %shard_map.219 = (bf16[512,256]{1,0:T(8,128)(2,1)}, bf16[512,256]{1,0:T(8,128)(2,1)S(1)}, bf16[512,256]{1,0:T(8,128)(2,1)S(1)}, bf16[512,256]{1,0:T(8,128)(2,1)S...) custom-call(s32[2,4]{1,0:T(2,128)S(1)} %bitcast.18, ...), custom_call_target="tpu_custom_call" | custom-call | flops 671088640 | bytes 4194304 | tf_op jit(solution)/shard_map/pallas_call | solution.py:497
  68.1 0.7 copy-done.12
  68.8 0.0 copy-start.9
  68.8 1.9 %shard_map.220 = (bf16[4,224,256]{2,1,0:T(8,128)(2,1)S(1)}, bf16[4,288,256]{2,1,0:T(8,128)(2,1)S(1)}, f32[512,256]{1,0:T(8,128)S(1)}, f32[512,256]{1,0:T(8,128)S(1)}) custom-call(s32[4,3]{1,0:T(4,128)S(1)} %copy-done.12, s32[2,4]{1,0:T(2,128)S(1)} %bitcast.19, s32[1,512]{1,0:T(1,128)S(1)} %bitcast.15, bf16[512,256]{1,0:T(8,128)(2,1)S(1)} %copy-done, ...), custom_call_target="tpu_custom_call" | custom-call | flops 536870912 | bytes 5242880 | tf_op jit(solution)/shard_map/pallas_call | solution.py:511
  70.7 1.9 %collective-permute-start.10 = (bf16[4,288,256]{2,1,0:T(8,128)(2,1)S(1)}, bf16[4,288,256]{2,1,0:T(8,128)(2,1)S(1)}, u32[]{:S(2)}, u32[]{:S(2)}) collective-permute-start(bf16[4,288,256]{2,1,0:T(8,128)(2,1)S(1)} %get-tuple-element.107), channel_id=1, source_target_pairs={{0,16},{16,0},{1,17},{17,1},{2,18},{18,2},{3,19},{19,3},{4,20},{20... | collective-permute-start | bytes 1769480 | tf_op jit(solution)/shard_map/ppermute | solution.py:529
  72.6 2.6 %collective-permute-start.7 = (bf16[256,256]{1,0:T(8,128)(2,1)S(1)}, bf16[256,256]{1,0:T(8,128)(2,1)S(1)}, u32[]{:S(2)}, u32[]{:S(2)}) collective-permute-start(bf16[256,256]{1,0:T(8,128)(2,1)S(1)} %get-tuple-element.104), channel_id=1, source_target_pairs={{16,32},{48,64},{80,96},{112,128},{144,160},{176,192},{208,224},{2... | collective-permute-start | bytes 393224 | tf_op jit(solution)/shard_map/ppermute | solution.py:435
  75.2 0.7 collective-permute-start.8
  75.9 6.9 %collective-permute-start.9 = (bf16[256,256]{1,0:T(8,128)(2,1)S(1)}, bf16[256,256]{1,0:T(8,128)(2,1)S(1)}, u32[]{:S(2)}, u32[]{:S(2)}) collective-permute-start(bf16[256,256]{1,0:T(8,128)(2,1)S(1)} %get-tuple-element.106), channel_id=1, source_target_pairs={{0,1},{2,3},{4,5},{6,7},{8,9},{10,11},{12,13},{14,15},{1,0},{3,2},... | collective-permute-start | bytes 393224 | tf_op jit(solution)/shard_map/ppermute | solution.py:435
  82.8 0.0 collective-permute-done.7.back0
  82.8 0.0 collective-permute-done.8.back1
  82.8 5.8 %collective-permute-done.9.back2 = bf16[256,256]{1,0:T(8,128)(2,1)S(1)} collective-permute-done((bf16[256,256]{1,0:T(8,128)(2,1)S(1)}, bf16[256,256]{1,0:T(8,128)(2,1)S(1)}, u32[]{:S(2)}, u32[]{:S(2)}) %collective-permute-start.9) | collective-permute-done | bytes 131104 | tf_op jit(solution)/shard_map/ppermute | solution.py:435
  88.6 0.0 collective-permute-done.10.got_node
  88.7 0.6 copy-done.13
  89.3 1.5 shard_map.221
  90.9 1.9 %collective-permute-start.11 = (bf16[4,80,256]{2,1,0:T(8,128)(2,1)S(1)}, bf16[4,80,256]{2,1,0:T(8,128)(2,1)S(1)}, u32[]{:S(2)}, u32[]{:S(2)}) collective-permute-start(bf16[4,80,256]{2,1,0:T(8,128)(2,1)S(1)} %get-tuple-element.113), channel_id=1, source_target_pairs={{0,16},{16,0},{1,17},{17,1},{2,18},{18,2},{3,19},{19,3},{4,20},{20... | collective-permute-start | bytes 491528 | tf_op jit(solution)/shard_map/ppermute | solution.py:544
  92.8 1.4 collective-permute-done.11.got_edge
  94.1 0.1 shard_map.222
  94.3 16.4 %all_to_all.37.received = bf16[4,304,256]{2,1,0:T(8,128)(2,1)S(1)} all-to-all(bf16[4,304,256]{2,1,0:T(8,128)(2,1)S(1)} %shard_map.222), channel_id=1, replica_groups=mesh['far'=4,'y'=4,'core'=2,'gy'=16] {'y'}, dimensions={0} | all-to-all | bytes 1245184 | tf_op jit(solution)/shard_map/all_to_all | solution.py:548
  110.7 0.1 shard_map.223
  110.8 16.5 %all_to_all.38.received = bf16[16,16,256]{2,1,0:T(8,128)(2,1)S(1)} all-to-all(bf16[16,16,256]{2,1,0:T(8,128)(2,1)S(1)} %get-tuple-element.115), channel_id=1, replica_groups=mesh['far'=4,'y'=4,'core'=2,'gy'=16] {'gy'}, dimensions={0} | all-to-all | bytes 262144 | tf_op jit(solution)/shard_map/all_to_all | solution.py:555
  127.3 21.9 %all_to_all.39.received = bf16[4,112,256]{2,1,0:T(8,128)(2,1)S(1)} all-to-all(bf16[4,112,256]{2,1,0:T(8,128)(2,1)S(1)} %shard_map.224), channel_id=1, replica_groups=mesh['far'=4,'y'=4,'core'=2,'gy'=16] {'far'}, dimensions={0} | all-to-all | bytes 458752 | tf_op jit(solution)/shard_map/all_to_all | solution.py:559
  149.3 10.6 %all_to_all.40.grads = bf16[16,16,256]{2,1,0:T(8,128)(2,1)S(1)} all-to-all(bf16[16,16,256]{2,1,0:T(8,128)(2,1)S(1)} %get-tuple-element.118), channel_id=1, replica_groups=mesh['far'=4,'y'=4,'core'=2,'gy'=16] {'gy'}, dimensions={0} | all-to-all | bytes 262144 | tf_op jit(solution)/shard_map/all_to_all | solution.py:566
  159.9 9.9 %all_to_all.41.mine = bf16[4,304,256]{2,1,0:T(8,128)(2,1)S(1)} all-to-all(bf16[4,304,256]{2,1,0:T(8,128)(2,1)S(1)} %shard_map.226), channel_id=1, replica_groups=mesh['far'=4,'y'=4,'core'=2,'gy'=16] {'y'}, dimensions={0} | all-to-all | bytes 1245184 | tf_op jit(solution)/shard_map/all_to_all | solution.py:570
  169.8 10.0 %collective-permute-start.12 = (bf16[4,304,256]{2,1,0:T(8,128)(2,1)S(1)}, bf16[4,304,256]{2,1,0:T(8,128)(2,1)S(1)}, u32[]{:S(2)}, u32[]{:S(2)}) collective-permute-start(bf16[4,304,256]{2,1,0:T(8,128)(2,1)S(1)} %all_to_all.41.mine), channel_id=1, source_target_pairs={{0,16},{16,0},{1,17},{17,1},{2,18},{18,2},{3,19},{19,3},{4,20},{20... | collective-permute-start | bytes 1867784 | tf_op jit(solution)/shard_map/ppermute | solution.py:571
  179.8 1.7 collective-permute-done.12.other
  181.4 1.6 shard_map.227
  (23 shorter events, 0.2 us)
Async XLA Ops:
  4.4 23.9 %copy-start.19 = (bf16[256,256]{1,0:T(8,128)(2,1)S(1)}, bf16[256,256]{1,0:T(8,128)(2,1)}, u32[]{:S(2)}) copy-start(bf16[256,256]{1,0:T(8,128)(2,1)} %get-tuple-element.76) | copy-start | bytes 393220
  4.4 27.2 %copy-start.18 = (bf16[256,256]{1,0:T(8,128)(2,1)S(1)}, bf16[256,256]{1,0:T(8,128)(2,1)}, u32[]{:S(2)}) copy-start(bf16[256,256]{1,0:T(8,128)(2,1)} %get-tuple-element.77) | copy-start | bytes 393220
  4.4 31.8 %copy-start.17 = (bf16[256,256]{1,0:T(8,128)(2,1)S(1)}, bf16[256,256]{1,0:T(8,128)(2,1)}, u32[]{:S(2)}) copy-start(bf16[256,256]{1,0:T(8,128)(2,1)} %get-tuple-element.78) | copy-start | bytes 393220
  23.6 40.0 %copy-start.1 = (f32[512,256]{1,0:T(8,128)S(1)}, f32[512,256]{1,0:T(8,128)}, u32[]{:S(2)}) copy-start(f32[512,256]{1,0:T(8,128)} %get-tuple-element.87.local) | copy-start | bytes 1572868
  23.6 15.2 %copy-start.16 = (bf16[256,256]{1,0:T(8,128)(2,1)S(1)}, bf16[256,256]{1,0:T(8,128)(2,1)}, u32[]{:S(2)}) copy-start(bf16[256,256]{1,0:T(8,128)(2,1)} %get-tuple-element.79) | copy-start | bytes 393220
  23.6 12.6 %collective-permute-start = (bf16[112,256]{1,0:T(8,128)(2,1)S(1)}, bf16[112,256]{1,0:T(8,128)(2,1)S(1)}, u32[]{:S(2)}, u32[]{:S(2)}) collective-permute-start(bf16[112,256]{1,0:T(8,128)(2,1)S(1)} %shard_map.215.mine), channel_id=1, source_target_pairs={{0,128},{128,0},{256,384},{384,256},{1,129},{129,1},{257,385},{385... | collective-permute-start | bytes 172040 | tf_op jit(solution)/shard_map/ppermute | solution.py:470
  28.3 23.9 %collective-permute-start.2 = (bf16[256,256]{1,0:T(8,128)(2,1)S(1)}, bf16[256,256]{1,0:T(8,128)(2,1)S(1)}, u32[]{:S(2)}, u32[]{:S(2)}) collective-permute-start(bf16[256,256]{1,0:T(8,128)(2,1)S(1)} %copy-done.19), channel_id=1, source_target_pairs={{16,32},{48,64},{80,96},{112,128},{144,160},{176,192},{208,224},{2... | collective-permute-start | bytes 393224 | tf_op jit(solution)/shard_map/ppermute | solution.py:435
  31.6 20.6 %collective-permute-start.3 = (bf16[256,256]{1,0:T(8,128)(2,1)S(1)}, bf16[256,256]{1,0:T(8,128)(2,1)S(1)}, u32[]{:S(2)}, u32[]{:S(2)}) collective-permute-start(bf16[256,256]{1,0:T(8,128)(2,1)S(1)} %copy-done.18), channel_id=1, source_target_pairs={{1,2},{3,4},{5,6},{7,8},{9,10},{11,12},{13,14},{2,1},{4,3},{6,5},{... | collective-permute-start | bytes 393224 | tf_op jit(solution)/shard_map/ppermute | solution.py:435
  36.2 16.0 %collective-permute-start.4 = (bf16[256,256]{1,0:T(8,128)(2,1)S(1)}, bf16[256,256]{1,0:T(8,128)(2,1)S(1)}, u32[]{:S(2)}, u32[]{:S(2)}) collective-permute-start(bf16[256,256]{1,0:T(8,128)(2,1)S(1)} %copy-done.17), channel_id=1, source_target_pairs={{0,1},{2,3},{4,5},{6,7},{8,9},{10,11},{12,13},{14,15},{1,0},{3,2},... | collective-permute-start | bytes 393224 | tf_op jit(solution)/shard_map/ppermute | solution.py:435
  38.8 13.4 %collective-permute-start.5 = (bf16[256,256]{1,0:T(8,128)(2,1)S(1)}, bf16[256,256]{1,0:T(8,128)(2,1)S(1)}, u32[]{:S(2)}, u32[]{:S(2)}) collective-permute-start(bf16[256,256]{1,0:T(8,128)(2,1)S(1)} %copy-done.16), channel_id=1, source_target_pairs={{0,16},{32,48},{64,80},{96,112},{128,144},{160,176},{192,208},{224... | collective-permute-start | bytes 393224 | tf_op jit(solution)/shard_map/ppermute | solution.py:435
  40.7 11.5 %collective-permute-start.1 = (bf16[112,256]{1,0:T(8,128)(2,1)S(1)}, bf16[112,256]{1,0:T(8,128)(2,1)S(1)}, u32[]{:S(2)}, u32[]{:S(2)}) collective-permute-start(bf16[112,256]{1,0:T(8,128)(2,1)S(1)} %shard_map.216.mine), channel_id=1, source_target_pairs={{0,384},{128,256},{256,128},{384,0},{1,385},{129,257},{257,129},{3... | collective-permute-start | bytes 172040 | tf_op jit(solution)/shard_map/ppermute | solution.py:475
  60.0 5.0 %collective-permute-start.6 = (bf16[4,96,256]{2,1,0:T(8,128)(2,1)S(1)}, bf16[4,96,256]{2,1,0:T(8,128)(2,1)S(1)}, u32[]{:S(2)}, u32[]{:S(2)}) collective-permute-start(bf16[4,96,256]{2,1,0:T(8,128)(2,1)S(1)} %all_to_all.36.mine), channel_id=1, source_target_pairs={{0,16},{16,0},{1,17},{17,1},{2,18},{18,2},{3,19},{19,3},{4,20},{20... | collective-permute-start | bytes 589832 | tf_op jit(solution)/shard_map/ppermute | solution.py:486
  63.6 0.7 copy-start.11
  64.2 0.9 copy-start
  64.2 1.1 copy-start.3
  64.2 1.1 copy-start.4
  64.3 1.1 copy-start.10
  64.3 1.2 copy-start.14
  64.3 1.2 copy-start.15
  65.4 2.7 %copy-start.2 = (bf16[4,3,128,128]{3,2,1,0:T(8,128)(2,1)S(1)}, bf16[4,3,128,128]{3,2,1,0:T(8,128)(2,1)}, u32[]{:S(2)}) copy-start(bf16[4,3,128,128]{3,2,1,0:T(8,128)(2,1)} %blocks.1) | copy-start | bytes 1179652
  68.1 0.7 copy-start.12
  68.8 19.9 %copy-start.5 = (bf16[1,1,4,2,128,128]{5,4,3,2,1,0:T(8,128)(2,1)S(1)}, bf16[1,1,4,2,128,128]{5,4,3,2,1,0:T(8,128)(2,1)}, u32[]{:S(2)}) copy-start(bf16[1,1,4,2,128,128]{5,4,3,2,1,0:T(8,128)(2,1)} %param.21) | copy-start | bytes 786436
  68.8 19.9 %copy-start.6 = (bf16[512,256]{1,0:T(8,128)(2,1)S(1)}, bf16[512,256]{1,0:T(8,128)(2,1)}, u32[]{:S(2)}) copy-start(bf16[512,256]{1,0:T(8,128)(2,1)} %get-tuple-element.95.lifted) | copy-start | bytes 786436
  68.8 19.9 %copy-start.7 = (bf16[512,256]{1,0:T(8,128)(2,1)S(1)}, bf16[512,256]{1,0:T(8,128)(2,1)}, u32[]{:S(2)}) copy-start(bf16[512,256]{1,0:T(8,128)(2,1)} %get-tuple-element.96.active) | copy-start | bytes 786436
  68.8 19.9 %copy-start.8 = (bf16[256,256]{1,0:T(8,128)(2,1)S(1)}, bf16[256,256]{1,0:T(8,128)(2,1)}, u32[]{:S(2)}) copy-start(bf16[256,256]{1,0:T(8,128)(2,1)} %edge_lift.1) | copy-start | bytes 393220
  68.8 19.9 %copy-start.9 = (bf16[256,256]{1,0:T(8,128)(2,1)S(1)}, bf16[256,256]{1,0:T(8,128)(2,1)}, u32[]{:S(2)}) copy-start(bf16[256,256]{1,0:T(8,128)(2,1)} %edge_emit.1) | copy-start | bytes 393220
  70.7 17.9 %collective-permute-start.10 = (bf16[4,288,256]{2,1,0:T(8,128)(2,1)S(1)}, bf16[4,288,256]{2,1,0:T(8,128)(2,1)S(1)}, u32[]{:S(2)}, u32[]{:S(2)}) collective-permute-start(bf16[4,288,256]{2,1,0:T(8,128)(2,1)S(1)} %get-tuple-element.107), channel_id=1, source_target_pairs={{0,16},{16,0},{1,17},{17,1},{2,18},{18,2},{3,19},{19,3},{4,20},{20... | collective-permute-start | bytes 1769480 | tf_op jit(solution)/shard_map/ppermute | solution.py:529
  72.6 10.2 %collective-permute-start.7 = (bf16[256,256]{1,0:T(8,128)(2,1)S(1)}, bf16[256,256]{1,0:T(8,128)(2,1)S(1)}, u32[]{:S(2)}, u32[]{:S(2)}) collective-permute-start(bf16[256,256]{1,0:T(8,128)(2,1)S(1)} %get-tuple-element.104), channel_id=1, source_target_pairs={{16,32},{48,64},{80,96},{112,128},{144,160},{176,192},{208,224},{2... | collective-permute-start | bytes 393224 | tf_op jit(solution)/shard_map/ppermute | solution.py:435
  75.2 7.6 %collective-permute-start.8 = (bf16[256,256]{1,0:T(8,128)(2,1)S(1)}, bf16[256,256]{1,0:T(8,128)(2,1)S(1)}, u32[]{:S(2)}, u32[]{:S(2)}) collective-permute-start(bf16[256,256]{1,0:T(8,128)(2,1)S(1)} %get-tuple-element.105), channel_id=1, source_target_pairs={{1,2},{3,4},{5,6},{7,8},{9,10},{11,12},{13,14},{2,1},{4,3},{6,5},{... | collective-permute-start | bytes 393224 | tf_op jit(solution)/shard_map/ppermute | solution.py:435
  75.9 12.8 %collective-permute-start.9 = (bf16[256,256]{1,0:T(8,128)(2,1)S(1)}, bf16[256,256]{1,0:T(8,128)(2,1)S(1)}, u32[]{:S(2)}, u32[]{:S(2)}) collective-permute-start(bf16[256,256]{1,0:T(8,128)(2,1)S(1)} %get-tuple-element.106), channel_id=1, source_target_pairs={{0,1},{2,3},{4,5},{6,7},{8,9},{10,11},{12,13},{14,15},{1,0},{3,2},... | collective-permute-start | bytes 393224 | tf_op jit(solution)/shard_map/ppermute | solution.py:435
  88.6 0.7 copy-start.13
  90.9 3.3 %collective-permute-start.11 = (bf16[4,80,256]{2,1,0:T(8,128)(2,1)S(1)}, bf16[4,80,256]{2,1,0:T(8,128)(2,1)S(1)}, u32[]{:S(2)}, u32[]{:S(2)}) collective-permute-start(bf16[4,80,256]{2,1,0:T(8,128)(2,1)S(1)} %get-tuple-element.113), channel_id=1, source_target_pairs={{0,16},{16,0},{1,17},{17,1},{2,18},{18,2},{3,19},{19,3},{4,20},{20... | collective-permute-start | bytes 491528 | tf_op jit(solution)/shard_map/ppermute | solution.py:544
  169.8 11.6 %collective-permute-start.12 = (bf16[4,304,256]{2,1,0:T(8,128)(2,1)S(1)}, bf16[4,304,256]{2,1,0:T(8,128)(2,1)S(1)}, u32[]{:S(2)}, u32[]{:S(2)}) collective-permute-start(bf16[4,304,256]{2,1,0:T(8,128)(2,1)S(1)} %all_to_all.41.mine), channel_id=1, source_target_pairs={{0,16},{16,0},{1,17},{17,1},{2,18},{18,2},{3,19},{19,3},{4,20},{20... | collective-permute-start | bytes 1867784 | tf_op jit(solution)/shard_map/ppermute | solution.py:571

commit v4 on v3

--- a/solution.py
+++ b/solution.py
@@ -168,7 +168,7 @@
 
 def node_kernel(target, clus, state, upstream, aggregate, mine, other, node_lift, node_emit, params,
                 updated, coarse, active, emit_grad, lifted_grad, aggregate_grad,
-                coarse_grad, back0, back1, back2, vectors, means, slopes, hot):
+                coarse_grad, back0, back1, back2, back3, vectors, means, slopes, hot):
     features = state.shape[1]
     clusters, share = means.shape[0], mine.shape[1]
     core = lax.axis_index("core")
@@ -218,7 +218,7 @@
     bias_grad += jnp.sum(down.astype(F32), axis=0, keepdims=True)
     aggregate_grad[...] = mm_nt(down, lift_agg).astype(BF16)
     coarse_grad[...] = mm_nt(down, lift_coarse).astype(BF16)
-    for slot, back in zip(slots("in"), (back0, back1, back2)):
+    for slot, back in zip(slots("in"), (back0, back1, back2, back3)):
         for cut in range(back.shape[0] // TILE):
             back[rows_of(cut)] = aggregate_grad[tile_rows(target[cut, slot])]
     vectors[...] = jnp.zeros(vectors.shape, F32)
@@ -239,11 +239,11 @@
     core = lax.axis_index("core")
     for index in range(keep.shape[0]):
         keep[index] = stack[2 * index + core]
-        send[index, 0:stack.shape[1]] = stack[2 * index + 1 - core]
-
-
-def weight_kernel(sizes, adjacency, target, clus, state, upstream, aggregate, coarse, active,
-                  emit_grad, lifted_grad, aggregate_grad, coarse_grad, blocks, node_lift,
+        send[index] = stack[2 * index + 1 - core]
+
+
+def weight_kernel(sizes, adjacency, clus, state, upstream, aggregate, coarse, active, emit_grad,
+                  lifted_grad, aggregate_grad, coarse_grad, blocks, node_lift,
                   keep, send, local, partial, stack, hot):
     peers, share, node_rows, _ = sizes
     features = state.shape[1]
@@ -256,11 +256,6 @@
         put_chunks(stack, share, node_rows, index * features, mm_tn(block[...], down))
     put_chunks(stack, share, node_rows, 3 * features, mm_tn(active[...], emit_grad[...]))
     part_ways(stack, keep, send)
-    each, last = send.shape[1] - keep.shape[1], slots("in")[3]
-    for index in range(send.shape[0]):
-        cut, row = divmod(index * each, TILE)
-        start = pl.multiple_of(target[cut, last] * TILE + row, each)
-        send[index, keep.shape[1]:] = aggregate_grad[pl.ds(start, each)]
     partial[...] = upstream[...].astype(F32) + mm_nt(down, node_lift[0:features])
     local[...] = jnp.zeros(local.shape, F32)
     for tile in range(state.shape[0] // TILE):
@@ -271,14 +266,12 @@
             )
 
 
-def edge_kernel(sizes, source, state, lifted, active, local, back0, back1, back2, got_node, cuts,
+def edge_kernel(sizes, source, state, lifted, active, local, back0, back1, back2, back3, cuts,
                 edge_lift, edge_emit, partial, vectors,
                 keep, send, partial_out, total, message_grad, lifted_grad, edge_part):
-    peers, share, node_rows, edge_rows = sizes
+    peers, _, _, edge_rows = sizes
     features = state.shape[1]
     total[...] = local[...]
-    first = share + node_rows
-    back3 = jnp.concatenate([got_node[index, first:] for index in range(got_node.shape[0])], axis=0)
     for slot, back in zip(slots("out"), (back0, back1, back2, back3)):
         for cut in range(cuts.shape[1]):
             total[tile_rows(source[cut, slot])] += mm_tn(cuts[slot, cut], back[rows_of(cut)])
@@ -303,9 +296,7 @@
 
 def merge_kernel(keep_node, keep_edge, got_node, got_edge, out):
     rows = keep_node.shape[1]
-    out[:, 0:rows] = (
-        keep_node[...].astype(F32) + got_node[:, 0:rows].astype(F32)
-    ).astype(BF16)
+    out[:, 0:rows] = (keep_node[...].astype(F32) + got_node[...].astype(F32)).astype(BF16)
     out[:, rows:] = (keep_edge[...].astype(F32) + got_edge[...].astype(F32)).astype(BF16)
 
 
@@ -494,9 +485,9 @@
     )(target, local, *arrived)
 
     (updated, coarse, node_active, emit_grad, lifted_grad, aggregate_grad, coarse_grad,
-     back0, back1, back2, vectors) = call(
+     back0, back1, back2, back3, vectors) = call(
         node_kernel,
-        [narrow] * 7 + [cut_part] * 3 + [like((8, features), F32)],
+        [narrow] * 7 + [cut_part] * 4 + [like((8, features), F32)],
         smem(1) + vmem(9),
         [
             pltpu.VMEM((peers * share, features), BF16),
@@ -510,22 +501,18 @@
 
     keep_node, send_node, message_local, partial = call(
         functools.partial(weight_kernel, sizes),
-        [
-            like((across, share + node_rows, features), BF16),
-            like((across, share + node_rows + cut_rows // across, features), BF16),
-            wide,
-            wide,
-        ],
-        smem(2) + vmem(12),
+        [like((across, share + node_rows, features), BF16)] * 2 + [wide, wide],
+        smem(1) + vmem(12),
         [
             pltpu.VMEM((peers, share + node_rows, features), BF16),
             pltpu.VMEM((peers * share, rows), BF16),
         ],
         flops=8 * layer,
         moved=5 << 20,
-    )(adjacency, target, clus, node_state, node_grad, aggregate, coarse, node_active, emit_grad,
+    )(adjacency, clus, node_state, node_grad, aggregate, coarse, node_active, emit_grad,
       lifted_grad, aggregate_grad, coarse_grad, edge_blocks, node_lift)
-    returned = swap((back0, back1, back2))
+    returned = swap((back0, back1, back2, back3))
+    send_node, *returned = lax.optimization_barrier((send_node, *returned))
     got_node = lax.ppermute(send_node, "core", both_cores)
     keep_edge, send_edge, partial = call(
         functools.partial(edge_kernel, sizes),
@@ -539,7 +526,7 @@
         ],
         flops=8 * layer,
         moved=5 << 20,
-    )(source, node_state, lifted, active, message_local, *returned, got_node, cuts, edge_lift, edge_emit,
+    )(source, node_state, lifted, active, message_local, *returned, cuts, edge_lift, edge_emit,
       partial, vectors)
     got_edge = lax.ppermute(send_edge, "core", both_cores)
     merged = call(

time: 184 us -> 182 us (0.989)
  waiting for transfers between devices: 15 us -> 9.51 us
  blocking collectives: 102 us -> 104 us
    ppermute x7 -> x8, waiting for transfers between devices: 5.81 us -> 0.44 us  [swap(): moved.append(lax.ppermute(part, axis, pairs + [(j, i) for i, j in pairs]))]
    all_to_all x1, blocking collectives: 16.4 us -> 19.6 us  [shards(): received = lax.all_to_all(merged, 'y', 0, 0, tiled=True)]
    ppermute x7 -> x8, starting transfers between devices: 18.6 us -> 20.1 us  [swap(): moved.append(lax.ppermute(part, axis, pairs + [(j, i) for i, j in pairs]))]
  transfers between devices with their start and end apart: 13 -> 14, of which waited for: 5 -> 5; matrix products, arithmetic and copies ran while one was open for 0% -> 0% of each run, Pallas kernels for 0% -> 2%
where the time goes in v4:
time: 182 us; the launch traced here: 181 us
  blocking collectives  104 us (57%)
  starting transfers between devices  51 us (28%)
  Pallas kernels  12.4 us (7%)
  waiting for transfers between devices  9.51 us (5%)
  local copies, waits for them, and re-layouts  2.45 us (1%)
    all_to_all x1, blocking collectives, shards(): received = lax.all_to_all(joined, 'far', 0, 0, tiled=True)  23.1 us
    ppermute x8, starting transfers between devices, swap(): moved.append(lax.ppermute(part, axis, pairs + [(j, i) for i, j in pairs]))  20.1 us
    all_to_all x1, blocking collectives, shards(): received = lax.all_to_all(merged, 'y', 0, 0, tiled=True)  19.6 us
    all_to_all x1, blocking collectives, shards(): received = lax.all_to_all(pool, near, 0, 0, tiled=True)  19.1 us
    all_to_all x1, blocking collectives, shards(): received = lax.all_to_all(grads, 'gy', 0, 0, tiled=True)  15.3 us
    all_to_all x1, blocking collectives, shards(): mine = lax.all_to_all(spread, 'y', 0, 0, tiled=True)  9.85 us
    all_to_all x1, blocking collectives, shards(): grads = lax.all_to_all(grads, 'gy', 0, 0, tiled=True)  9.82 us
    ppermute x1, starting transfers between devices, shards(): other = lax.ppermute(mine, 'core', both_cores)  9.23 us
  transfers between devices with their start and end apart: 14, of which 5 were waited for; matrix products, arithmetic and copies ran while one was open for 0% of the time, Pallas kernels for 2%

profile of v4, /device:TPU:1, one launch (start us, length us, event | category | flops | bytes accessed | tf_op | source)
XLA Modules:
  0.0 180.9 jit_solution(2674297569549399953)
XLA Ops:
  0.6 3.7 %shard_map.214 = (bf16[8,112,256]{2,1,0:T(8,128)(2,1)}, bf16[256,256]{1,0:T(8,128)(2,1)}, bf16[256,256]{1,0:T(8,128)(2,1)}, bf16[256,256]{1,0:T(8,128)(2,1)}, bf...) custom-call(s32[1,512]{1,0:T(1,128)} %bitcast.13, ...), custom_call_target="tpu_custom_call" | custom-call | flops 536870912 | bytes 4194304 | tf_op jit(solution)/shard_map/pallas_call | solution.py:432
  4.4 0.0 copy-start.19
  4.4 0.0 copy-start.18
  4.4 0.0 copy-start.17
  4.4 19.1 %all_to_all.35.received = bf16[8,112,256]{2,1,0:T(8,128)(2,1)S(1)} all-to-all(bf16[8,112,256]{2,1,0:T(8,128)(2,1)} %get-tuple-element.75), channel_id=1, replica_groups=mesh['far'=4,'y'=4,'core'=2,'gy'=16] {'y','core'}, dimensions={0} | all-to-all | bytes 917504 | tf_op jit(solution)/shard_map/all_to_all | solution.py:451
  23.6 0.1 shard_map.215.mine
  23.6 4.7 %collective-permute-start = (bf16[112,256]{1,0:T(8,128)(2,1)S(1)}, bf16[112,256]{1,0:T(8,128)(2,1)S(1)}, u32[]{:S(2)}, u32[]{:S(2)}) collective-permute-start(bf16[112,256]{1,0:T(8,128)(2,1)S(1)} %shard_map.215.mine), channel_id=1, source_target_pairs={{0,128},{128,0},{256,384},{384,256},{1,129},{129,1},{257,385},{385... | collective-permute-start | bytes 172040 | tf_op jit(solution)/shard_map/ppermute | solution.py:461
  28.3 3.3 %collective-permute-start.2 = (bf16[256,256]{1,0:T(8,128)(2,1)S(1)}, bf16[256,256]{1,0:T(8,128)(2,1)S(1)}, u32[]{:S(2)}, u32[]{:S(2)}) collective-permute-start(bf16[256,256]{1,0:T(8,128)(2,1)S(1)} %copy-done.19), channel_id=1, source_target_pairs={{16,32},{48,64},{80,96},{112,128},{144,160},{176,192},{208,224},{2... | collective-permute-start | bytes 393224 | tf_op jit(solution)/shard_map/ppermute | solution.py:426
  31.6 0.0 copy-done.18
  31.6 0.7 collective-permute-start.3
  32.3 3.9 %collective-permute-done.other = bf16[112,256]{1,0:T(8,128)(2,1)S(1)} collective-permute-done((bf16[112,256]{1,0:T(8,128)(2,1)S(1)}, bf16[112,256]{1,0:T(8,128)(2,1)S(1)}, u32[]{:S(2)}, u32[]{:S(2)}) %collective-permute-start) | collective-permute-done | bytes 57376 | tf_op jit(solution)/shard_map/ppermute | solution.py:461
  36.2 2.6 %collective-permute-start.4 = (bf16[256,256]{1,0:T(8,128)(2,1)S(1)}, bf16[256,256]{1,0:T(8,128)(2,1)S(1)}, u32[]{:S(2)}, u32[]{:S(2)}) collective-permute-start(bf16[256,256]{1,0:T(8,128)(2,1)S(1)} %copy-done.17), channel_id=1, source_target_pairs={{0,1},{2,3},{4,5},{6,7},{8,9},{10,11},{12,13},{14,15},{1,0},{3,2},... | collective-permute-start | bytes 393224 | tf_op jit(solution)/shard_map/ppermute | solution.py:426
  38.8 1.9 %collective-permute-start.5 = (bf16[256,256]{1,0:T(8,128)(2,1)S(1)}, bf16[256,256]{1,0:T(8,128)(2,1)S(1)}, u32[]{:S(2)}, u32[]{:S(2)}) collective-permute-start(bf16[256,256]{1,0:T(8,128)(2,1)S(1)} %copy-done.16), channel_id=1, source_target_pairs={{0,16},{32,48},{64,80},{96,112},{128,144},{160,176},{192,208},{224... | collective-permute-start | bytes 393224 | tf_op jit(solution)/shard_map/ppermute | solution.py:426
  40.7 9.2 %collective-permute-start.1 = (bf16[112,256]{1,0:T(8,128)(2,1)S(1)}, bf16[112,256]{1,0:T(8,128)(2,1)S(1)}, u32[]{:S(2)}, u32[]{:S(2)}) collective-permute-start(bf16[112,256]{1,0:T(8,128)(2,1)S(1)} %shard_map.216.mine), channel_id=1, source_target_pairs={{0,384},{128,256},{256,128},{384,0},{1,385},{129,257},{257,129},{3... | collective-permute-start | bytes 172040 | tf_op jit(solution)/shard_map/ppermute | solution.py:466
  50.0 2.3 %collective-permute-done.1.other = bf16[112,256]{1,0:T(8,128)(2,1)S(1)} collective-permute-done((bf16[112,256]{1,0:T(8,128)(2,1)S(1)}, bf16[112,256]{1,0:T(8,128)(2,1)S(1)}, u32[]{:S(2)}, u32[]{:S(2)}) %collective-permute-start.1) | collective-permute-done | bytes 57376 | tf_op jit(solution)/shard_map/ppermute | solution.py:466
  52.2 0.0 collective-permute-done.2.arrived0
  52.2 0.0 collective-permute-done.3.arrived1
  52.2 0.0 collective-permute-done.4.arrived2
  52.2 0.0 collective-permute-done.5.arrived3
  52.3 0.1 shard_map.217
  52.4 7.7 %all_to_all.36.mine = bf16[4,96,256]{2,1,0:T(8,128)(2,1)S(1)} all-to-all(bf16[4,96,256]{2,1,0:T(8,128)(2,1)S(1)} %get-tuple-element.88), channel_id=1, replica_groups=mesh['far'=4,'y'=4,'core'=2,'gy'=16] {'y'}, dimensions={0} | all-to-all | bytes 393216 | tf_op jit(solution)/shard_map/all_to_all | solution.py:476
  60.0 3.5 %collective-permute-start.6 = (bf16[4,96,256]{2,1,0:T(8,128)(2,1)S(1)}, bf16[4,96,256]{2,1,0:T(8,128)(2,1)S(1)}, u32[]{:S(2)}, u32[]{:S(2)}) collective-permute-start(bf16[4,96,256]{2,1,0:T(8,128)(2,1)S(1)} %all_to_all.36.mine), channel_id=1, source_target_pairs={{0,16},{16,0},{1,17},{17,1},{2,18},{18,2},{3,19},{19,3},{4,20},{20... | collective-permute-start | bytes 589832 | tf_op jit(solution)/shard_map/ppermute | solution.py:477
  63.6 0.0 copy-start.13
  63.6 0.7 copy-done.13
  64.3 0.0 copy-start.14
  64.3 0.7 shard_map.218.aggregate
  65.0 0.0 collective-permute-done.6.other
  65.0 0.2 copy-done
  65.2 0.1 copy-done.3
  65.3 0.1 copy-done.4
  65.4 0.0 copy-done.14
  65.4 0.0 copy-done.15
  65.4 2.4 %shard_map.219 = (bf16[512,256]{1,0:T(8,128)(2,1)}, bf16[512,256]{1,0:T(8,128)(2,1)S(1)}, bf16[512,256]{1,0:T(8,128)(2,1)S(1)}, bf16[512,256]{1,0:T(8,128)(2,1)S...) custom-call(s32[2,4]{1,0:T(2,128)S(1)} %bitcast.20, ...), custom_call_target="tpu_custom_call" | custom-call | flops 671088640 | bytes 4194304 | tf_op jit(solution)/shard_map/pallas_call | solution.py:488
  67.9 2.1 %collective-permute-start.7 = (bf16[256,256]{1,0:T(8,128)(2,1)S(1)}, bf16[256,256]{1,0:T(8,128)(2,1)S(1)}, u32[]{:S(2)}, u32[]{:S(2)}) collective-permute-start(bf16[256,256]{1,0:T(8,128)(2,1)S(1)} %get-tuple-element.111), channel_id=1, source_target_pairs={{16,32},{48,64},{80,96},{112,128},{144,160},{176,192},{208,224},{2... | collective-permute-start | bytes 393224 | tf_op jit(solution)/shard_map/ppermute | solution.py:426
  70.0 0.7 collective-permute-start.8
  70.7 6.9 %collective-permute-start.9 = (bf16[256,256]{1,0:T(8,128)(2,1)S(1)}, bf16[256,256]{1,0:T(8,128)(2,1)S(1)}, u32[]{:S(2)}, u32[]{:S(2)}) collective-permute-start(bf16[256,256]{1,0:T(8,128)(2,1)S(1)} %get-tuple-element.113), channel_id=1, source_target_pairs={{0,1},{2,3},{4,5},{6,7},{8,9},{10,11},{12,13},{14,15},{1,0},{3,2},... | collective-permute-start | bytes 393224 | tf_op jit(solution)/shard_map/ppermute | solution.py:426
  77.6 1.9 %collective-permute-start.10 = (bf16[256,256]{1,0:T(8,128)(2,1)S(1)}, bf16[256,256]{1,0:T(8,128)(2,1)S(1)}, u32[]{:S(2)}, u32[]{:S(2)}) collective-permute-start(bf16[256,256]{1,0:T(8,128)(2,1)S(1)} %get-tuple-element.114), channel_id=1, source_target_pairs={{0,16},{32,48},{64,80},{96,112},{128,144},{160,176},{192,208},{224... | collective-permute-start | bytes 393224 | tf_op jit(solution)/shard_map/ppermute | solution.py:426
  79.5 0.0 copy-start.11
  79.5 0.7 copy-done.11
  80.2 0.0 copy-start.9
  80.2 1.9 %shard_map.220 = (bf16[4,224,256]{2,1,0:T(8,128)(2,1)S(1)}, bf16[4,224,256]{2,1,0:T(8,128)(2,1)S(1)}, f32[512,256]{1,0:T(8,128)S(1)}, f32[512,256]{1,0:T(8,128)S(1)}) custom-call(s32[4,3]{1,0:T(4,128)S(1)} %copy-done.11, s32[1,512]{1,0:T(1,128)S(1)} %bitcast.15, bf16[512,256]{1,0:T(8,128)(2,1)S(1)} %copy-done, bf16[512,256]{1,0:T(8,128)(2,1)S(1)} %copy-done.4, ...), custom_call_target="tpu_custom_call" | custom-call | flops 536870912 | bytes 5242880 | tf_op jit(solution)/shard_map/pallas_call | solution.py:502
  82.1 0.0 collective-permute-done.7.back0
  82.1 0.0 collective-permute-done.8.back1
  82.1 0.4 collective-permute-done.9.back2
  82.5 0.0 collective-permute-done.10.back3
  82.5 2.3 %collective-permute-start.11 = (bf16[4,224,256]{2,1,0:T(8,128)(2,1)S(1)}, bf16[4,224,256]{2,1,0:T(8,128)(2,1)S(1)}, u32[]{:S(2)}, u32[]{:S(2)}) collective-permute-start(bf16[4,224,256]{2,1,0:T(8,128)(2,1)S(1)} %get-tuple-element.124), channel_id=1, source_target_pairs={{0,16},{16,0},{1,17},{17,1},{2,18},{18,2},{3,19},{19,3},{4,20},{20... | collective-permute-start | bytes 1376264 | tf_op jit(solution)/shard_map/ppermute | solution.py:516
  84.9 0.0 copy-start.12
  84.9 0.0 copy-done.5
  84.9 0.0 copy-done.6
  84.9 0.6 copy-done.12
  85.5 1.5 shard_map.221
  87.1 2.0 %collective-permute-start.12 = (bf16[4,80,256]{2,1,0:T(8,128)(2,1)S(1)}, bf16[4,80,256]{2,1,0:T(8,128)(2,1)S(1)}, u32[]{:S(2)}, u32[]{:S(2)}) collective-permute-start(bf16[4,80,256]{2,1,0:T(8,128)(2,1)S(1)} %get-tuple-element.125), channel_id=1, source_target_pairs={{0,16},{16,0},{1,17},{17,1},{2,18},{18,2},{3,19},{19,3},{4,20},{20... | collective-permute-start | bytes 491528 | tf_op jit(solution)/shard_map/ppermute | solution.py:531
  89.1 1.3 collective-permute-done.12.got_edge
  90.4 0.0 collective-permute-done.11.got_node
  90.4 0.1 shard_map.222
  90.5 19.6 %all_to_all.37.received = bf16[4,304,256]{2,1,0:T(8,128)(2,1)S(1)} all-to-all(bf16[4,304,256]{2,1,0:T(8,128)(2,1)S(1)} %shard_map.222), channel_id=1, replica_groups=mesh['far'=4,'y'=4,'core'=2,'gy'=16] {'y'}, dimensions={0} | all-to-all | bytes 1245184 | tf_op jit(solution)/shard_map/all_to_all | solution.py:535
  110.1 0.1 shard_map.223
  110.2 15.3 %all_to_all.38.received = bf16[16,16,256]{2,1,0:T(8,128)(2,1)S(1)} all-to-all(bf16[16,16,256]{2,1,0:T(8,128)(2,1)S(1)} %get-tuple-element.127), channel_id=1, replica_groups=mesh['far'=4,'y'=4,'core'=2,'gy'=16] {'gy'}, dimensions={0} | all-to-all | bytes 262144 | tf_op jit(solution)/shard_map/all_to_all | solution.py:542
  125.5 23.1 %all_to_all.39.received = bf16[4,112,256]{2,1,0:T(8,128)(2,1)S(1)} all-to-all(bf16[4,112,256]{2,1,0:T(8,128)(2,1)S(1)} %shard_map.224), channel_id=1, replica_groups=mesh['far'=4,'y'=4,'core'=2,'gy'=16] {'far'}, dimensions={0} | all-to-all | bytes 458752 | tf_op jit(solution)/shard_map/all_to_all | solution.py:546
  148.6 9.8 %all_to_all.40.grads = bf16[16,16,256]{2,1,0:T(8,128)(2,1)S(1)} all-to-all(bf16[16,16,256]{2,1,0:T(8,128)(2,1)S(1)} %get-tuple-element.130), channel_id=1, replica_groups=mesh['far'=4,'y'=4,'core'=2,'gy'=16] {'gy'}, dimensions={0} | all-to-all | bytes 262144 | tf_op jit(solution)/shard_map/all_to_all | solution.py:553
  158.5 9.9 %all_to_all.41.mine = bf16[4,304,256]{2,1,0:T(8,128)(2,1)S(1)} all-to-all(bf16[4,304,256]{2,1,0:T(8,128)(2,1)S(1)} %shard_map.226), channel_id=1, replica_groups=mesh['far'=4,'y'=4,'core'=2,'gy'=16] {'y'}, dimensions={0} | all-to-all | bytes 1245184 | tf_op jit(solution)/shard_map/all_to_all | solution.py:557
  168.4 9.2 %collective-permute-start.13 = (bf16[4,304,256]{2,1,0:T(8,128)(2,1)S(1)}, bf16[4,304,256]{2,1,0:T(8,128)(2,1)S(1)}, u32[]{:S(2)}, u32[]{:S(2)}) collective-permute-start(bf16[4,304,256]{2,1,0:T(8,128)(2,1)S(1)} %all_to_all.41.mine), channel_id=1, source_target_pairs={{0,16},{16,0},{1,17},{17,1},{2,18},{18,2},{3,19},{19,3},{4,20},{20... | collective-permute-start | bytes 1867784 | tf_op jit(solution)/shard_map/ppermute | solution.py:558
  177.6 1.7 collective-permute-done.13.other
  179.3 1.6 shard_map.227
  (25 shorter events, 0.2 us)
Async XLA Ops:
  4.4 23.9 %copy-start.19 = (bf16[256,256]{1,0:T(8,128)(2,1)S(1)}, bf16[256,256]{1,0:T(8,128)(2,1)}, u32[]{:S(2)}) copy-start(bf16[256,256]{1,0:T(8,128)(2,1)} %get-tuple-element.82) | copy-start | bytes 393220
  4.4 27.2 %copy-start.18 = (bf16[256,256]{1,0:T(8,128)(2,1)S(1)}, bf16[256,256]{1,0:T(8,128)(2,1)}, u32[]{:S(2)}) copy-start(bf16[256,256]{1,0:T(8,128)(2,1)} %get-tuple-element.83) | copy-start | bytes 393220
  4.4 31.8 %copy-start.17 = (bf16[256,256]{1,0:T(8,128)(2,1)S(1)}, bf16[256,256]{1,0:T(8,128)(2,1)}, u32[]{:S(2)}) copy-start(bf16[256,256]{1,0:T(8,128)(2,1)} %get-tuple-element.84) | copy-start | bytes 393220
  23.6 40.0 %copy-start.1 = (f32[512,256]{1,0:T(8,128)S(1)}, f32[512,256]{1,0:T(8,128)}, u32[]{:S(2)}) copy-start(f32[512,256]{1,0:T(8,128)} %get-tuple-element.93.local) | copy-start | bytes 1572868
  23.6 15.2 %copy-start.16 = (bf16[256,256]{1,0:T(8,128)(2,1)S(1)}, bf16[256,256]{1,0:T(8,128)(2,1)}, u32[]{:S(2)}) copy-start(bf16[256,256]{1,0:T(8,128)(2,1)} %get-tuple-element.85) | copy-start | bytes 393220
  23.6 12.6 %collective-permute-start = (bf16[112,256]{1,0:T(8,128)(2,1)S(1)}, bf16[112,256]{1,0:T(8,128)(2,1)S(1)}, u32[]{:S(2)}, u32[]{:S(2)}) collective-permute-start(bf16[112,256]{1,0:T(8,128)(2,1)S(1)} %shard_map.215.mine), channel_id=1, source_target_pairs={{0,128},{128,0},{256,384},{384,256},{1,129},{129,1},{257,385},{385... | collective-permute-start | bytes 172040 | tf_op jit(solution)/shard_map/ppermute | solution.py:461
  28.3 23.9 %collective-permute-start.2 = (bf16[256,256]{1,0:T(8,128)(2,1)S(1)}, bf16[256,256]{1,0:T(8,128)(2,1)S(1)}, u32[]{:S(2)}, u32[]{:S(2)}) collective-permute-start(bf16[256,256]{1,0:T(8,128)(2,1)S(1)} %copy-done.19), channel_id=1, source_target_pairs={{16,32},{48,64},{80,96},{112,128},{144,160},{176,192},{208,224},{2... | collective-permute-start | bytes 393224 | tf_op jit(solution)/shard_map/ppermute | solution.py:426
  31.6 20.6 %collective-permute-start.3 = (bf16[256,256]{1,0:T(8,128)(2,1)S(1)}, bf16[256,256]{1,0:T(8,128)(2,1)S(1)}, u32[]{:S(2)}, u32[]{:S(2)}) collective-permute-start(bf16[256,256]{1,0:T(8,128)(2,1)S(1)} %copy-done.18), channel_id=1, source_target_pairs={{1,2},{3,4},{5,6},{7,8},{9,10},{11,12},{13,14},{2,1},{4,3},{6,5},{... | collective-permute-start | bytes 393224 | tf_op jit(solution)/shard_map/ppermute | solution.py:426
  36.2 16.0 %collective-permute-start.4 = (bf16[256,256]{1,0:T(8,128)(2,1)S(1)}, bf16[256,256]{1,0:T(8,128)(2,1)S(1)}, u32[]{:S(2)}, u32[]{:S(2)}) collective-permute-start(bf16[256,256]{1,0:T(8,128)(2,1)S(1)} %copy-done.17), channel_id=1, source_target_pairs={{0,1},{2,3},{4,5},{6,7},{8,9},{10,11},{12,13},{14,15},{1,0},{3,2},... | collective-permute-start | bytes 393224 | tf_op jit(solution)/shard_map/ppermute | solution.py:426
  38.8 13.4 %collective-permute-start.5 = (bf16[256,256]{1,0:T(8,128)(2,1)S(1)}, bf16[256,256]{1,0:T(8,128)(2,1)S(1)}, u32[]{:S(2)}, u32[]{:S(2)}) collective-permute-start(bf16[256,256]{1,0:T(8,128)(2,1)S(1)} %copy-done.16), channel_id=1, source_target_pairs={{0,16},{32,48},{64,80},{96,112},{128,144},{160,176},{192,208},{224... | collective-permute-start | bytes 393224 | tf_op jit(solution)/shard_map/ppermute | solution.py:426
  40.7 11.5 %collective-permute-start.1 = (bf16[112,256]{1,0:T(8,128)(2,1)S(1)}, bf16[112,256]{1,0:T(8,128)(2,1)S(1)}, u32[]{:S(2)}, u32[]{:S(2)}) collective-permute-start(bf16[112,256]{1,0:T(8,128)(2,1)S(1)} %shard_map.216.mine), channel_id=1, source_target_pairs={{0,384},{128,256},{256,128},{384,0},{1,385},{129,257},{257,129},{3... | collective-permute-start | bytes 172040 | tf_op jit(solution)/shard_map/ppermute | solution.py:466
  60.0 5.0 %collective-permute-start.6 = (bf16[4,96,256]{2,1,0:T(8,128)(2,1)S(1)}, bf16[4,96,256]{2,1,0:T(8,128)(2,1)S(1)}, u32[]{:S(2)}, u32[]{:S(2)}) collective-permute-start(bf16[4,96,256]{2,1,0:T(8,128)(2,1)S(1)} %all_to_all.36.mine), channel_id=1, source_target_pairs={{0,16},{16,0},{1,17},{17,1},{2,18},{18,2},{3,19},{19,3},{4,20},{20... | collective-permute-start | bytes 589832 | tf_op jit(solution)/shard_map/ppermute | solution.py:477
  63.6 0.7 copy-start.13
  64.2 0.9 copy-start
  64.2 1.1 copy-start.3
  64.2 1.1 copy-start.4
  64.3 1.1 copy-start.10
  64.3 1.2 copy-start.14
  64.3 1.2 copy-start.15
  65.4 14.1 %copy-start.2 = (bf16[4,3,128,128]{3,2,1,0:T(8,128)(2,1)S(1)}, bf16[4,3,128,128]{3,2,1,0:T(8,128)(2,1)}, u32[]{:S(2)}) copy-start(bf16[4,3,128,128]{3,2,1,0:T(8,128)(2,1)} %blocks.1) | copy-start | bytes 1179652
  67.9 14.2 %collective-permute-start.7 = (bf16[256,256]{1,0:T(8,128)(2,1)S(1)}, bf16[256,256]{1,0:T(8,128)(2,1)S(1)}, u32[]{:S(2)}, u32[]{:S(2)}) collective-permute-start(bf16[256,256]{1,0:T(8,128)(2,1)S(1)} %get-tuple-element.111), channel_id=1, source_target_pairs={{16,32},{48,64},{80,96},{112,128},{144,160},{176,192},{208,224},{2... | collective-permute-start | bytes 393224 | tf_op jit(solution)/shard_map/ppermute | solution.py:426
  70.0 12.1 %collective-permute-start.8 = (bf16[256,256]{1,0:T(8,128)(2,1)S(1)}, bf16[256,256]{1,0:T(8,128)(2,1)S(1)}, u32[]{:S(2)}, u32[]{:S(2)}) collective-permute-start(bf16[256,256]{1,0:T(8,128)(2,1)S(1)} %get-tuple-element.112), channel_id=1, source_target_pairs={{1,2},{3,4},{5,6},{7,8},{9,10},{11,12},{13,14},{2,1},{4,3},{6,5},{... | collective-permute-start | bytes 393224 | tf_op jit(solution)/shard_map/ppermute | solution.py:426
  70.7 11.9 %collective-permute-start.9 = (bf16[256,256]{1,0:T(8,128)(2,1)S(1)}, bf16[256,256]{1,0:T(8,128)(2,1)S(1)}, u32[]{:S(2)}, u32[]{:S(2)}) collective-permute-start(bf16[256,256]{1,0:T(8,128)(2,1)S(1)} %get-tuple-element.113), channel_id=1, source_target_pairs={{0,1},{2,3},{4,5},{6,7},{8,9},{10,11},{12,13},{14,15},{1,0},{3,2},... | collective-permute-start | bytes 393224 | tf_op jit(solution)/shard_map/ppermute | solution.py:426
  77.6 5.0 %collective-permute-start.10 = (bf16[256,256]{1,0:T(8,128)(2,1)S(1)}, bf16[256,256]{1,0:T(8,128)(2,1)S(1)}, u32[]{:S(2)}, u32[]{:S(2)}) collective-permute-start(bf16[256,256]{1,0:T(8,128)(2,1)S(1)} %get-tuple-element.114), channel_id=1, source_target_pairs={{0,16},{32,48},{64,80},{96,112},{128,144},{160,176},{192,208},{224... | collective-permute-start | bytes 393224 | tf_op jit(solution)/shard_map/ppermute | solution.py:426
  79.5 0.7 copy-start.11
  80.2 4.7 %copy-start.5 = (bf16[1,1,4,2,128,128]{5,4,3,2,1,0:T(8,128)(2,1)S(1)}, bf16[1,1,4,2,128,128]{5,4,3,2,1,0:T(8,128)(2,1)}, u32[]{:S(2)}) copy-start(bf16[1,1,4,2,128,128]{5,4,3,2,1,0:T(8,128)(2,1)} %param.21) | copy-start | bytes 786436
  80.2 4.7 %copy-start.6 = (bf16[512,256]{1,0:T(8,128)(2,1)S(1)}, bf16[512,256]{1,0:T(8,128)(2,1)}, u32[]{:S(2)}) copy-start(bf16[512,256]{1,0:T(8,128)(2,1)} %get-tuple-element.101.lifted) | copy-start | bytes 786436
  80.2 4.7 %copy-start.7 = (bf16[512,256]{1,0:T(8,128)(2,1)S(1)}, bf16[512,256]{1,0:T(8,128)(2,1)}, u32[]{:S(2)}) copy-start(bf16[512,256]{1,0:T(8,128)(2,1)} %get-tuple-element.102.active) | copy-start | bytes 786436
  80.2 4.7 %copy-start.8 = (bf16[256,256]{1,0:T(8,128)(2,1)S(1)}, bf16[256,256]{1,0:T(8,128)(2,1)}, u32[]{:S(2)}) copy-start(bf16[256,256]{1,0:T(8,128)(2,1)} %edge_lift.1) | copy-start | bytes 393220
  80.2 4.7 %copy-start.9 = (bf16[256,256]{1,0:T(8,128)(2,1)S(1)}, bf16[256,256]{1,0:T(8,128)(2,1)}, u32[]{:S(2)}) copy-start(bf16[256,256]{1,0:T(8,128)(2,1)} %edge_emit.1) | copy-start | bytes 393220
  82.5 7.8 %collective-permute-start.11 = (bf16[4,224,256]{2,1,0:T(8,128)(2,1)S(1)}, bf16[4,224,256]{2,1,0:T(8,128)(2,1)S(1)}, u32[]{:S(2)}, u32[]{:S(2)}) collective-permute-start(bf16[4,224,256]{2,1,0:T(8,128)(2,1)S(1)} %get-tuple-element.124), channel_id=1, source_target_pairs={{0,16},{16,0},{1,17},{17,1},{2,18},{18,2},{3,19},{19,3},{4,20},{20... | collective-permute-start | bytes 1376264 | tf_op jit(solution)/shard_map/ppermute | solution.py:516
  84.9 0.7 copy-start.12
  87.1 3.3 %collective-permute-start.12 = (bf16[4,80,256]{2,1,0:T(8,128)(2,1)S(1)}, bf16[4,80,256]{2,1,0:T(8,128)(2,1)S(1)}, u32[]{:S(2)}, u32[]{:S(2)}) collective-permute-start(bf16[4,80,256]{2,1,0:T(8,128)(2,1)S(1)} %get-tuple-element.125), channel_id=1, source_target_pairs={{0,16},{16,0},{1,17},{17,1},{2,18},{18,2},{3,19},{19,3},{4,20},{20... | collective-permute-start | bytes 491528 | tf_op jit(solution)/shard_map/ppermute | solution.py:531
  168.4 10.9 %collective-permute-start.13 = (bf16[4,304,256]{2,1,0:T(8,128)(2,1)S(1)}, bf16[4,304,256]{2,1,0:T(8,128)(2,1)S(1)}, u32[]{:S(2)}, u32[]{:S(2)}) collective-permute-start(bf16[4,304,256]{2,1,0:T(8,128)(2,1)S(1)} %all_to_all.41.mine), channel_id=1, source_target_pairs={{0,16},{16,0},{1,17},{17,1},{2,18},{18,2},{3,19},{19,3},{4,20},{20... | collective-permute-start | bytes 1867784 | tf_op jit(solution)/shard_map/ppermute | solution.py:558

commit v5 on v4

--- a/solution.py
+++ b/solution.py
@@ -83,22 +83,20 @@
     return jax.ShapeDtypeStruct(shape, kind)
 
 
-def front_kernel(share, *refs):
-    far, refs = refs[:11], refs[11:]
-    (pool, part0, part1, part2, part3, lifted, active, local, params), refs = refs[:9], refs[9:]
-    near, (message, hot, sems) = refs[:11], refs[11:]
+def fetch(far, near, sems):
     copies = [
         pltpu.make_async_copy(*pair, sems.at[index])
         for index, pair in enumerate(zip(far, near))
     ]
     for copy in copies:
         copy.start()
-    (clus, state, edge_bias, node_bias, norm_gain, edge_lift, edge_emit, source, adjacency, cuts,
-     blocks) = near
+    return copies
+
+
+def pool_kernel(share, clus_far, state_far, pool, clus, state, hot, sems):
+    for copy in fetch((clus_far, state_far), (clus, state), sems):
+        copy.wait()
     rows, features = state.shape
-    tiles = rows // TILE
-    for copy in copies[:2]:
-        copy.wait()
     clus_row = clus[...]
     line = lax.broadcasted_iota(jnp.int32, (16, TILE), 0)
     for peer in range(pool.shape[0]):
@@ -115,8 +113,17 @@
         )
         pool[peer, share:share + 16, 0:TILE] = digits.astype(BF16)
         pool[peer, share:share + 16, TILE:] = jnp.zeros((16, features - TILE), BF16)
-    for copy in copies[2:]:
+
+
+def front_kernel(*refs):
+    far, refs = refs[:10], refs[10:]
+    (part0, part1, part2, part3, lifted, active, local, params), refs = refs[:8], refs[8:]
+    near, (message, sems) = refs[:10], refs[10:]
+    for copy in fetch(far, near, sems):
         copy.wait()
+    (state, edge_bias, node_bias, norm_gain, edge_lift, edge_emit, source, adjacency, cuts,
+     blocks) = near
+    tiles = state.shape[0] // TILE
     params[...] = jnp.zeros(params.shape, F32)
     for index, vector in enumerate((node_bias, norm_gain)):
         params[index:index + 1] = vector[...].astype(F32).reshape(1, -1)
@@ -139,7 +146,8 @@
         local[rows_of(tile)] = total
 
 
-def aggregate_kernel(target, local, arrived0, arrived1, arrived2, arrived3, aggregate, summed):
+def aggregate_kernel(target, _source, _adjacency, local, arrived0, arrived1, arrived2, arrived3,
+                     aggregate, summed):
     summed[...] = local[...]
     for slot, arrived in zip(slots("in"), (arrived0, arrived1, arrived2, arrived3)):
         for cut in range(arrived.shape[0] // TILE):
@@ -235,11 +243,12 @@
         done += count
 
 
-def part_ways(stack, keep, send):
+def part_ways(stack, keep, send, first=0):
     core = lax.axis_index("core")
     for index in range(keep.shape[0]):
-        keep[index] = stack[2 * index + core]
-        send[index] = stack[2 * index + 1 - core]
+        rows = slice(first, first + stack.shape[1])
+        keep[index, rows] = stack[2 * index + core]
+        send[index, rows] = stack[2 * index + 1 - core]
 
 
 def weight_kernel(sizes, adjacency, clus, state, upstream, aggregate, coarse, active, emit_grad,
@@ -267,7 +276,7 @@
 
 
 def edge_kernel(sizes, source, state, lifted, active, local, back0, back1, back2, back3, cuts,
-                edge_lift, edge_emit, partial, vectors,
+                edge_lift, edge_emit, partial, vectors, keep_node, send_node,
                 keep, send, partial_out, total, message_grad, lifted_grad, edge_part):
     peers, _, _, edge_rows = sizes
     features = state.shape[1]
@@ -291,13 +300,9 @@
     edge_part[0, edge_rows:] = jnp.where(
         last == 0, vectors[0:1], jnp.where(last == 1, vectors[1:2], jnp.where(last == 2, bias_grad, 0.0))
     ).astype(BF16)
-    part_ways(edge_part, keep, send)
-
-
-def merge_kernel(keep_node, keep_edge, got_node, got_edge, out):
-    rows = keep_node.shape[1]
-    out[:, 0:rows] = (keep_node[...].astype(F32) + got_node[...].astype(F32)).astype(BF16)
-    out[:, rows:] = (keep_edge[...].astype(F32) + got_edge[...].astype(F32)).astype(BF16)
+    part_ways(edge_part, keep, send, keep_node.shape[1])
+    keep[:, 0:keep_node.shape[1]] = keep_node[...]
+    send[:, 0:keep_node.shape[1]] = send_node[...]
 
 
 def split_kernel(share, received, pool, grads):
@@ -426,25 +431,36 @@
             moved.append(lax.ppermute(part, axis, pairs + [(j, i) for i, j in pairs]))
         return moved
 
-    operands = (clus, node_state, edge_bias, node_bias, norm_gain, edge_lift, edge_emit, source,
+    anywhere = pl.BlockSpec(memory_space=pl.ANY)
+    pool = call(
+        functools.partial(pool_kernel, share),
+        like((peers, share + 16, features), BF16),
+        [anywhere] * 2,
+        [
+            pltpu.VMEM((1, rows), jnp.int32),
+            pltpu.VMEM((rows, features), BF16),
+            pltpu.VMEM((peers * TILE, rows), BF16),
+            pltpu.SemaphoreType.DMA((2,)),
+        ],
+        FIRST_LIMIT,
+        out_specs=pl.BlockSpec(memory_space=pltpu.VMEM),
+        flops=2 * layer,
+        moved=1 << 20,
+    )(clus, node_state)
+    operands = (node_state, edge_bias, node_bias, norm_gain, edge_lift, edge_emit, source,
                 adjacency, cuts, edge_blocks)
     tables = (source, adjacency)
-    pool, part0, part1, part2, part3, lifted, active, local, params = call(
-        functools.partial(front_kernel, share),
-        [like((peers, share + 16, features), BF16)] + [cut_part] * 4
-        + [narrow, narrow, wide, like((8, features), F32)],
-        [pl.BlockSpec(memory_space=pl.ANY)] * len(operands),
+    part0, part1, part2, part3, lifted, active, local, params = call(
+        front_kernel,
+        [cut_part] * 4 + [narrow, narrow, wide, like((8, features), F32)],
+        [anywhere] * len(operands),
         [
             (pltpu.SMEM if any(v is table for table in tables) else pltpu.VMEM)(v.shape, v.dtype)
             for v in operands
         ]
-        + [
-            pltpu.VMEM((rows, features), BF16),
-            pltpu.VMEM((peers * TILE, rows), BF16),
-            pltpu.SemaphoreType.DMA((len(operands),)),
-        ],
+        + [pltpu.VMEM((rows, features), BF16), pltpu.SemaphoreType.DMA((len(operands),))],
         FIRST_LIMIT,
-        out_specs=vmem(9),
+        out_specs=vmem(8),
         flops=8 * layer,
         moved=4 << 20,
     )(*operands)
@@ -479,10 +495,10 @@
     aggregate = call(
         aggregate_kernel,
         narrow,
-        smem(1) + vmem(5),
+        smem(3) + vmem(5),
         [pltpu.VMEM((rows, features), F32)],
         moved=2 << 20,
-    )(target, local, *arrived)
+    )(target, source, adjacency, local, *arrived)
 
     (updated, coarse, node_active, emit_grad, lifted_grad, aggregate_grad, coarse_grad,
      back0, back1, back2, back3, vectors) = call(
@@ -512,12 +528,10 @@
     )(adjacency, clus, node_state, node_grad, aggregate, coarse, node_active, emit_grad,
       lifted_grad, aggregate_grad, coarse_grad, edge_blocks, node_lift)
     returned = swap((back0, back1, back2, back3))
-    send_node, *returned = lax.optimization_barrier((send_node, *returned))
-    got_node = lax.ppermute(send_node, "core", both_cores)
-    keep_edge, send_edge, partial = call(
+    keep, send, partial = call(
         functools.partial(edge_kernel, sizes),
-        [like((across, edge_rows + 16, features), BF16)] * 2 + [wide],
-        smem(1) + vmem(13),
+        [like((across, packed_rows, features), BF16)] * 2 + [wide],
+        smem(1) + vmem(15),
         [
             pltpu.VMEM((rows, features), F32),
             pltpu.VMEM((rows, features), BF16),
@@ -527,11 +541,9 @@
         flops=8 * layer,
         moved=5 << 20,
     )(source, node_state, lifted, active, message_local, *returned, cuts, edge_lift, edge_emit,
-      partial, vectors)
-    got_edge = lax.ppermute(send_edge, "core", both_cores)
-    merged = call(
-        merge_kernel, like((across, packed_rows, features), BF16), vmem(4), moved=2 << 20
-    )(keep_node, keep_edge, got_node, got_edge)
+      partial, vectors, keep_node, send_node)
+    got = lax.ppermute(send, "core", both_cores)
+    merged = call(add_kernel, like(keep.shape, BF16), vmem(2), moved=2 << 20)(keep, got)
     received = lax.all_to_all(merged, "y", 0, 0, tiled=True)
     pool, grads = call(
         functools.partial(split_kernel, share),

time: 182 us -> 178 us (0.978)
  blocking collectives: 104 us -> 84.9 us
  starting transfers between devices: 51 us -> 59.8 us
  waiting for transfers between devices: 9.51 us -> 16.1 us
  Pallas kernels: 12.4 us -> 14.4 us
    all_to_all x1 -> x0, blocking collectives: 19.1 us -> none  [shards(): received = lax.all_to_all(pool, near, 0, 0, tiled=True)]
    all_to_all x0 -> x1, starting transfers between devices: none -> 10.3 us  [shards(): received = lax.all_to_all(pool, near, 0, 0, tiled=True)]
    all_to_all x0 -> x1, waiting for transfers between devices: none -> 5.58 us  [shards(): received = lax.all_to_all(pool, near, 0, 0, tiled=True)]
    ppermute x2 -> x1, starting transfers between devices: 4.3 us -> 2.29 us  [shards(): got = lax.ppermute(send, 'core', both_cores)]
    pallas_call x4 -> x5, Pallas kernels: 6.12 us -> 8.1 us  [the longest x1 3.19 us: shards(): call(front_kernel, [cut_part] * 4 + [narrow, narrow, wide, like((8, featu...]
  transfers between devices with their start and end apart: 14 -> 14, of which waited for: 5 -> 6; matrix products, arithmetic and copies ran while one was open for 0% -> 0% of each run, Pallas kernels for 2% -> 3%
where the time goes in v5:
time: 178 us; the launch traced here: 177 us
  blocking collectives  84.9 us (48%)
  starting transfers between devices  59.8 us (34%)
  waiting for transfers between devices  16.1 us (9%)
  Pallas kernels  14.4 us (8%)
    all_to_all x1, blocking collectives, shards(): received = lax.all_to_all(joined, 'far', 0, 0, tiled=True)  23.4 us
    ppermute x8, starting transfers between devices, swap(): moved.append(lax.ppermute(part, axis, pairs + [(j, i) for i, j in pairs]))  20 us
    all_to_all x1, blocking collectives, shards(): received = lax.all_to_all(merged, 'y', 0, 0, tiled=True)  18.7 us
    all_to_all x1, blocking collectives, shards(): received = lax.all_to_all(grads, 'gy', 0, 0, tiled=True)  15.4 us
    all_to_all x1, starting transfers between devices, shards(): received = lax.all_to_all(pool, near, 0, 0, tiled=True)  10.3 us
    all_to_all x1, blocking collectives, shards(): mine = lax.all_to_all(spread, 'y', 0, 0, tiled=True)  9.85 us
    all_to_all x1, blocking collectives, shards(): grads = lax.all_to_all(grads, 'gy', 0, 0, tiled=True)  9.83 us
    ppermute x1, starting transfers between devices, shards(): other = lax.ppermute(mine, 'core', both_cores)  9.52 us
  transfers between devices with their start and end apart: 14, of which 6 were waited for; matrix products, arithmetic and copies ran while one was open for 0% of the time, Pallas kernels for 3%

profile of v5, /device:TPU:1, one launch (start us, length us, event | category | flops | bytes accessed | tf_op | source)
XLA Modules:
  0.0 177.2 jit_solution(1886114875768182792)
XLA Ops:
  0.6 2.4 %shard_map.215 = bf16[8,112,256]{2,1,0:T(8,128)(2,1)} custom-call(s32[1,512]{1,0:T(1,128)} %bitcast.13, bf16[512,256]{1,0:T(8,128)(2,1)} %state.5), custom_call_target="tpu_custom_call" | custom-call | flops 134217728 | bytes 1048576 | tf_op jit(solution)/shard_map/pallas_call | solution.py:435
  3.1 10.3 %all-to-all-start = ((bf16[8,112,256]{2,1,0:T(8,128)(2,1)}), bf16[8,112,256]{2,1,0:T(8,128)(2,1)S(1)}, u32[]{:S(2)}, u32[]{:S(2)}) async-start(bf16[8,112,256]{2,1,0:T(8,128)(2,1)} %shard_map.215), calls=%async_computation | async-start | bytes 917504 | tf_op jit(solution)/shard_map/all_to_all | solution.py:467
  13.4 3.2 %shard_map.214 = (bf16[256,256]{1,0:T(8,128)(2,1)}, bf16[256,256]{1,0:T(8,128)(2,1)}, bf16[256,256]{1,0:T(8,128)(2,1)}, bf16[256,256]{1,0:T(8,128)(2,1)}, bf16[5...) custom-call(bf16[512,256]{1,0:T(8,128)(2,1)} %state.5, ...), custom_call_target="tpu_custom_call" | custom-call | flops 536870912 | bytes 4194304 | tf_op jit(solution)/shard_map/pallas_call | solution.py:453
  16.6 0.0 copy-start.1
  16.6 5.6 %all-to-all-done.received = bf16[8,112,256]{2,1,0:T(8,128)(2,1)S(1)} async-done(((bf16[8,112,256]{2,1,0:T(8,128)(2,1)}), bf16[8,112,256]{2,1,0:T(8,128)(2,1)S(1)}, u32[]{:S(2)}, u32[]{:S(2)}) %all-to-all-start) | async-done | bytes 458784 | tf_op jit(solution)/shard_map/all_to_all | solution.py:467
  22.2 0.1 shard_map.216.mine
  22.2 0.0 copy-start.16
  22.2 4.6 %collective-permute-start = (bf16[112,256]{1,0:T(8,128)(2,1)S(1)}, bf16[112,256]{1,0:T(8,128)(2,1)S(1)}, u32[]{:S(2)}, u32[]{:S(2)}) collective-permute-start(bf16[112,256]{1,0:T(8,128)(2,1)S(1)} %shard_map.216.mine), channel_id=1, source_target_pairs={{0,128},{128,0},{256,384},{384,256},{1,129},{129,1},{257,385},{385... | collective-permute-start | bytes 172040 | tf_op jit(solution)/shard_map/ppermute | solution.py:477
  26.9 3.2 %collective-permute-start.2 = (bf16[256,256]{1,0:T(8,128)(2,1)}, bf16[256,256]{1,0:T(8,128)(2,1)S(1)}, u32[]{:S(2)}, u32[]{:S(2)}) collective-permute-start(bf16[256,256]{1,0:T(8,128)(2,1)} %get-tuple-element.75), channel_id=1, source_target_pairs={{16,32},{48,64},{80,96},{112,128},{144,160},{176,192},{208,224},{2... | collective-permute-start | bytes 393224 | tf_op jit(solution)/shard_map/ppermute | solution.py:431
  30.1 0.7 collective-permute-start.3
  30.8 3.9 %collective-permute-done.other = bf16[112,256]{1,0:T(8,128)(2,1)S(1)} collective-permute-done((bf16[112,256]{1,0:T(8,128)(2,1)S(1)}, bf16[112,256]{1,0:T(8,128)(2,1)S(1)}, u32[]{:S(2)}, u32[]{:S(2)}) %collective-permute-start) | collective-permute-done | bytes 57376 | tf_op jit(solution)/shard_map/ppermute | solution.py:477
  34.7 2.5 %collective-permute-start.4 = (bf16[256,256]{1,0:T(8,128)(2,1)}, bf16[256,256]{1,0:T(8,128)(2,1)S(1)}, u32[]{:S(2)}, u32[]{:S(2)}) collective-permute-start(bf16[256,256]{1,0:T(8,128)(2,1)} %get-tuple-element.77), channel_id=1, source_target_pairs={{0,1},{2,3},{4,5},{6,7},{8,9},{10,11},{12,13},{14,15},{1,0},{3,2},... | collective-permute-start | bytes 393224 | tf_op jit(solution)/shard_map/ppermute | solution.py:431
  37.3 0.0 copy-done.16
  37.3 1.9 %collective-permute-start.5 = (bf16[256,256]{1,0:T(8,128)(2,1)S(1)}, bf16[256,256]{1,0:T(8,128)(2,1)S(1)}, u32[]{:S(2)}, u32[]{:S(2)}) collective-permute-start(bf16[256,256]{1,0:T(8,128)(2,1)S(1)} %copy-done.16), channel_id=1, source_target_pairs={{0,16},{32,48},{64,80},{96,112},{128,144},{160,176},{192,208},{224... | collective-permute-start | bytes 393224 | tf_op jit(solution)/shard_map/ppermute | solution.py:431
  39.2 9.3 %collective-permute-start.1 = (bf16[112,256]{1,0:T(8,128)(2,1)S(1)}, bf16[112,256]{1,0:T(8,128)(2,1)S(1)}, u32[]{:S(2)}, u32[]{:S(2)}) collective-permute-start(bf16[112,256]{1,0:T(8,128)(2,1)S(1)} %shard_map.217.mine), channel_id=1, source_target_pairs={{0,384},{128,256},{256,128},{384,0},{1,385},{129,257},{257,129},{3... | collective-permute-start | bytes 172040 | tf_op jit(solution)/shard_map/ppermute | solution.py:482
  48.6 2.3 %collective-permute-done.1.other = bf16[112,256]{1,0:T(8,128)(2,1)S(1)} collective-permute-done((bf16[112,256]{1,0:T(8,128)(2,1)S(1)}, bf16[112,256]{1,0:T(8,128)(2,1)S(1)}, u32[]{:S(2)}, u32[]{:S(2)}) %collective-permute-start.1) | collective-permute-done | bytes 57376 | tf_op jit(solution)/shard_map/ppermute | solution.py:482
  50.8 0.0 collective-permute-done.2.arrived0
  50.8 0.0 collective-permute-done.3.arrived1
  50.8 0.0 collective-permute-done.4.arrived2
  50.8 0.0 collective-permute-done.5.arrived3
  50.8 0.1 shard_map.218
  51.0 0.0 copy-start.13
  51.0 7.7 %all_to_all.35.mine = bf16[4,96,256]{2,1,0:T(8,128)(2,1)S(1)} all-to-all(bf16[4,96,256]{2,1,0:T(8,128)(2,1)S(1)} %get-tuple-element.81), channel_id=1, replica_groups=mesh['far'=4,'y'=4,'core'=2,'gy'=16] {'y'}, dimensions={0} | all-to-all | bytes 393216 | tf_op jit(solution)/shard_map/all_to_all | solution.py:492
  58.6 3.7 %collective-permute-start.6 = (bf16[4,96,256]{2,1,0:T(8,128)(2,1)S(1)}, bf16[4,96,256]{2,1,0:T(8,128)(2,1)S(1)}, u32[]{:S(2)}, u32[]{:S(2)}) collective-permute-start(bf16[4,96,256]{2,1,0:T(8,128)(2,1)S(1)} %all_to_all.35.mine), channel_id=1, source_target_pairs={{0,16},{16,0},{1,17},{17,1},{2,18},{18,2},{3,19},{19,3},{4,20},{20... | collective-permute-start | bytes 589832 | tf_op jit(solution)/shard_map/ppermute | solution.py:493
  62.3 0.0 copy-start.12
  62.4 0.0 copy-done.1
  62.4 0.6 copy-done.12
  63.0 0.0 copy-start.14
  63.1 0.8 shard_map.219.aggregate
  63.8 0.0 collective-permute-done.6.other
  63.8 0.1 copy-done
  64.0 0.1 copy-done.3
  64.1 0.1 copy-done.4
  64.2 0.0 copy-done.14
  64.2 2.4 %shard_map.220 = (bf16[512,256]{1,0:T(8,128)(2,1)}, bf16[512,256]{1,0:T(8,128)(2,1)S(1)}, bf16[512,256]{1,0:T(8,128)(2,1)S(1)}, bf16[512,256]{1,0:T(8,128)(2,1)S...) custom-call(s32[2,4]{1,0:T(2,128)S(1)} %bitcast.21, ...), custom_call_target="tpu_custom_call" | custom-call | flops 671088640 | bytes 4194304 | tf_op jit(solution)/shard_map/pallas_call | solution.py:504
  66.7 2.1 %collective-permute-start.7 = (bf16[256,256]{1,0:T(8,128)(2,1)S(1)}, bf16[256,256]{1,0:T(8,128)(2,1)S(1)}, u32[]{:S(2)}, u32[]{:S(2)}) collective-permute-start(bf16[256,256]{1,0:T(8,128)(2,1)S(1)} %get-tuple-element.103), channel_id=1, source_target_pairs={{16,32},{48,64},{80,96},{112,128},{144,160},{176,192},{208,224},{2... | collective-permute-start | bytes 393224 | tf_op jit(solution)/shard_map/ppermute | solution.py:431
  68.7 0.7 collective-permute-start.8
  69.4 6.9 %collective-permute-start.9 = (bf16[256,256]{1,0:T(8,128)(2,1)S(1)}, bf16[256,256]{1,0:T(8,128)(2,1)S(1)}, u32[]{:S(2)}, u32[]{:S(2)}) collective-permute-start(bf16[256,256]{1,0:T(8,128)(2,1)S(1)} %get-tuple-element.105), channel_id=1, source_target_pairs={{0,1},{2,3},{4,5},{6,7},{8,9},{10,11},{12,13},{14,15},{1,0},{3,2},... | collective-permute-start | bytes 393224 | tf_op jit(solution)/shard_map/ppermute | solution.py:431
  76.4 1.9 %collective-permute-start.10 = (bf16[256,256]{1,0:T(8,128)(2,1)S(1)}, bf16[256,256]{1,0:T(8,128)(2,1)S(1)}, u32[]{:S(2)}, u32[]{:S(2)}) collective-permute-start(bf16[256,256]{1,0:T(8,128)(2,1)S(1)} %get-tuple-element.106), channel_id=1, source_target_pairs={{0,16},{32,48},{64,80},{96,112},{128,144},{160,176},{192,208},{224... | collective-permute-start | bytes 393224 | tf_op jit(solution)/shard_map/ppermute | solution.py:431
  78.3 0.0 copy-done.2
  78.3 0.0 copy-start.5
  78.3 0.0 copy-start.6
  78.3 0.0 copy-start.7
  78.4 0.0 copy-start.8
  78.4 0.0 copy-start.9
  78.4 1.9 %shard_map.221 = (bf16[4,224,256]{2,1,0:T(8,128)(2,1)S(1)}, bf16[4,224,256]{2,1,0:T(8,128)(2,1)S(1)}, f32[512,256]{1,0:T(8,128)S(1)}, f32[512,256]{1,0:T(8,128)S(1)}) custom-call(s32[4,3]{1,0:T(4,128)S(1)} %copy-done.11, s32[1,512]{1,0:T(1,128)S(1)} %bitcast.15, bf16[512,256]{1,0:T(8,128)(2,1)S(1)} %copy-done, bf16[512,256]{1,0:T(8,128)(2,1)S(1)} %copy-done.4, ...), custom_call_target="tpu_custom_call" | custom-call | flops 536870912 | bytes 5242880 | tf_op jit(solution)/shard_map/pallas_call | solution.py:518
  80.2 0.0 collective-permute-done.7.back0
  80.2 0.0 collective-permute-done.8.back1
  80.3 1.0 collective-permute-done.9.back2
  81.2 0.0 collective-permute-done.10.back3
  81.3 0.0 copy-done.6
  81.3 1.6 shard_map.222
  82.8 2.3 %collective-permute-start.11 = (bf16[4,304,256]{2,1,0:T(8,128)(2,1)S(1)}, bf16[4,304,256]{2,1,0:T(8,128)(2,1)S(1)}, u32[]{:S(2)}, u32[]{:S(2)}) collective-permute-start(bf16[4,304,256]{2,1,0:T(8,128)(2,1)S(1)} %get-tuple-element.113), channel_id=1, source_target_pairs={{0,16},{16,0},{1,17},{17,1},{2,18},{18,2},{3,19},{19,3},{4,20},{20... | collective-permute-start | bytes 1867784 | tf_op jit(solution)/shard_map/ppermute | solution.py:545
  85.1 1.7 collective-permute-done.11.other
  86.8 0.1 shard_map.223
  86.9 18.7 %all_to_all.36.received = bf16[4,304,256]{2,1,0:T(8,128)(2,1)S(1)} all-to-all(bf16[4,304,256]{2,1,0:T(8,128)(2,1)S(1)} %shard_map.223), channel_id=1, replica_groups=mesh['far'=4,'y'=4,'core'=2,'gy'=16] {'y'}, dimensions={0} | all-to-all | bytes 1245184 | tf_op jit(solution)/shard_map/all_to_all | solution.py:547
  105.6 0.1 shard_map.224
  105.7 15.4 %all_to_all.37.received = bf16[16,16,256]{2,1,0:T(8,128)(2,1)S(1)} all-to-all(bf16[16,16,256]{2,1,0:T(8,128)(2,1)S(1)} %get-tuple-element.115), channel_id=1, replica_groups=mesh['far'=4,'y'=4,'core'=2,'gy'=16] {'gy'}, dimensions={0} | all-to-all | bytes 262144 | tf_op jit(solution)/shard_map/all_to_all | solution.py:554
  121.1 23.4 %all_to_all.38.received = bf16[4,112,256]{2,1,0:T(8,128)(2,1)S(1)} all-to-all(bf16[4,112,256]{2,1,0:T(8,128)(2,1)S(1)} %shard_map.225), channel_id=1, replica_groups=mesh['far'=4,'y'=4,'core'=2,'gy'=16] {'far'}, dimensions={0} | all-to-all | bytes 458752 | tf_op jit(solution)/shard_map/all_to_all | solution.py:558
  144.6 9.8 %all_to_all.39.grads = bf16[16,16,256]{2,1,0:T(8,128)(2,1)S(1)} all-to-all(bf16[16,16,256]{2,1,0:T(8,128)(2,1)S(1)} %get-tuple-element.118), channel_id=1, replica_groups=mesh['far'=4,'y'=4,'core'=2,'gy'=16] {'gy'}, dimensions={0} | all-to-all | bytes 262144 | tf_op jit(solution)/shard_map/all_to_all | solution.py:565
  154.5 9.9 %all_to_all.40.mine = bf16[4,304,256]{2,1,0:T(8,128)(2,1)S(1)} all-to-all(bf16[4,304,256]{2,1,0:T(8,128)(2,1)S(1)} %shard_map.227), channel_id=1, replica_groups=mesh['far'=4,'y'=4,'core'=2,'gy'=16] {'y'}, dimensions={0} | all-to-all | bytes 1245184 | tf_op jit(solution)/shard_map/all_to_all | solution.py:569
  164.4 9.5 %collective-permute-start.12 = (bf16[4,304,256]{2,1,0:T(8,128)(2,1)S(1)}, bf16[4,304,256]{2,1,0:T(8,128)(2,1)S(1)}, u32[]{:S(2)}, u32[]{:S(2)}) collective-permute-start(bf16[4,304,256]{2,1,0:T(8,128)(2,1)S(1)} %all_to_all.40.mine), channel_id=1, source_target_pairs={{0,16},{16,0},{1,17},{17,1},{2,18},{18,2},{3,19},{19,3},{4,20},{20... | collective-permute-start | bytes 1867784 | tf_op jit(solution)/shard_map/ppermute | solution.py:570
  173.9 1.7 collective-permute-done.12.other
  175.5 1.6 shard_map.228
  (19 shorter events, 0.2 us)
Async XLA Ops:
  3.1 19.1 %all-to-all-start = ((bf16[8,112,256]{2,1,0:T(8,128)(2,1)}), bf16[8,112,256]{2,1,0:T(8,128)(2,1)S(1)}, u32[]{:S(2)}, u32[]{:S(2)}) async-start(bf16[8,112,256]{2,1,0:T(8,128)(2,1)} %shard_map.215), calls=%async_computation | async-start | bytes 917504 | tf_op jit(solution)/shard_map/all_to_all | solution.py:467
  16.6 45.8 %copy-start.1 = (f32[512,256]{1,0:T(8,128)S(1)}, f32[512,256]{1,0:T(8,128)}, u32[]{:S(2)}) copy-start(f32[512,256]{1,0:T(8,128)} %get-tuple-element.86.local) | copy-start | bytes 1572868
  22.2 15.0 %copy-start.16 = (bf16[256,256]{1,0:T(8,128)(2,1)S(1)}, bf16[256,256]{1,0:T(8,128)(2,1)}, u32[]{:S(2)}) copy-start(bf16[256,256]{1,0:T(8,128)(2,1)} %get-tuple-element.78) | copy-start | bytes 393220
  22.2 12.5 %collective-permute-start = (bf16[112,256]{1,0:T(8,128)(2,1)S(1)}, bf16[112,256]{1,0:T(8,128)(2,1)S(1)}, u32[]{:S(2)}, u32[]{:S(2)}) collective-permute-start(bf16[112,256]{1,0:T(8,128)(2,1)S(1)} %shard_map.216.mine), channel_id=1, source_target_pairs={{0,128},{128,0},{256,384},{384,256},{1,129},{129,1},{257,385},{385... | collective-permute-start | bytes 172040 | tf_op jit(solution)/shard_map/ppermute | solution.py:477
  26.9 23.9 %collective-permute-start.2 = (bf16[256,256]{1,0:T(8,128)(2,1)}, bf16[256,256]{1,0:T(8,128)(2,1)S(1)}, u32[]{:S(2)}, u32[]{:S(2)}) collective-permute-start(bf16[256,256]{1,0:T(8,128)(2,1)} %get-tuple-element.75), channel_id=1, source_target_pairs={{16,32},{48,64},{80,96},{112,128},{144,160},{176,192},{208,224},{2... | collective-permute-start | bytes 393224 | tf_op jit(solution)/shard_map/ppermute | solution.py:431
  30.1 20.7 %collective-permute-start.3 = (bf16[256,256]{1,0:T(8,128)(2,1)}, bf16[256,256]{1,0:T(8,128)(2,1)S(1)}, u32[]{:S(2)}, u32[]{:S(2)}) collective-permute-start(bf16[256,256]{1,0:T(8,128)(2,1)} %get-tuple-element.76), channel_id=1, source_target_pairs={{1,2},{3,4},{5,6},{7,8},{9,10},{11,12},{13,14},{2,1},{4,3},{6,5},{... | collective-permute-start | bytes 393224 | tf_op jit(solution)/shard_map/ppermute | solution.py:431
  34.7 16.1 %collective-permute-start.4 = (bf16[256,256]{1,0:T(8,128)(2,1)}, bf16[256,256]{1,0:T(8,128)(2,1)S(1)}, u32[]{:S(2)}, u32[]{:S(2)}) collective-permute-start(bf16[256,256]{1,0:T(8,128)(2,1)} %get-tuple-element.77), channel_id=1, source_target_pairs={{0,1},{2,3},{4,5},{6,7},{8,9},{10,11},{12,13},{14,15},{1,0},{3,2},... | collective-permute-start | bytes 393224 | tf_op jit(solution)/shard_map/ppermute | solution.py:431
  37.3 13.6 %collective-permute-start.5 = (bf16[256,256]{1,0:T(8,128)(2,1)S(1)}, bf16[256,256]{1,0:T(8,128)(2,1)S(1)}, u32[]{:S(2)}, u32[]{:S(2)}) collective-permute-start(bf16[256,256]{1,0:T(8,128)(2,1)S(1)} %copy-done.16), channel_id=1, source_target_pairs={{0,16},{32,48},{64,80},{96,112},{128,144},{160,176},{192,208},{224... | collective-permute-start | bytes 393224 | tf_op jit(solution)/shard_map/ppermute | solution.py:431
  39.2 11.6 %collective-permute-start.1 = (bf16[112,256]{1,0:T(8,128)(2,1)S(1)}, bf16[112,256]{1,0:T(8,128)(2,1)S(1)}, u32[]{:S(2)}, u32[]{:S(2)}) collective-permute-start(bf16[112,256]{1,0:T(8,128)(2,1)S(1)} %shard_map.217.mine), channel_id=1, source_target_pairs={{0,384},{128,256},{256,128},{384,0},{1,385},{129,257},{257,129},{3... | collective-permute-start | bytes 172040 | tf_op jit(solution)/shard_map/ppermute | solution.py:482
  51.0 11.4 %copy-start.13 = (s32[1,1,4,2]{2,3,1,0:T(2,128)S(1)}, s32[1,1,4,2]{2,3,1,0:T(2,128)}, u32[]{:S(2)}) copy-start(s32[1,1,4,2]{2,3,1,0:T(2,128)} %param.20) | copy-start | bytes 100
  58.6 3.8 %copy-start.11 = (s32[4,3]{1,0:T(4,128)S(1)}, s32[4,3]{1,0:T(4,128)}, u32[]{:S(2)}) copy-start(s32[4,3]{1,0:T(4,128)} %adjacency.1) | copy-start | bytes 148
  58.6 5.2 %collective-permute-start.6 = (bf16[4,96,256]{2,1,0:T(8,128)(2,1)S(1)}, bf16[4,96,256]{2,1,0:T(8,128)(2,1)S(1)}, u32[]{:S(2)}, u32[]{:S(2)}) collective-permute-start(bf16[4,96,256]{2,1,0:T(8,128)(2,1)S(1)} %all_to_all.35.mine), channel_id=1, source_target_pairs={{0,16},{16,0},{1,17},{17,1},{2,18},{18,2},{3,19},{19,3},{4,20},{20... | collective-permute-start | bytes 589832 | tf_op jit(solution)/shard_map/ppermute | solution.py:493
  62.3 0.7 copy-start.12
  63.0 0.9 copy-start
  63.0 1.1 copy-start.3
  63.0 1.1 copy-start.4
  63.0 1.1 copy-start.10
  63.0 1.2 copy-start.14
  63.1 1.2 copy-start.15
  64.2 14.1 %copy-start.2 = (bf16[4,3,128,128]{3,2,1,0:T(8,128)(2,1)S(1)}, bf16[4,3,128,128]{3,2,1,0:T(8,128)(2,1)}, u32[]{:S(2)}) copy-start(bf16[4,3,128,128]{3,2,1,0:T(8,128)(2,1)} %blocks.1) | copy-start | bytes 1179652
  66.7 13.6 %collective-permute-start.7 = (bf16[256,256]{1,0:T(8,128)(2,1)S(1)}, bf16[256,256]{1,0:T(8,128)(2,1)S(1)}, u32[]{:S(2)}, u32[]{:S(2)}) collective-permute-start(bf16[256,256]{1,0:T(8,128)(2,1)S(1)} %get-tuple-element.103), channel_id=1, source_target_pairs={{16,32},{48,64},{80,96},{112,128},{144,160},{176,192},{208,224},{2... | collective-permute-start | bytes 393224 | tf_op jit(solution)/shard_map/ppermute | solution.py:431
  68.7 11.5 %collective-permute-start.8 = (bf16[256,256]{1,0:T(8,128)(2,1)S(1)}, bf16[256,256]{1,0:T(8,128)(2,1)S(1)}, u32[]{:S(2)}, u32[]{:S(2)}) collective-permute-start(bf16[256,256]{1,0:T(8,128)(2,1)S(1)} %get-tuple-element.104), channel_id=1, source_target_pairs={{1,2},{3,4},{5,6},{7,8},{9,10},{11,12},{13,14},{2,1},{4,3},{6,5},{... | collective-permute-start | bytes 393224 | tf_op jit(solution)/shard_map/ppermute | solution.py:431
  69.4 11.8 %collective-permute-start.9 = (bf16[256,256]{1,0:T(8,128)(2,1)S(1)}, bf16[256,256]{1,0:T(8,128)(2,1)S(1)}, u32[]{:S(2)}, u32[]{:S(2)}) collective-permute-start(bf16[256,256]{1,0:T(8,128)(2,1)S(1)} %get-tuple-element.105), channel_id=1, source_target_pairs={{0,1},{2,3},{4,5},{6,7},{8,9},{10,11},{12,13},{14,15},{1,0},{3,2},... | collective-permute-start | bytes 393224 | tf_op jit(solution)/shard_map/ppermute | solution.py:431
  76.4 4.9 %collective-permute-start.10 = (bf16[256,256]{1,0:T(8,128)(2,1)S(1)}, bf16[256,256]{1,0:T(8,128)(2,1)S(1)}, u32[]{:S(2)}, u32[]{:S(2)}) collective-permute-start(bf16[256,256]{1,0:T(8,128)(2,1)S(1)} %get-tuple-element.106), channel_id=1, source_target_pairs={{0,16},{32,48},{64,80},{96,112},{128,144},{160,176},{192,208},{224... | collective-permute-start | bytes 393224 | tf_op jit(solution)/shard_map/ppermute | solution.py:431
  78.3 2.9 %copy-start.5 = (bf16[1,1,4,2,128,128]{5,4,3,2,1,0:T(8,128)(2,1)S(1)}, bf16[1,1,4,2,128,128]{5,4,3,2,1,0:T(8,128)(2,1)}, u32[]{:S(2)}) copy-start(bf16[1,1,4,2,128,128]{5,4,3,2,1,0:T(8,128)(2,1)} %param.21) | copy-start | bytes 786436
  78.3 2.9 %copy-start.6 = (bf16[512,256]{1,0:T(8,128)(2,1)S(1)}, bf16[512,256]{1,0:T(8,128)(2,1)}, u32[]{:S(2)}) copy-start(bf16[512,256]{1,0:T(8,128)(2,1)} %get-tuple-element.94.lifted) | copy-start | bytes 786436
  78.3 2.9 %copy-start.7 = (bf16[512,256]{1,0:T(8,128)(2,1)S(1)}, bf16[512,256]{1,0:T(8,128)(2,1)}, u32[]{:S(2)}) copy-start(bf16[512,256]{1,0:T(8,128)(2,1)} %get-tuple-element.95.active) | copy-start | bytes 786436
  78.4 2.9 %copy-start.8 = (bf16[256,256]{1,0:T(8,128)(2,1)S(1)}, bf16[256,256]{1,0:T(8,128)(2,1)}, u32[]{:S(2)}) copy-start(bf16[256,256]{1,0:T(8,128)(2,1)} %edge_lift.1) | copy-start | bytes 393220
  78.4 2.9 %copy-start.9 = (bf16[256,256]{1,0:T(8,128)(2,1)S(1)}, bf16[256,256]{1,0:T(8,128)(2,1)}, u32[]{:S(2)}) copy-start(bf16[256,256]{1,0:T(8,128)(2,1)} %edge_emit.1) | copy-start | bytes 393220
  82.8 4.0 %collective-permute-start.11 = (bf16[4,304,256]{2,1,0:T(8,128)(2,1)S(1)}, bf16[4,304,256]{2,1,0:T(8,128)(2,1)S(1)}, u32[]{:S(2)}, u32[]{:S(2)}) collective-permute-start(bf16[4,304,256]{2,1,0:T(8,128)(2,1)S(1)} %get-tuple-element.113), channel_id=1, source_target_pairs={{0,16},{16,0},{1,17},{17,1},{2,18},{18,2},{3,19},{19,3},{4,20},{20... | collective-permute-start | bytes 1867784 | tf_op jit(solution)/shard_map/ppermute | solution.py:545
  164.4 11.2 %collective-permute-start.12 = (bf16[4,304,256]{2,1,0:T(8,128)(2,1)S(1)}, bf16[4,304,256]{2,1,0:T(8,128)(2,1)S(1)}, u32[]{:S(2)}, u32[]{:S(2)}) collective-permute-start(bf16[4,304,256]{2,1,0:T(8,128)(2,1)S(1)} %all_to_all.40.mine), channel_id=1, source_target_pairs={{0,16},{16,0},{1,17},{17,1},{2,18},{18,2},{3,19},{19,3},{4,20},{20... | collective-permute-start | bytes 1867784 | tf_op jit(solution)/shard_map/ppermute | solution.py:570

commit v6 on v5

--- a/solution.py
+++ b/solution.py
@@ -346,8 +346,22 @@
             out[peer, share + first:share + first + count] = grads[first // chunk, 0:count]
 
 
-def last_kernel(sizes, scale, clus, partial, mine, other, state_grad, edge_lift, edge_bias,
-                edge_emit, node_lift, node_bias, node_emit, norm_gain, means, hot):
+def pooled_kernel(share, clus, partial, mine, hot, out, means):
+    core = lax.axis_index("core")
+    peers = means.shape[0] // share
+    for peer in range(peers):
+        chunk = mine[peer // 2, 0:share]
+        means[peer * share:(peer + 1) * share] = jnp.where(
+            core == peer % 2, chunk, jnp.zeros_like(chunk)
+        )
+    for tile in range(partial.shape[0] // TILE):
+        rows = rows_of(tile)
+        hot[rows] = hot_columns(clus[0:1, rows], peers * share)
+    out[...] = partial[...] + mm(hot[...], means[...])
+
+
+def last_kernel(sizes, scale, hot, partial, mine, other, state_grad, edge_lift, edge_bias,
+                edge_emit, node_lift, node_bias, node_emit, norm_gain, means):
     peers, share, node_rows, edge_rows = sizes
     features = partial.shape[1]
     core = lax.axis_index("core")
@@ -357,10 +371,10 @@
         return jnp.where(core == peer % 2, mine[peer // 2, rows], other[peer // 2, rows])
 
     for peer in range(peers):
-        means[peer * share:(peer + 1) * share] = gathered(peer, 0, share)
-    for tile in range(partial.shape[0] // TILE):
-        rows = rows_of(tile)
-        hot[rows] = hot_columns(clus[0:1, rows], peers * share)
+        chunk = other[peer // 2, 0:share]
+        means[peer * share:(peer + 1) * share] = jnp.where(
+            core == peer % 2, jnp.zeros_like(chunk), chunk
+        )
     state_grad[...] = (partial[...] + mm(hot[...], means[...])).astype(BF16)
 
     def take(first, size, outs):
@@ -491,7 +505,6 @@
     )(summed, other)
     my_means = lax.all_to_all(means, "y", 0, 0, tiled=True)
     other_means = lax.ppermute(my_means, "core", both_cores)
-    local, my_means, *arrived = lax.optimization_barrier((local, my_means, *arrived))
     aggregate = call(
         aggregate_kernel,
         narrow,
@@ -568,6 +581,14 @@
     )(means, grads)
     mine = lax.all_to_all(spread, "y", 0, 0, tiled=True)
     other = lax.ppermute(mine, "core", both_cores)
+    hot, partial = call(
+        functools.partial(pooled_kernel, share),
+        [like((rows, peers * share), BF16), wide],
+        vmem(3),
+        [pltpu.VMEM((peers * share, features), BF16)],
+        flops=3 * layer,
+        moved=4 << 20,
+    )(clus, partial, mine)
     scale = float(rows * along * columns) ** (-0.5)
     square, line = like((features, features), F32), like((1, features), F32)
     (state_grad, edge_lift_grad, edge_bias_grad, edge_emit_grad, node_lift_grad, node_bias_grad,
@@ -575,10 +596,10 @@
         functools.partial(last_kernel, sizes, scale),
         [narrow, square, line, square, like((3 * features, features), F32), line, square, line],
         vmem(4),
-        [pltpu.VMEM((peers * share, features), BF16), pltpu.VMEM((rows, peers * share), BF16)],
+        [pltpu.VMEM((peers * share, features), BF16)],
         flops=3 * layer,
         moved=4 << 20,
-    )(clus, partial, mine, other)
+    )(hot, partial, mine, other)
     return (
         updated,
         state_grad,

time: 178 us -> 178 us (level)
  transfers between devices with their start and end apart: 14 -> 14, of which waited for: 6 -> 6; matrix products, arithmetic and copies ran while one was open for 0% -> 0% of each run, Pallas kernels for 3% -> 4%
where the time goes in v6:
time: 178 us; the launch traced here: 177 us
  blocking collectives  84.9 us (48%)
  starting transfers between devices  59.8 us (34%)
  waiting for transfers between devices  15.6 us (9%)
  Pallas kernels  14.8 us (8%)
    all_to_all x1, blocking collectives, shards(): received = lax.all_to_all(joined, 'far', 0, 0, tiled=True)  23.4 us
    ppermute x8, starting transfers between devices, swap(): moved.append(lax.ppermute(part, axis, pairs + [(j, i) for i, j in pairs]))  20 us
    all_to_all x1, blocking collectives, shards(): received = lax.all_to_all(merged, 'y', 0, 0, tiled=True)  18.7 us
    all_to_all x1, blocking collectives, shards(): received = lax.all_to_all(grads, 'gy', 0, 0, tiled=True)  15.4 us
    all_to_all x1, starting transfers between devices, shards(): received = lax.all_to_all(pool, near, 0, 0, tiled=True)  10.3 us
    all_to_all x1, blocking collectives, shards(): mine = lax.all_to_all(spread, 'y', 0, 0, tiled=True)  9.85 us
    all_to_all x1, blocking collectives, shards(): grads = lax.all_to_all(grads, 'gy', 0, 0, tiled=True)  9.83 us
    ppermute x1, starting transfers between devices, shards(): other = lax.ppermute(mine, 'core', both_cores)  9.52 us
  transfers between devices with their start and end apart: 14, of which 6 were waited for; matrix products, arithmetic and copies ran while one was open for 0% of the time, Pallas kernels for 4%

profile of v6, /device:TPU:1, one launch (start us, length us, event | category | flops | bytes accessed | tf_op | source)
XLA Modules:
  0.0 177.1 jit_solution(16027722310277524287)
XLA Ops:
  0.6 2.5 %shard_map.215 = bf16[8,112,256]{2,1,0:T(8,128)(2,1)} custom-call(s32[1,512]{1,0:T(1,128)} %bitcast.13, bf16[512,256]{1,0:T(8,128)(2,1)} %state.5), custom_call_target="tpu_custom_call" | custom-call | flops 134217728 | bytes 1048576 | tf_op jit(solution)/shard_map/pallas_call | solution.py:449
  3.1 10.3 %all-to-all-start = ((bf16[8,112,256]{2,1,0:T(8,128)(2,1)}), bf16[8,112,256]{2,1,0:T(8,128)(2,1)S(1)}, u32[]{:S(2)}, u32[]{:S(2)}) async-start(bf16[8,112,256]{2,1,0:T(8,128)(2,1)} %shard_map.215), calls=%async_computation | async-start | bytes 917504 | tf_op jit(solution)/shard_map/all_to_all | solution.py:481
  13.4 3.2 %shard_map.214 = (bf16[256,256]{1,0:T(8,128)(2,1)}, bf16[256,256]{1,0:T(8,128)(2,1)}, bf16[256,256]{1,0:T(8,128)(2,1)}, bf16[256,256]{1,0:T(8,128)(2,1)}, bf16[5...) custom-call(bf16[512,256]{1,0:T(8,128)(2,1)} %state.5, ...), custom_call_target="tpu_custom_call" | custom-call | flops 536870912 | bytes 4194304 | tf_op jit(solution)/shard_map/pallas_call | solution.py:467
  16.6 0.0 copy-start.1
  16.6 5.6 %all-to-all-done.received = bf16[8,112,256]{2,1,0:T(8,128)(2,1)S(1)} async-done(((bf16[8,112,256]{2,1,0:T(8,128)(2,1)}), bf16[8,112,256]{2,1,0:T(8,128)(2,1)S(1)}, u32[]{:S(2)}, u32[]{:S(2)}) %all-to-all-start) | async-done | bytes 458784 | tf_op jit(solution)/shard_map/all_to_all | solution.py:481
  22.2 0.1 shard_map.216.mine
  22.2 4.6 %collective-permute-start = (bf16[112,256]{1,0:T(8,128)(2,1)S(1)}, bf16[112,256]{1,0:T(8,128)(2,1)S(1)}, u32[]{:S(2)}, u32[]{:S(2)}) collective-permute-start(bf16[112,256]{1,0:T(8,128)(2,1)S(1)} %shard_map.216.mine), channel_id=1, source_target_pairs={{0,128},{128,0},{256,384},{384,256},{1,129},{129,1},{257,385},{385... | collective-permute-start | bytes 172040 | tf_op jit(solution)/shard_map/ppermute | solution.py:491
  26.9 3.2 %collective-permute-start.2 = (bf16[256,256]{1,0:T(8,128)(2,1)}, bf16[256,256]{1,0:T(8,128)(2,1)S(1)}, u32[]{:S(2)}, u32[]{:S(2)}) collective-permute-start(bf16[256,256]{1,0:T(8,128)(2,1)} %get-tuple-element.71), channel_id=1, source_target_pairs={{16,32},{48,64},{80,96},{112,128},{144,160},{176,192},{208,224},{2... | collective-permute-start | bytes 393224 | tf_op jit(solution)/shard_map/ppermute | solution.py:445
  30.1 0.7 collective-permute-start.3
  30.8 3.9 %collective-permute-done.other = bf16[112,256]{1,0:T(8,128)(2,1)S(1)} collective-permute-done((bf16[112,256]{1,0:T(8,128)(2,1)S(1)}, bf16[112,256]{1,0:T(8,128)(2,1)S(1)}, u32[]{:S(2)}, u32[]{:S(2)}) %collective-permute-start) | collective-permute-done | bytes 57376 | tf_op jit(solution)/shard_map/ppermute | solution.py:491
  34.7 2.5 %collective-permute-start.4 = (bf16[256,256]{1,0:T(8,128)(2,1)}, bf16[256,256]{1,0:T(8,128)(2,1)S(1)}, u32[]{:S(2)}, u32[]{:S(2)}) collective-permute-start(bf16[256,256]{1,0:T(8,128)(2,1)} %get-tuple-element.73), channel_id=1, source_target_pairs={{0,1},{2,3},{4,5},{6,7},{8,9},{10,11},{12,13},{14,15},{1,0},{3,2},... | collective-permute-start | bytes 393224 | tf_op jit(solution)/shard_map/ppermute | solution.py:445
  37.3 0.0 copy-done.16
  37.3 1.9 %collective-permute-start.5 = (bf16[256,256]{1,0:T(8,128)(2,1)S(1)}, bf16[256,256]{1,0:T(8,128)(2,1)S(1)}, u32[]{:S(2)}, u32[]{:S(2)}) collective-permute-start(bf16[256,256]{1,0:T(8,128)(2,1)S(1)} %copy-done.16), channel_id=1, source_target_pairs={{0,16},{32,48},{64,80},{96,112},{128,144},{160,176},{192,208},{224... | collective-permute-start | bytes 393224 | tf_op jit(solution)/shard_map/ppermute | solution.py:445
  39.2 9.3 %collective-permute-start.1 = (bf16[112,256]{1,0:T(8,128)(2,1)S(1)}, bf16[112,256]{1,0:T(8,128)(2,1)S(1)}, u32[]{:S(2)}, u32[]{:S(2)}) collective-permute-start(bf16[112,256]{1,0:T(8,128)(2,1)S(1)} %shard_map.217.mine), channel_id=1, source_target_pairs={{0,384},{128,256},{256,128},{384,0},{1,385},{129,257},{257,129},{3... | collective-permute-start | bytes 172040 | tf_op jit(solution)/shard_map/ppermute | solution.py:496
  48.6 2.3 %collective-permute-done.1.other = bf16[112,256]{1,0:T(8,128)(2,1)S(1)} collective-permute-done((bf16[112,256]{1,0:T(8,128)(2,1)S(1)}, bf16[112,256]{1,0:T(8,128)(2,1)S(1)}, u32[]{:S(2)}, u32[]{:S(2)}) %collective-permute-start.1) | collective-permute-done | bytes 57376 | tf_op jit(solution)/shard_map/ppermute | solution.py:496
  50.8 0.0 collective-permute-done.2.arrived0
  50.8 0.0 collective-permute-done.3.arrived1
  50.8 0.0 collective-permute-done.4.arrived2
  50.9 0.0 collective-permute-done.5.arrived3
  50.9 0.1 shard_map.219
  51.0 0.0 copy-start.13
  51.0 7.7 %all_to_all.35.mine = bf16[4,96,256]{2,1,0:T(8,128)(2,1)S(1)} all-to-all(bf16[4,96,256]{2,1,0:T(8,128)(2,1)S(1)} %get-tuple-element.81), channel_id=1, replica_groups=mesh['far'=4,'y'=4,'core'=2,'gy'=16] {'y'}, dimensions={0} | all-to-all | bytes 393216 | tf_op jit(solution)/shard_map/all_to_all | solution.py:506
  58.6 3.7 %collective-permute-start.6 = (bf16[4,96,256]{2,1,0:T(8,128)(2,1)S(1)}, bf16[4,96,256]{2,1,0:T(8,128)(2,1)S(1)}, u32[]{:S(2)}, u32[]{:S(2)}) collective-permute-start(bf16[4,96,256]{2,1,0:T(8,128)(2,1)S(1)} %all_to_all.35.mine), channel_id=1, source_target_pairs={{0,16},{16,0},{1,17},{17,1},{2,18},{18,2},{3,19},{19,3},{4,20},{20... | collective-permute-start | bytes 589832 | tf_op jit(solution)/shard_map/ppermute | solution.py:507
  62.4 0.0 copy-start.12
  62.4 0.0 copy-done.1
  62.4 0.0 copy-done.13
  62.4 0.0 copy-done.11
  62.4 0.6 copy-done.12
  63.1 0.0 copy-start.14
  63.1 0.8 shard_map.218.aggregate
  63.8 0.0 collective-permute-done.6.other
  63.9 0.1 copy-done
  64.0 0.1 copy-done.3
  64.1 0.1 copy-done.4
  64.2 0.0 copy-done.14
  64.2 2.4 %shard_map.220 = (bf16[512,256]{1,0:T(8,128)(2,1)}, bf16[512,256]{1,0:T(8,128)(2,1)S(1)}, bf16[512,256]{1,0:T(8,128)(2,1)S(1)}, bf16[512,256]{1,0:T(8,128)(2,1)S...) custom-call(s32[2,4]{1,0:T(2,128)S(1)} %bitcast.21, ...), custom_call_target="tpu_custom_call" | custom-call | flops 671088640 | bytes 4194304 | tf_op jit(solution)/shard_map/pallas_call | solution.py:517
  66.7 2.1 %collective-permute-start.7 = (bf16[256,256]{1,0:T(8,128)(2,1)S(1)}, bf16[256,256]{1,0:T(8,128)(2,1)S(1)}, u32[]{:S(2)}, u32[]{:S(2)}) collective-permute-start(bf16[256,256]{1,0:T(8,128)(2,1)S(1)} %get-tuple-element.93), channel_id=1, source_target_pairs={{16,32},{48,64},{80,96},{112,128},{144,160},{176,192},{208,224},{2... | collective-permute-start | bytes 393224 | tf_op jit(solution)/shard_map/ppermute | solution.py:445
  68.8 0.7 collective-permute-start.8
  69.4 6.9 %collective-permute-start.9 = (bf16[256,256]{1,0:T(8,128)(2,1)S(1)}, bf16[256,256]{1,0:T(8,128)(2,1)S(1)}, u32[]{:S(2)}, u32[]{:S(2)}) collective-permute-start(bf16[256,256]{1,0:T(8,128)(2,1)S(1)} %get-tuple-element.95), channel_id=1, source_target_pairs={{0,1},{2,3},{4,5},{6,7},{8,9},{10,11},{12,13},{14,15},{1,0},{3,2},... | collective-permute-start | bytes 393224 | tf_op jit(solution)/shard_map/ppermute | solution.py:445
  76.4 1.9 %collective-permute-start.10 = (bf16[256,256]{1,0:T(8,128)(2,1)S(1)}, bf16[256,256]{1,0:T(8,128)(2,1)S(1)}, u32[]{:S(2)}, u32[]{:S(2)}) collective-permute-start(bf16[256,256]{1,0:T(8,128)(2,1)S(1)} %get-tuple-element.96), channel_id=1, source_target_pairs={{0,16},{32,48},{64,80},{96,112},{128,144},{160,176},{192,208},{224... | collective-permute-start | bytes 393224 | tf_op jit(solution)/shard_map/ppermute | solution.py:445
  78.3 0.0 copy-start.5
  78.3 0.0 copy-start.6
  78.4 0.0 copy-start.7
  78.4 0.0 copy-start.8
  78.4 0.0 copy-start.9
  78.4 1.9 %shard_map.221 = (bf16[4,224,256]{2,1,0:T(8,128)(2,1)S(1)}, bf16[4,224,256]{2,1,0:T(8,128)(2,1)S(1)}, f32[512,256]{1,0:T(8,128)S(1)}, f32[512,256]{1,0:T(8,128)S(1)}) custom-call(s32[4,3]{1,0:T(4,128)S(1)} %copy-done.11, s32[1,512]{1,0:T(1,128)S(1)} %bitcast.15, bf16[512,256]{1,0:T(8,128)(2,1)S(1)} %copy-done, bf16[512,256]{1,0:T(8,128)(2,1)S(1)} %copy-done.4, ...), custom_call_target="tpu_custom_call" | custom-call | flops 536870912 | bytes 5242880 | tf_op jit(solution)/shard_map/pallas_call | solution.py:531
  80.3 0.0 collective-permute-done.7.back0
  80.3 0.0 collective-permute-done.8.back1
  80.3 1.0 collective-permute-done.9.back2
  81.3 0.0 collective-permute-done.10.back3
  81.3 1.6 shard_map.222
  82.9 2.3 %collective-permute-start.11 = (bf16[4,304,256]{2,1,0:T(8,128)(2,1)S(1)}, bf16[4,304,256]{2,1,0:T(8,128)(2,1)S(1)}, u32[]{:S(2)}, u32[]{:S(2)}) collective-permute-start(bf16[4,304,256]{2,1,0:T(8,128)(2,1)S(1)} %get-tuple-element.103), channel_id=1, source_target_pairs={{0,16},{16,0},{1,17},{17,1},{2,18},{18,2},{3,19},{19,3},{4,20},{20... | collective-permute-start | bytes 1867784 | tf_op jit(solution)/shard_map/ppermute | solution.py:558
  85.2 1.7 collective-permute-done.11.other
  86.8 0.1 shard_map.223
  87.0 18.7 %all_to_all.36.received = bf16[4,304,256]{2,1,0:T(8,128)(2,1)S(1)} all-to-all(bf16[4,304,256]{2,1,0:T(8,128)(2,1)S(1)} %shard_map.223), channel_id=1, replica_groups=mesh['far'=4,'y'=4,'core'=2,'gy'=16] {'y'}, dimensions={0} | all-to-all | bytes 1245184 | tf_op jit(solution)/shard_map/all_to_all | solution.py:560
  105.7 0.1 shard_map.224
  105.7 15.4 %all_to_all.37.received = bf16[16,16,256]{2,1,0:T(8,128)(2,1)S(1)} all-to-all(bf16[16,16,256]{2,1,0:T(8,128)(2,1)S(1)} %get-tuple-element.105), channel_id=1, replica_groups=mesh['far'=4,'y'=4,'core'=2,'gy'=16] {'gy'}, dimensions={0} | all-to-all | bytes 262144 | tf_op jit(solution)/shard_map/all_to_all | solution.py:567
  121.2 23.4 %all_to_all.38.received = bf16[4,112,256]{2,1,0:T(8,128)(2,1)S(1)} all-to-all(bf16[4,112,256]{2,1,0:T(8,128)(2,1)S(1)} %shard_map.225), channel_id=1, replica_groups=mesh['far'=4,'y'=4,'core'=2,'gy'=16] {'far'}, dimensions={0} | all-to-all | bytes 458752 | tf_op jit(solution)/shard_map/all_to_all | solution.py:571
  144.6 9.8 %all_to_all.39.grads = bf16[16,16,256]{2,1,0:T(8,128)(2,1)S(1)} all-to-all(bf16[16,16,256]{2,1,0:T(8,128)(2,1)S(1)} %get-tuple-element.108), channel_id=1, replica_groups=mesh['far'=4,'y'=4,'core'=2,'gy'=16] {'gy'}, dimensions={0} | all-to-all | bytes 262144 | tf_op jit(solution)/shard_map/all_to_all | solution.py:578
  154.5 9.9 %all_to_all.40.mine = bf16[4,304,256]{2,1,0:T(8,128)(2,1)S(1)} all-to-all(bf16[4,304,256]{2,1,0:T(8,128)(2,1)S(1)} %shard_map.227), channel_id=1, replica_groups=mesh['far'=4,'y'=4,'core'=2,'gy'=16] {'y'}, dimensions={0} | all-to-all | bytes 1245184 | tf_op jit(solution)/shard_map/all_to_all | solution.py:582
  164.4 9.5 %collective-permute-start.12 = (bf16[4,304,256]{2,1,0:T(8,128)(2,1)S(1)}, bf16[4,304,256]{2,1,0:T(8,128)(2,1)S(1)}, u32[]{:S(2)}, u32[]{:S(2)}) collective-permute-start(bf16[4,304,256]{2,1,0:T(8,128)(2,1)S(1)} %all_to_all.40.mine), channel_id=1, source_target_pairs={{0,16},{16,0},{1,17},{17,1},{2,18},{18,2},{3,19},{19,3},{4,20},{20... | collective-permute-start | bytes 1867784 | tf_op jit(solution)/shard_map/ppermute | solution.py:583
  173.9 0.4 shard_map.228
  174.3 1.2 collective-permute-done.12.other
  175.6 1.6 shard_map.229
  (20 shorter events, 0.2 us)
Async XLA Ops:
  3.1 19.1 %all-to-all-start = ((bf16[8,112,256]{2,1,0:T(8,128)(2,1)}), bf16[8,112,256]{2,1,0:T(8,128)(2,1)S(1)}, u32[]{:S(2)}, u32[]{:S(2)}) async-start(bf16[8,112,256]{2,1,0:T(8,128)(2,1)} %shard_map.215), calls=%async_computation | async-start | bytes 917504 | tf_op jit(solution)/shard_map/all_to_all | solution.py:481
  16.6 45.8 %copy-start.1 = (f32[512,256]{1,0:T(8,128)S(1)}, f32[512,256]{1,0:T(8,128)}, u32[]{:S(2)}) copy-start(f32[512,256]{1,0:T(8,128)} %get-tuple-element.64.local) | copy-start | bytes 1572868
  22.2 15.0 %copy-start.16 = (bf16[256,256]{1,0:T(8,128)(2,1)S(1)}, bf16[256,256]{1,0:T(8,128)(2,1)}, u32[]{:S(2)}) copy-start(bf16[256,256]{1,0:T(8,128)(2,1)} %get-tuple-element.74) | copy-start | bytes 393220
  22.2 12.5 %collective-permute-start = (bf16[112,256]{1,0:T(8,128)(2,1)S(1)}, bf16[112,256]{1,0:T(8,128)(2,1)S(1)}, u32[]{:S(2)}, u32[]{:S(2)}) collective-permute-start(bf16[112,256]{1,0:T(8,128)(2,1)S(1)} %shard_map.216.mine), channel_id=1, source_target_pairs={{0,128},{128,0},{256,384},{384,256},{1,129},{129,1},{257,385},{385... | collective-permute-start | bytes 172040 | tf_op jit(solution)/shard_map/ppermute | solution.py:491
  26.9 23.9 %collective-permute-start.2 = (bf16[256,256]{1,0:T(8,128)(2,1)}, bf16[256,256]{1,0:T(8,128)(2,1)S(1)}, u32[]{:S(2)}, u32[]{:S(2)}) collective-permute-start(bf16[256,256]{1,0:T(8,128)(2,1)} %get-tuple-element.71), channel_id=1, source_target_pairs={{16,32},{48,64},{80,96},{112,128},{144,160},{176,192},{208,224},{2... | collective-permute-start | bytes 393224 | tf_op jit(solution)/shard_map/ppermute | solution.py:445
  30.1 20.7 %collective-permute-start.3 = (bf16[256,256]{1,0:T(8,128)(2,1)}, bf16[256,256]{1,0:T(8,128)(2,1)S(1)}, u32[]{:S(2)}, u32[]{:S(2)}) collective-permute-start(bf16[256,256]{1,0:T(8,128)(2,1)} %get-tuple-element.72), channel_id=1, source_target_pairs={{1,2},{3,4},{5,6},{7,8},{9,10},{11,12},{13,14},{2,1},{4,3},{6,5},{... | collective-permute-start | bytes 393224 | tf_op jit(solution)/shard_map/ppermute | solution.py:445
  34.7 16.1 %collective-permute-start.4 = (bf16[256,256]{1,0:T(8,128)(2,1)}, bf16[256,256]{1,0:T(8,128)(2,1)S(1)}, u32[]{:S(2)}, u32[]{:S(2)}) collective-permute-start(bf16[256,256]{1,0:T(8,128)(2,1)} %get-tuple-element.73), channel_id=1, source_target_pairs={{0,1},{2,3},{4,5},{6,7},{8,9},{10,11},{12,13},{14,15},{1,0},{3,2},... | collective-permute-start | bytes 393224 | tf_op jit(solution)/shard_map/ppermute | solution.py:445
  37.3 13.6 %collective-permute-start.5 = (bf16[256,256]{1,0:T(8,128)(2,1)S(1)}, bf16[256,256]{1,0:T(8,128)(2,1)S(1)}, u32[]{:S(2)}, u32[]{:S(2)}) collective-permute-start(bf16[256,256]{1,0:T(8,128)(2,1)S(1)} %copy-done.16), channel_id=1, source_target_pairs={{0,16},{32,48},{64,80},{96,112},{128,144},{160,176},{192,208},{224... | collective-permute-start | bytes 393224 | tf_op jit(solution)/shard_map/ppermute | solution.py:445
  39.2 11.6 %collective-permute-start.1 = (bf16[112,256]{1,0:T(8,128)(2,1)S(1)}, bf16[112,256]{1,0:T(8,128)(2,1)S(1)}, u32[]{:S(2)}, u32[]{:S(2)}) collective-permute-start(bf16[112,256]{1,0:T(8,128)(2,1)S(1)} %shard_map.217.mine), channel_id=1, source_target_pairs={{0,384},{128,256},{256,128},{384,0},{1,385},{129,257},{257,129},{3... | collective-permute-start | bytes 172040 | tf_op jit(solution)/shard_map/ppermute | solution.py:496
  51.0 11.4 %copy-start.13 = (s32[1,1,4,2]{2,3,1,0:T(2,128)S(1)}, s32[1,1,4,2]{2,3,1,0:T(2,128)}, u32[]{:S(2)}) copy-start(s32[1,1,4,2]{2,3,1,0:T(2,128)} %param.20) | copy-start | bytes 100
  58.6 3.8 %copy-start.11 = (s32[4,3]{1,0:T(4,128)S(1)}, s32[4,3]{1,0:T(4,128)}, u32[]{:S(2)}) copy-start(s32[4,3]{1,0:T(4,128)} %adjacency.1) | copy-start | bytes 148
  58.6 5.2 %collective-permute-start.6 = (bf16[4,96,256]{2,1,0:T(8,128)(2,1)S(1)}, bf16[4,96,256]{2,1,0:T(8,128)(2,1)S(1)}, u32[]{:S(2)}, u32[]{:S(2)}) collective-permute-start(bf16[4,96,256]{2,1,0:T(8,128)(2,1)S(1)} %all_to_all.35.mine), channel_id=1, source_target_pairs={{0,16},{16,0},{1,17},{17,1},{2,18},{18,2},{3,19},{19,3},{4,20},{20... | collective-permute-start | bytes 589832 | tf_op jit(solution)/shard_map/ppermute | solution.py:507
  62.4 0.7 copy-start.12
  63.0 0.9 copy-start
  63.0 1.1 copy-start.3
  63.1 1.1 copy-start.4
  63.1 1.1 copy-start.10
  63.1 1.2 copy-start.14
  63.1 1.2 copy-start.15
  64.2 14.1 %copy-start.2 = (bf16[4,3,128,128]{3,2,1,0:T(8,128)(2,1)S(1)}, bf16[4,3,128,128]{3,2,1,0:T(8,128)(2,1)}, u32[]{:S(2)}) copy-start(bf16[4,3,128,128]{3,2,1,0:T(8,128)(2,1)} %blocks.1) | copy-start | bytes 1179652
  66.7 13.6 %collective-permute-start.7 = (bf16[256,256]{1,0:T(8,128)(2,1)S(1)}, bf16[256,256]{1,0:T(8,128)(2,1)S(1)}, u32[]{:S(2)}, u32[]{:S(2)}) collective-permute-start(bf16[256,256]{1,0:T(8,128)(2,1)S(1)} %get-tuple-element.93), channel_id=1, source_target_pairs={{16,32},{48,64},{80,96},{112,128},{144,160},{176,192},{208,224},{2... | collective-permute-start | bytes 393224 | tf_op jit(solution)/shard_map/ppermute | solution.py:445
  68.8 11.5 %collective-permute-start.8 = (bf16[256,256]{1,0:T(8,128)(2,1)S(1)}, bf16[256,256]{1,0:T(8,128)(2,1)S(1)}, u32[]{:S(2)}, u32[]{:S(2)}) collective-permute-start(bf16[256,256]{1,0:T(8,128)(2,1)S(1)} %get-tuple-element.94), channel_id=1, source_target_pairs={{1,2},{3,4},{5,6},{7,8},{9,10},{11,12},{13,14},{2,1},{4,3},{6,5},{... | collective-permute-start | bytes 393224 | tf_op jit(solution)/shard_map/ppermute | solution.py:445
  69.4 11.8 %collective-permute-start.9 = (bf16[256,256]{1,0:T(8,128)(2,1)S(1)}, bf16[256,256]{1,0:T(8,128)(2,1)S(1)}, u32[]{:S(2)}, u32[]{:S(2)}) collective-permute-start(bf16[256,256]{1,0:T(8,128)(2,1)S(1)} %get-tuple-element.95), channel_id=1, source_target_pairs={{0,1},{2,3},{4,5},{6,7},{8,9},{10,11},{12,13},{14,15},{1,0},{3,2},... | collective-permute-start | bytes 393224 | tf_op jit(solution)/shard_map/ppermute | solution.py:445
  76.4 4.9 %collective-permute-start.10 = (bf16[256,256]{1,0:T(8,128)(2,1)S(1)}, bf16[256,256]{1,0:T(8,128)(2,1)S(1)}, u32[]{:S(2)}, u32[]{:S(2)}) collective-permute-start(bf16[256,256]{1,0:T(8,128)(2,1)S(1)} %get-tuple-element.96), channel_id=1, source_target_pairs={{0,16},{32,48},{64,80},{96,112},{128,144},{160,176},{192,208},{224... | collective-permute-start | bytes 393224 | tf_op jit(solution)/shard_map/ppermute | solution.py:445
  78.3 2.9 %copy-start.5 = (bf16[1,1,4,2,128,128]{5,4,3,2,1,0:T(8,128)(2,1)S(1)}, bf16[1,1,4,2,128,128]{5,4,3,2,1,0:T(8,128)(2,1)}, u32[]{:S(2)}) copy-start(bf16[1,1,4,2,128,128]{5,4,3,2,1,0:T(8,128)(2,1)} %param.21) | copy-start | bytes 786436
  78.3 2.9 %copy-start.6 = (bf16[512,256]{1,0:T(8,128)(2,1)S(1)}, bf16[512,256]{1,0:T(8,128)(2,1)}, u32[]{:S(2)}) copy-start(bf16[512,256]{1,0:T(8,128)(2,1)} %get-tuple-element.84.lifted) | copy-start | bytes 786436
  78.4 2.9 %copy-start.7 = (bf16[512,256]{1,0:T(8,128)(2,1)S(1)}, bf16[512,256]{1,0:T(8,128)(2,1)}, u32[]{:S(2)}) copy-start(bf16[512,256]{1,0:T(8,128)(2,1)} %get-tuple-element.85.active) | copy-start | bytes 786436
  78.4 2.9 %copy-start.8 = (bf16[256,256]{1,0:T(8,128)(2,1)S(1)}, bf16[256,256]{1,0:T(8,128)(2,1)}, u32[]{:S(2)}) copy-start(bf16[256,256]{1,0:T(8,128)(2,1)} %edge_lift.1) | copy-start | bytes 393220
  78.4 2.9 %copy-start.9 = (bf16[256,256]{1,0:T(8,128)(2,1)S(1)}, bf16[256,256]{1,0:T(8,128)(2,1)}, u32[]{:S(2)}) copy-start(bf16[256,256]{1,0:T(8,128)(2,1)} %edge_emit.1) | copy-start | bytes 393220
  82.9 4.0 %collective-permute-start.11 = (bf16[4,304,256]{2,1,0:T(8,128)(2,1)S(1)}, bf16[4,304,256]{2,1,0:T(8,128)(2,1)S(1)}, u32[]{:S(2)}, u32[]{:S(2)}) collective-permute-start(bf16[4,304,256]{2,1,0:T(8,128)(2,1)S(1)} %get-tuple-element.103), channel_id=1, source_target_pairs={{0,16},{16,0},{1,17},{17,1},{2,18},{18,2},{3,19},{19,3},{4,20},{20... | collective-permute-start | bytes 1867784 | tf_op jit(solution)/shard_map/ppermute | solution.py:558
  164.4 11.2 %collective-permute-start.12 = (bf16[4,304,256]{2,1,0:T(8,128)(2,1)S(1)}, bf16[4,304,256]{2,1,0:T(8,128)(2,1)S(1)}, u32[]{:S(2)}, u32[]{:S(2)}) collective-permute-start(bf16[4,304,256]{2,1,0:T(8,128)(2,1)S(1)} %all_to_all.40.mine), channel_id=1, source_target_pairs={{0,16},{16,0},{1,17},{17,1},{2,18},{18,2},{3,19},{19,3},{4,20},{20... | collective-permute-start | bytes 1867784 | tf_op jit(solution)/shard_map/ppermute | solution.py:583
